TPU v7x, 512 devices: a whole 4x8x8 slice. The times are simulated.
512 devices in a mesh: grp: 2 (over z_lo), seq: 64 (over x, y, core), mdl: 4 (over z_hi).
Axes of the slice: x: 4, y: 8, z: 8 (z_hi: 4, z_lo: 2; z = z_hi * 2 + z_lo), core: 2. Of those that a mesh axis runs over, the one named last changes fastest.
Arguments:
- audio: bfloat16 [49152, 1280], P('seq'), may hold values from -6 to 6
- frame_count: int32 [1], replicated, may hold values from 24576 to 49152
- ln_gain: float32 [1280], replicated, may hold values from 0.1 to 1.9
- glu_weight: bfloat16 [2, 1280, 1280], P(None, None, 'mdl'), may hold values from -0.15625 to 0.15625
- dw_kernel: float32 [31, 1280], P(None, 'mdl'), may hold values from -1 to 1
- pw_weight: bfloat16 [1280, 1280], P('mdl'), may hold values from -0.15625 to 0.15625
- adapt_weight: bfloat16 [1280, 3584], P('seq', 'mdl'), may hold values from -0.15625 to 0.15625
- text: bfloat16 [12288, 3584], P('seq', 'mdl'), may hold values from -6 to 6
- norm_gain: float32 [3584], replicated, may hold values from 0.1 to 1.9
- qkv_weight: bfloat16 [3584, 4608], P('seq', 'mdl'), may hold values from -0.09375 to 0.09375
- qkv_bias: float32 [4608], P('mdl'), may hold values from -3 to 3
Outputs:
- sectioned: bfloat16 [2, 12288, 3584], P('grp', 'seq', 'mdl')
All inputs are finite; a program needn't handle non-finite values.
Results may differ from a plain program's by a relative error of at most 0.02.
Values may be sent and summed in bfloat16 or wider, within the bound.
No kernel may reach another device: no remote copies, remote signals or barrier semaphores. Data moves between devices by JAX's collectives and lax.ppermute only.
A program may use at most 64 MiB of HBM per device.

v0:
```python
import jax
import jax.numpy as jnp
from jax import lax
from jax.sharding import PartitionSpec as P

HEADS = 28
KV = 4
HEAD = 128


def padded_2(value, sides, width):
    for axis, dim in sides:
        count, length = (lax.axis_size(axis), value.shape[dim])
        up = [(i, (i + 1) % count) for i in range(count - 1)]
        down = [(j, i) for i, j in up]
        last = lax.slice_in_dim(value, length - width, length, axis=dim)
        initial = lax.slice_in_dim(value, 0, width, axis=dim)
        before = lax.ppermute(last, axis, up)
        after = lax.ppermute(initial, axis, down)
        value = jnp.concatenate([before, value, after], axis=dim)
    return value


def from_behind(block, axis, distance):
    devices = range(lax.axis_size(axis))
    route = [(i - distance, i) for i in devices if i - distance in devices]
    return lax.ppermute(block, axis, route)


def rotate(values, positions):
    half = values.shape[-1] // 2
    freq = 1000000.0 ** (-(jnp.arange(half, dtype=jnp.float32) * 2.0 / values.shape[-1]))
    angle = positions.astype(jnp.float32)[:, None] * freq[None, :]
    cosine = jnp.cos(angle)[:, None, :]
    sine = jnp.sin(angle)[:, None, :]
    first = values[..., :half]
    second = values[..., half:]
    return jnp.concatenate(
        [first * cosine - second * sine, second * cosine + first * sine], axis=-1
    )


def encode(audio, frame_count, ln_gain, glu_weight, dw_kernel, pw_weight, adapt_weight):
    frames_dev = audio.shape[0]
    rows = audio.astype(jnp.float32)
    centred = rows - jnp.mean(rows, axis=-1, keepdims=True)
    spread = jnp.mean(centred * centred, axis=-1, keepdims=True)
    normed = (centred * lax.rsqrt(spread + 1e-05) * ln_gain).astype(jnp.bfloat16)
    first_frame = lax.axis_index("seq") * frames_dev
    valid = (first_frame + jnp.arange(frames_dev, dtype=jnp.int32) < frame_count[0]).astype(
        jnp.float32
    )
    left = jnp.dot(normed, glu_weight[0], preferred_element_type=jnp.float32)
    right = jnp.dot(normed, glu_weight[1], preferred_element_type=jnp.float32)
    gated = (left * jax.nn.sigmoid(right) * valid[:, None]).astype(jnp.bfloat16)
    taps = dw_kernel.shape[0]
    margin = (taps - 1) // 2
    padded = padded_2(gated, (("seq", 0),), margin)
    conv = jnp.zeros(gated.shape, jnp.float32)
    for offset in range(taps):
        conv = conv + padded[offset : offset + frames_dev].astype(jnp.float32) * dw_kernel[offset]
    act = (conv * jax.nn.sigmoid(conv)).astype(jnp.bfloat16)
    partial_out = jnp.dot(act, pw_weight, preferred_element_type=jnp.float32)
    width = rows.shape[1]
    pooled_count = frames_dev // 4
    pooled_term = jnp.mean(partial_out.reshape(pooled_count, 4, width), axis=1).astype(jnp.bfloat16)
    pooled_audio = jnp.mean(rows.reshape(pooled_count, 4, width), axis=1)
    total = lax.psum(pooled_term.astype(jnp.float32).astype(jnp.bfloat16), "mdl").astype(
        jnp.float32
    )
    pooled = (pooled_audio + total).astype(jnp.bfloat16)
    tokens = jnp.dot(
        pooled,
        lax.all_gather(adapt_weight, "seq", axis=0, tiled=True),
        preferred_element_type=jnp.float32,
    )
    return tokens.astype(jnp.bfloat16)


def decode(sound, words, norm_gain, qkv_weight, qkv_bias):
    count = sound.shape[0]
    joined = jnp.concatenate([sound, words], axis=0).astype(jnp.float32)
    scale_rows = lax.rsqrt(jnp.mean(joined * joined, axis=-1, keepdims=True) + 1e-06)
    normal_rows = (joined * scale_rows * norm_gain).astype(jnp.bfloat16)
    projected = (
        jnp.dot(
            normal_rows,
            lax.all_gather(qkv_weight, "seq", axis=0, tiled=True),
            preferred_element_type=jnp.float32,
        )
        + qkv_bias
    )
    heads_dev = HEADS // lax.axis_size("mdl")
    kv_dev = KV // lax.axis_size("mdl")
    group = HEADS // KV
    query_cols = heads_dev * HEAD
    key_cols = kv_dev * HEAD
    positions = jnp.arange(2 * count, dtype=jnp.int32)
    query = rotate(projected[:, :query_cols].reshape(2 * count, heads_dev, HEAD), positions).astype(
        jnp.bfloat16
    )
    keys = rotate(
        projected[:, query_cols : query_cols + key_cols].reshape(2 * count, kv_dev, HEAD), positions
    ).astype(jnp.bfloat16)
    values = (
        projected[:, query_cols + key_cols :].reshape(2 * count, kv_dev, HEAD).astype(jnp.bfloat16)
    )
    asked = query[count:].reshape(count, kv_dev, group, HEAD)
    scores = jnp.einsum(
        "qkgd,pkd->kgqp", asked, keys, preferred_element_type=jnp.float32
    ) / jnp.sqrt(jnp.float32(HEAD))
    allowed = (positions[None, :] <= positions[count:][:, None]).astype(jnp.float32)
    weights = jnp.exp(scores) * allowed
    probs = (weights / jnp.sum(weights, axis=-1, keepdims=True)).astype(jnp.bfloat16)
    context = jnp.einsum("kgqp,pkd->qkgd", probs, values, preferred_element_type=jnp.float32)
    return context.reshape(count, heads_dev * HEAD).astype(jnp.bfloat16)


def shards(
    audio,
    frame_count,
    ln_gain,
    glu_weight,
    dw_kernel,
    pw_weight,
    adapt_weight,
    text,
    norm_gain,
    qkv_weight,
    qkv_bias,
):
    group_index = lax.axis_index("grp")
    encoded = encode(audio, frame_count, ln_gain, glu_weight, dw_kernel, pw_weight, adapt_weight)
    own = jnp.where(group_index == 0, encoded, text)
    handed = from_behind(own, "grp", 1)
    sound, words = (
        lax.all_gather(handed, "mdl", axis=1, tiled=True),
        lax.all_gather(text, "mdl", axis=1, tiled=True),
    )
    decoded = decode(sound, words, norm_gain, qkv_weight, qkv_bias)
    result = jnp.where(group_index == 1, decoded, own)
    return result[None]


def solution(mesh):
    in_specs = (
        P("seq", None),
        P(),
        P(),
        P(None, None, "mdl"),
        P(None, "mdl"),
        P("mdl", None),
        P("seq", "mdl"),
        P("seq", "mdl"),
        P(),
        P("seq", "mdl"),
        P("mdl"),
    )
    out_specs = P("grp", "seq", "mdl")
    return jax.shard_map(shards, mesh=mesh, in_specs=in_specs, out_specs=out_specs, check_vma=False)
```

profile of v0, /device:TPU:1, one launch (start us, length us, event | category | flops | bytes accessed | tf_op | source)
XLA Modules:
  0.0 309.9 jit_solution(16757112280415260400)
XLA Ops:
  8.8 1.9 convert_reduce_fusion
  12.8 0.9 fusion.9
  13.7 0.9 fusion.11
  14.7 4.6 %collective-permute-start = (bf16[15,320]{0,1:T(8,128)(2,1)S(1)}, bf16[15,320]{0,1:T(8,128)(2,1)S(1)}, u32[]{:S(2)}, u32[]{:S(2)}) collective-permute-start(bf16[15,320]{0,1:T(8,128)(2,1)S(1)} %get-tuple-element.40), channel_id=1, source_target_pairs={{0,4},{4,8},{8,12},{12,16},{16,20},{20,24},{24,28},{28,32},{32,36}... | collective-permute-start | bytes 28808 | tf_op jit(solution)/shard_map/ppermute | solution.py:18
  19.3 5.7 %collective-permute-start.1 = (bf16[15,320]{0,1:T(8,128)(2,1)S(1)}, bf16[15,320]{0,1:T(8,128)(2,1)S(1)}, u32[]{:S(2)}, u32[]{:S(2)}) collective-permute-start(bf16[15,320]{0,1:T(8,128)(2,1)S(1)} %get-tuple-element.41), channel_id=1, source_target_pairs={{4,0},{8,4},{12,8},{16,12},{20,16},{24,20},{28,24},{32,28},{36,32}... | collective-permute-start | bytes 28808 | tf_op jit(solution)/shard_map/ppermute | solution.py:19
  25.7 9.2 %fusion.49 = f32[768,1280]{1,0:T(8,128)} fusion(bf16[320,1280]{1,0:T(8,128)(2,1)S(1)} %copy-done, bf16[768,320]{0,1:T(8,128)(2,1)S(1)} %fusion.11, bf16[15,320]{0,1:T(8,128)(2,1)S(1)} %collective-permute-done.1, bf16[15,320]{0,1:T(8,128)(2,1)S(1)} %collective-permute-done, f32[320]{0:T(512)S(1)} %get-tuple-element.34, f32[320]{0:T(512)S(1)} %get-tuple-element.35, ...), kind=kOutput, calls=%fused_computation.120 | convolution fusion | flops 675102720 | bytes 5301760 | tf_op jit(solution)/shard_map/dot_general | solution.py:63
  34.8 5.1 %reshape.203 = f32[192,4,1280]{2,1,0:T(4,128)} reshape(f32[768,1280]{1,0:T(8,128)} %fusion.49) | data formatting | bytes 7864320 | tf_op jit(solution)/shard_map/reshape | solution.py:66
  40.0 5.4 %reduce_sum.57 = f32[192,1280]{1,0:T(8,128)} reduce(f32[192,4,1280]{2,1,0:T(4,128)} %reshape.203, f32[]{:T(128)} %constant.15.clone.1), dimensions={1}, to_apply=%region_3.0 | reduce | flops 737280 | bytes 4915204 | tf_op jit(solution)/shard_map/reduce_sum | solution.py:66
  45.4 2.0 multiply_convert_fusion.1
  48.5 2.8 reshape.202
  51.3 5.4 %reduce_sum.54 = f32[192,1280]{1,0:T(8,128)} reduce(f32[192,4,1280]{2,1,0:T(4,128)} %reshape.202, f32[]{:T(128)} %constant.15.clone.1), dimensions={1}, to_apply=%region_0.0 | reduce | flops 737280 | bytes 4915204 | tf_op jit(solution)/shard_map/reduce_sum | solution.py:67
  56.7 43.9 %all-gather.12.cloned.1.call-done = bf16[64,20,896]{2,1,0:T(8,128)(2,1)} async-done(((bf16[1,20,896]{2,1,0:T(8,128)(2,1)}), bf16[64,20,896]{2,1,0:T(8,128)(2,1)}) %all-gather.12.cloned.1.call-update) | async-done | bytes 2293776 | tf_op jit(solution)/shard_map/all_gather | solution.py:74
  100.6 3.5 %reshape.208 = bf16[1280,896]{1,0:T(8,128)(2,1)S(1)} reshape(bf16[64,20,896]{2,1,0:T(8,128)(2,1)} %all-gather.12.cloned.1.call-done) | data formatting | bytes 4587520
  104.1 5.4 %all-reduce.2.cloned.1.call-done = bf16[192,1280]{1,0:T(8,128)(2,1)} async-done(((bf16[192,1280]{1,0:T(8,128)(2,1)}), bf16[192,1280]{1,0:T(8,128)(2,1)}) %all-reduce.2.cloned.1.call-update) | async-done | bytes 491536 | tf_op jit(solution)/shard_map/psum | solution.py:68
  109.4 2.0 fusion.12
  112.2 3.0 collective-permute-start.2
  115.3 22.0 %collective-permute-done.2 = bf16[192,896]{1,0:T(8,128)(2,1)S(1)} collective-permute-done((bf16[192,896]{1,0:T(8,128)(2,1)S(1)}, bf16[192,896]{1,0:T(8,128)(2,1)S(1)}, u32[]{:S(2)}, u32[]{:S(2)}) %collective-permute-start.2) | collective-permute-done | bytes 344096 | tf_op jit(solution)/shard_map/ppermute | solution.py:27
  138.8 1.5 multiply_cosine_fusion
  140.4 8.2 %all-gather.8.cloned.1.call-done = bf16[192,3584]{1,0:T(8,128)(2,1)} async-done(((bf16[192,896]{1,0:T(8,128)(2,1)}), bf16[192,3584]{1,0:T(8,128)(2,1)}) %all-gather.8.cloned.1.call-update) | async-done | bytes 1376272 | tf_op jit(solution)/shard_map/all_gather | solution.py:138
  148.6 43.2 %all-gather.6.cloned.1.call-done = bf16[192,3584]{1,0:T(8,128)(2,1)} async-done(((bf16[192,896]{1,0:T(8,128)(2,1)}), bf16[192,3584]{1,0:T(8,128)(2,1)}) %all-gather.6.cloned.1.call-update) | async-done | bytes 1376272 | tf_op jit(solution)/shard_map/all_gather | solution.py:137
  191.8 2.4 fusion
  194.2 87.3 %all-gather.10.cloned.1.call-done = bf16[3584,1152]{1,0:T(8,128)(2,1)} async-done(((bf16[56,1152]{1,0:T(8,128)(2,1)}), bf16[3584,1152]{1,0:T(8,128)(2,1)}) %all-gather.10.cloned.1.call-update) | async-done | bytes 8257552 | tf_op jit(solution)/shard_map/all_gather | solution.py:88
  281.5 7.6 %convolution_add_fusion = f32[384,1152]{1,0:T(8,128)S(1)} fusion(bf16[3584,1152]{1,0:T(8,128)(2,1)} %all-gather.10.cloned.1.call-done, f32[3584]{0:T(1024)S(1)} %copy-done.11, f32[384]{0:T(512)S(1)} %add_rsqrt_fusion.1, bf16[192,3584]{1,0:T(8,128)(2,1)S(1)} %copy-done.3, bf16[192,3584]{1,0:T(8,128)(2,1)} %all-gather.6.cloned.1.call-done, f32[1152]{0:T(1024)S(1)} %copy-done.12), kind=kOutput, calls=%fused_computation.7 | convolution fusion | flops 3180969984 | bytes 12800000 | tf_op jit(solution)/shard_map/dot_general | solution.py:86
  289.1 1.3 slice.389
  290.7 1.8 copy.19
  292.5 1.0 fusion.75
  293.5 1.5 copy.23
  295.0 1.5 copy.24
  296.6 0.8 fusion.67
  297.4 1.8 subtract_convert_fusion
  299.2 0.8 fusion.6
  300.1 1.6 fusion.13
  (55 shorter events, 8.3 us)
Async XLA Ops:
  7.4 18.3 %copy-start = (bf16[320,1280]{1,0:T(8,128)(2,1)S(1)}, bf16[320,1280]{1,0:T(8,128)(2,1)}, u32[]{:S(2)}) copy-start(bf16[320,1280]{1,0:T(8,128)(2,1)} %param.16) | copy-start | bytes 2457604
  7.4 3.3 %copy-start.1 = (bf16[768,1280]{1,0:T(8,128)(2,1)S(1)}, bf16[768,1280]{1,0:T(8,128)(2,1)}, u32[]{:S(2)}) copy-start(bf16[768,1280]{1,0:T(8,128)(2,1)} %param.11) | copy-start | bytes 5898244
  7.4 4.0 %copy-start.9 = (f32[1280]{0:T(1024)S(1)}, f32[1280]{0:T(1024)}, u32[]{:S(2)}) copy-start(f32[1280]{0:T(1024)} %param.13) | copy-start | bytes 15364
  7.4 93.2 %all-gather.12.cloned.1.call-start = ((), (), s32[]{:S(2)}) async-start(), calls=%async_computation.4 | async-start | bytes 2795520 | tf_op jit(solution)/shard_map/all_gather | solution.py:74
  8.1 101.3 %all-reduce.2.cloned.1.call-start = ((), (), s32[]{:S(2)}) async-start(), calls=%async_computation | async-start | bytes 983040 | tf_op jit(solution)/shard_map/psum | solution.py:68
  11.4 1.4 copy-start.10
  13.7 11.3 %copy-start.8 = (f32[31,320]{1,0:T(8,128)S(1)}, f32[31,320]{1,0:T(8,128)}, u32[]{:S(2)}) copy-start(f32[31,320]{1,0:T(8,128)} %param.15) | copy-start | bytes 119044
  14.7 10.5 %collective-permute-start = (bf16[15,320]{0,1:T(8,128)(2,1)S(1)}, bf16[15,320]{0,1:T(8,128)(2,1)S(1)}, u32[]{:S(2)}, u32[]{:S(2)}) collective-permute-start(bf16[15,320]{0,1:T(8,128)(2,1)S(1)} %get-tuple-element.40), channel_id=1, source_target_pairs={{0,4},{4,8},{8,12},{12,16},{16,20},{20,24},{24,28},{28,32},{32,36}... | collective-permute-start | bytes 28808 | tf_op jit(solution)/shard_map/ppermute | solution.py:18
  19.3 6.4 %collective-permute-start.1 = (bf16[15,320]{0,1:T(8,128)(2,1)S(1)}, bf16[15,320]{0,1:T(8,128)(2,1)S(1)}, u32[]{:S(2)}, u32[]{:S(2)}) collective-permute-start(bf16[15,320]{0,1:T(8,128)(2,1)S(1)} %get-tuple-element.41), channel_id=1, source_target_pairs={{4,0},{8,4},{12,8},{16,12},{20,16},{24,20},{28,24},{32,28},{36,32}... | collective-permute-start | bytes 28808 | tf_op jit(solution)/shard_map/ppermute | solution.py:19
  47.5 101.1 %all-gather.8.cloned.1.call-start = ((), (), s32[]{:S(2)}) async-start(), calls=%async_computation.2 | async-start | bytes 1720320 | tf_op jit(solution)/shard_map/all_gather | solution.py:138
  48.2 143.6 %all-gather.6.cloned.1.call-start = ((), (), s32[]{:S(2)}) async-start(), calls=%async_computation.1 | async-start | bytes 1720320 | tf_op jit(solution)/shard_map/all_gather | solution.py:137
  56.7 52.7 %copy-start.4 = (bf16[192,896]{1,0:T(8,128)(2,1)S(1)}, bf16[192,896]{1,0:T(8,128)(2,1)}, u32[]{:S(2)}) copy-start(bf16[192,896]{1,0:T(8,128)(2,1)} %param.18) | copy-start | bytes 1032196
  111.5 0.7 copy-start.5
  112.2 169.3 %copy-start.11 = (f32[3584]{0:T(1024)S(1)}, f32[3584]{0:T(1024)}, u32[]{:S(2)}) copy-start(f32[3584]{0:T(1024)} %param.19) | copy-start | bytes 43012
  112.2 169.3 %copy-start.12 = (f32[1152]{0:T(1024)S(1)}, f32[1152]{0:T(1024)}, u32[]{:S(2)}) copy-start(f32[1152]{0:T(1024)} %param.21) | copy-start | bytes 13828
  112.2 25.1 %collective-permute-start.2 = (bf16[192,896]{1,0:T(8,128)(2,1)S(1)}, bf16[192,896]{1,0:T(8,128)(2,1)S(1)}, u32[]{:S(2)}, u32[]{:S(2)}) collective-permute-start(bf16[192,896]{1,0:T(8,128)(2,1)S(1)} %fusion.12), channel_id=1, source_target_pairs={{0,256},{1,257},{2,258},{3,259},{4,260},{5,261},{6,262},{7,263},{8... | collective-permute-start | bytes 1032200 | tf_op jit(solution)/shard_map/ppermute | solution.py:27
  137.3 0.7 copy-start.7
  138.1 143.5 %all-gather.10.cloned.1.call-start = ((), (), s32[]{:S(2)}) async-start(), calls=%async_computation.3 | async-start | bytes 8386560 | tf_op jit(solution)/shard_map/all_gather | solution.py:88
  148.6 132.9 %copy-start.3 = (bf16[192,3584]{1,0:T(8,128)(2,1)S(1)}, bf16[192,3584]{1,0:T(8,128)(2,1)}, u32[]{:S(2)}) copy-start(bf16[192,3584]{1,0:T(8,128)(2,1)} %all-gather.8.cloned.1.call-done) | copy-start | bytes 4128772
  289.1 1.6 copy-start.2
  300.1 1.9 copy-start.6
Sparse Core Ops, SparseCore 0:
  11.5 89.0 all-gather.11
  102.9 45.6 all-gather.7
  150.9 40.8 all-gather.5
  195.4 86.0 all-gather.9
Sparse Core Ops, SparseCore 1:
  47.6 61.8 all-reduce.1
where the time goes:
time: 311 us; the launch traced here: 310 us
  waiting for transfers between devices  213 us (68%)
  other arithmetic  23.5 us (8%)
  matrix products  23 us (7%)
  local copies, waits for them, and re-layouts  21.7 us (7%)
  between operations  15.5 us (5%)
  starting transfers between devices  13.7 us (4%)
    all_gather x1, waiting for transfers between devices, decode(): lax.all_gather(qkv_weight, 'seq', axis=0, tiled=True)  87.3 us
    all_gather x1, waiting for transfers between devices, encode(): lax.all_gather(adapt_weight, 'seq', axis=0, tiled=True)  43.9 us
    all_gather x1, waiting for transfers between devices, shards(): lax.all_gather(handed, 'mdl', axis=1, tiled=True)  43.2 us
    ppermute x1, waiting for transfers between devices, from_behind(): return lax.ppermute(block, axis, route)  22 us
    dot_general x1, matrix products, encode(): partial_out = jnp.dot(act, pw_weight, preferred_element_type=jnp.float32)  9.18 us
    unnamed x29, local copies, waits for them, and re-layouts  9.12 us
    all_gather x1, waiting for transfers between devices, shards(): lax.all_gather(text, 'mdl', axis=1, tiled=True)  8.24 us
    dot_general x1, matrix products, decode(): jnp.dot(normal_rows, lax.all_gather(qkv_weight, 'seq', axis=0, tiled=True...  7.56 us
  transfers between devices with their start and end apart: 8, of which 7 were waited for; matrix products, arithmetic and copies ran while one was open for 14% of the time, Pallas kernels for 0%

commit v1 on v0

v1 whole, which is shorter than its diff:
```python
import functools

import jax
import jax.numpy as jnp
from jax import lax
from jax.experimental import pallas as pl
from jax.experimental.pallas import tpu as pltpu
from jax.sharding import PartitionSpec as P

HEADS = 28
KV = 4
HEAD = 128
VMEM = 48 * 1024 * 1024


def rotary_tables(count):
    half = HEAD // 2
    freq = 1000000.0 ** (-(jnp.arange(half, dtype=jnp.float32) * 2.0 / HEAD))
    angle = jnp.arange(count, dtype=jnp.int32).astype(jnp.float32)[:, None] * freq[None, :]
    cosine, sine = jnp.cos(angle), jnp.sin(angle)
    return jnp.concatenate([cosine, cosine], 1), jnp.concatenate([-sine, sine], 1)


def turned(values, cosine, sine):
    return values * cosine + pltpu.roll(values, HEAD // 2, 1) * sine


def text_kernel(x_ref, gain_ref, w_ref, bias_ref, cos_ref, sin_ref, q_ref, k_ref, v_ref, acc, square):
    step = pl.program_id(0)

    @pl.when(step == 0)
    def _():
        acc[...] = jnp.zeros_like(acc)
        square[...] = jnp.zeros_like(square)

    x = x_ref[0].astype(jnp.float32)
    square[...] += jnp.sum(x * x, axis=1, keepdims=True)
    acc[...] += jnp.dot(
        (x * gain_ref[0]).astype(jnp.bfloat16), w_ref[...], preferred_element_type=jnp.float32
    )

    @pl.when(step == pl.num_programs(0) - 1)
    def _():
        scale = lax.rsqrt(square[...] / (pl.num_programs(0) * x.shape[1]) + 1e-6)
        cosine, sine = cos_ref[...], sin_ref[...]
        heads = q_ref.shape[1] // HEAD
        for h in range(heads + 2):
            cols = pl.ds(h * HEAD, HEAD)
            value = acc[:, cols] * scale + bias_ref[:, cols]
            if h < heads + 1:
                value = turned(value, cosine, sine)
            value = value.astype(jnp.bfloat16)
            if h < heads:
                q_ref[:, cols] = value
            elif h == heads:
                k_ref[...] = value
            else:
                v_ref[...] = value


def audio_kernel(
    order_ref, *refs, parts
):
    xs = refs[:parts]
    (gain_ref, wk_ref, wv_ref, bias_ref, cos_ref, sin_ref, q_ref, kt_ref, vt_ref, out_ref, acc_k, acc_v, square) = refs[parts:]
    step = pl.program_id(0)

    @pl.when(step == 0)
    def _():
        acc_k[...] = jnp.zeros_like(acc_k)
        acc_v[...] = jnp.zeros_like(acc_v)
        square[...] = jnp.zeros_like(square)

    for i in range(parts):

        @pl.when(step == i)
        def _():
            x = xs[i][...].astype(jnp.float32)
            square[...] += jnp.sum(x * x, axis=1, keepdims=True)
            xg = (x * gain_ref[0]).astype(jnp.bfloat16)
            acc_k[...] += jnp.dot(xg, wk_ref[...], preferred_element_type=jnp.float32)
            acc_v[...] += jnp.dot(xg, wv_ref[...], preferred_element_type=jnp.float32)

    @pl.when(step == pl.num_programs(0) - 1)
    def _():
        count = acc_k.shape[0]
        heads = q_ref.shape[1] // HEAD
        scale = lax.rsqrt(square[...] / (parts * xs[0].shape[1]) + 1e-6)
        keys = turned(acc_k[...] * scale + bias_ref[:, :HEAD], cos_ref[...], sin_ref[...])
        keys = jnp.concatenate([keys.astype(jnp.bfloat16), kt_ref[...]], axis=0)
        values = (acc_v[...] * scale + bias_ref[:, HEAD:]).astype(jnp.bfloat16)
        values = jnp.concatenate([values, vt_ref[...]], axis=0)
        row = lax.broadcasted_iota(jnp.int32, (count, 2 * count), 0)
        col = lax.broadcasted_iota(jnp.int32, (count, 2 * count), 1)
        allowed = col <= row + count
        for h in range(heads):
            cols = pl.ds(h * HEAD, HEAD)
            scores = lax.dot_general(
                q_ref[:, cols], keys, (((1,), (1,)), ((), ())), preferred_element_type=jnp.float32
            ) * (HEAD**-0.5)
            scores = jnp.where(allowed, scores, -1e30)
            weights = jnp.exp(scores - jnp.max(scores, axis=1, keepdims=True))
            probs = weights * (1.0 / jnp.sum(weights, axis=1, keepdims=True))
            out_ref[:, cols] = jnp.dot(
                probs.astype(jnp.bfloat16), values, preferred_element_type=jnp.float32
            ).astype(jnp.bfloat16)


def text_part(x, gain, weight, bias, tables):
    parts, count, width = x.shape
    total = weight.shape[1]
    heads = total // HEAD - 2
    cosine, sine = tables
    whole = lambda *shape: pl.BlockSpec(shape, lambda k: (0,) * len(shape))
    return pl.pallas_call(
        text_kernel,
        grid=(parts,),
        in_specs=[
            pl.BlockSpec((1, count, width), lambda k: (k, 0, 0)),
            pl.BlockSpec((1, 1, width), lambda k: (k, 0, 0)),
            pl.BlockSpec((width, total), lambda k: (k, 0)),
            whole(1, total),
            pl.BlockSpec((count, HEAD), lambda k: (1, 0)),
            pl.BlockSpec((count, HEAD), lambda k: (1, 0)),
        ],
        out_specs=[whole(count, heads * HEAD), whole(count, HEAD), whole(count, HEAD)],
        out_shape=[
            jax.ShapeDtypeStruct((count, heads * HEAD), jnp.bfloat16),
            jax.ShapeDtypeStruct((count, HEAD), jnp.bfloat16),
            jax.ShapeDtypeStruct((count, HEAD), jnp.bfloat16),
        ],
        scratch_shapes=[pltpu.VMEM((count, total), jnp.float32), pltpu.VMEM((count, 1), jnp.float32)],
        compiler_params=pltpu.CompilerParams(vmem_limit_bytes=VMEM),
        cost_estimate=pl.CostEstimate(
            flops=2 * count * parts * width * total, bytes_accessed=2 * parts * width * (total + count), transcendentals=0
        ),
        name="text_part",
    )(x, gain, weight, bias, cosine, sine)


def audio_part(order, xs, gain, weight, bias, tables, q, kt, vt):
    parts = len(xs)
    count, width = xs[0].shape
    total = weight.shape[1]
    heads = total // HEAD - 2
    cosine, sine = tables
    whole = lambda *shape: pl.BlockSpec(shape, lambda k, o: (0,) * len(shape))
    return pl.pallas_call(
        functools.partial(audio_kernel, parts=parts),
        grid_spec=pltpu.PrefetchScalarGridSpec(
            num_scalar_prefetch=1,
            grid=(parts,),
            in_specs=[whole(count, width)] * parts
            + [
                pl.BlockSpec((1, 1, width), lambda k, o: (o[k], 0, 0)),
                pl.BlockSpec((width, HEAD), lambda k, o: (o[k], heads)),
                pl.BlockSpec((width, HEAD), lambda k, o: (o[k], heads + 1)),
                whole(1, 2 * HEAD),
                whole(count, HEAD),
                whole(count, HEAD),
                whole(count, heads * HEAD),
                whole(count, HEAD),
                whole(count, HEAD),
            ],
            out_specs=whole(count, heads * HEAD),
            scratch_shapes=[
                pltpu.VMEM((count, HEAD), jnp.float32),
                pltpu.VMEM((count, HEAD), jnp.float32),
                pltpu.VMEM((count, 1), jnp.float32),
            ],
        ),
        out_shape=jax.ShapeDtypeStruct((count, heads * HEAD), jnp.bfloat16),
        compiler_params=pltpu.CompilerParams(vmem_limit_bytes=VMEM),
        cost_estimate=pl.CostEstimate(
            flops=2 * count * parts * width * 2 * HEAD, bytes_accessed=2 * parts * width * (2 * HEAD + count), transcendentals=0
        ),
        name="audio_part",
    )(order, *xs, gain, weight, weight, bias, cosine[:count], sine[:count], q, kt, vt)


def pooling(rows):
    r = lax.broadcasted_iota(jnp.int32, (rows // 4, rows), 0)
    c = lax.broadcasted_iota(jnp.int32, (rows // 4, rows), 1)
    return jnp.where(c // 4 == r, 0.25, 0.0).astype(jnp.bfloat16)


def encode(audio, frame_count, ln_gain, glu_weight, dw_kernel, pw_weight):
    frames_dev = audio.shape[0]
    rows = audio.astype(jnp.float32)
    centred = rows - jnp.mean(rows, axis=-1, keepdims=True)
    spread = jnp.mean(centred * centred, axis=-1, keepdims=True)
    normed = (centred * lax.rsqrt(spread + 1e-05) * ln_gain).astype(jnp.bfloat16)
    first_frame = lax.axis_index("seq") * frames_dev
    valid = (first_frame + jnp.arange(frames_dev, dtype=jnp.int32) < frame_count[0]).astype(
        jnp.float32
    )
    left = jnp.dot(normed, glu_weight[0], preferred_element_type=jnp.float32)
    right = jnp.dot(normed, glu_weight[1], preferred_element_type=jnp.float32)
    gated = (left * jax.nn.sigmoid(right) * valid[:, None]).astype(jnp.bfloat16)
    taps = dw_kernel.shape[0]
    margin = (taps - 1) // 2
    count = lax.axis_size("seq")
    up = [(i, i + 1) for i in range(count - 1)]
    down = [(j, i) for i, j in up]
    before = lax.ppermute(gated[frames_dev - margin :], "seq", up)
    after = lax.ppermute(gated[:margin], "seq", down)
    padded = jnp.concatenate([before, gated, after], axis=0)
    conv = jnp.zeros(gated.shape, jnp.float32)
    for offset in range(taps):
        conv = conv + padded[offset : offset + frames_dev].astype(jnp.float32) * dw_kernel[offset]
    act = (conv * jax.nn.sigmoid(conv)).astype(jnp.bfloat16)
    pool = pooling(frames_dev)
    pooled_act = jnp.dot(pool, act, preferred_element_type=jnp.float32).astype(jnp.bfloat16)
    term = jnp.dot(pooled_act, pw_weight, preferred_element_type=jnp.float32).astype(jnp.bfloat16)
    pooled_audio = jnp.dot(pool, audio, preferred_element_type=jnp.float32)
    return term, pooled_audio


def gather_rows(block):
    return lax.all_gather(block, "seq", axis=0, tiled=True)


def shards(
    audio, frame_count, ln_gain, glu_weight, dw_kernel, pw_weight, adapt_weight, text, norm_gain, qkv_weight, qkv_bias
):
    grp = lax.axis_index("grp")
    mdl = lax.axis_index("mdl")
    n_mdl = lax.axis_size("mdl")
    both = ("grp", "mdl")
    width = adapt_weight.shape[1]
    held = jnp.pad(
        adapt_weight,
        ((0, qkv_weight.shape[0] - adapt_weight.shape[0]), (0, qkv_weight.shape[1] - width)),
    )
    gathered = gather_rows(jnp.where(grp == 0, held, qkv_weight))

    words = [text] + [
        lax.ppermute(text, both, [(n_mdl + i, n_mdl + (i + k) % n_mdl) for i in range(n_mdl)])
        for k in range(1, n_mdl)
    ]
    term, pooled_audio = encode(audio, frame_count, ln_gain, glu_weight, dw_kernel, pw_weight)
    total = pooled_audio + term.astype(jnp.float32)
    for k in range(1, n_mdl):
        total = total + lax.ppermute(
            term, both, [(i, (i + k) % n_mdl) for i in range(n_mdl)]
        ).astype(jnp.float32)
    pooled = total.astype(jnp.bfloat16)
    n_seq = lax.axis_size("seq")
    adapter = gathered.reshape(n_seq, qkv_weight.shape[0], -1)[:, : adapt_weight.shape[0], :width]
    adapter = adapter.reshape(n_seq * adapt_weight.shape[0], width)
    tokens = jnp.dot(pooled, adapter, preferred_element_type=jnp.float32).astype(jnp.bfloat16)

    tables = rotary_tables(2 * text.shape[0])
    gain = norm_gain.reshape(n_mdl, 1, width)
    order = (mdl - jnp.arange(n_mdl, dtype=jnp.int32)) % n_mdl
    x = jnp.stack(words)
    x = jnp.stack([lax.dynamic_index_in_dim(x, (mdl - i) % n_mdl, 0, keepdims=False) for i in range(n_mdl)])
    q, kt, vt = text_part(x, gain, gathered, qkv_bias[None], tables)
    sounds = [
        lax.ppermute(tokens, both, [(i, n_mdl + (i + k) % n_mdl) for i in range(n_mdl)])
        for k in range(n_mdl)
    ]
    context = audio_part(order, sounds, gain, gathered, qkv_bias[None, -2 * HEAD :], tables, q, kt, vt)
    return jnp.where(grp == 0, tokens, context)[None]


def solution(mesh):
    in_specs = (
        P("seq", None),
        P(),
        P(),
        P(None, None, "mdl"),
        P(None, "mdl"),
        P("mdl", None),
        P("seq", "mdl"),
        P("seq", "mdl"),
        P(),
        P("seq", "mdl"),
        P("mdl"),
    )
    out_specs = P("grp", "seq", "mdl")
    return jax.shard_map(shards, mesh=mesh, in_specs=in_specs, out_specs=out_specs, check_vma=False)
```

time: 311 us -> 164 us (0.53)
  waiting for transfers between devices: 213 us -> 47.6 us
  starting transfers between devices: 13.7 us -> 38.9 us
  Pallas kernels: 0 us -> 12.4 us
  other arithmetic: 23.5 us -> 12.2 us
  local copies, waits for them, and re-layouts: 21.7 us -> 10.9 us
  matrix products: 23 us -> 26.6 us
    all_gather x4 -> x1, waiting for transfers between devices: 183 us -> 34.1 us  [gather_rows(): return lax.all_gather(block, 'seq', axis=0, tiled=True)]
    ppermute x3 -> x12, starting transfers between devices: 13.3 us -> 38.9 us  [the longest x3 13 us: shards(): lax.ppermute(term, both, [(i, (i + k) % n_mdl) for i in range(n_mdl)])]
    reduce_sum x3 -> x0, other arithmetic: 13.2 us -> none  [the longest x1 5.42 us: encode(): jnp.mean(partial_out.reshape(pooled_count, 4, width), axis=1)]
    pallas_call x0 -> x2, Pallas kernels: none -> 12.4 us  [the longest x1 6.57 us: audio_part(): pl.pallas_call(functools.partial(audio_kernel, parts=parts), grid_spec=pl...]
    ppermute x3 -> x12, waiting for transfers between devices: 22.6 us -> 13.5 us  [the longest x4 13.5 us: shards(): lax.ppermute(tokens, both, [(i, n_mdl + (i + k) % n_mdl) for i in range(n...]
    unnamed x29 -> x24, local copies, waits for them, and re-layouts: 9.12 us -> 0.82 us
    psum x1 -> x0, waiting for transfers between devices: 5.35 us -> none  [encode(): lax.psum(pooled_term.astype(jnp.float32).astype(jnp.bfloat16), 'mdl')]
    dot_general x5 -> x2, matrix products: 21.2 us -> 24.8 us  [the longest x1 20.6 us: encode(): jnp.dot(pooled_act, pw_weight, preferred_element_type=jnp.float32)]
  transfers between devices with their start and end apart: 8 -> 13, of which waited for: 7 -> 4; matrix products, arithmetic and copies ran while one was open for 14% -> 26% of each run, Pallas kernels for 0% -> 4%
where the time goes in v1:
time: 164 us; the launch traced here: 163 us
  waiting for transfers between devices  47.6 us (29%)
  starting transfers between devices  38.9 us (24%)
  matrix products  26.6 us (16%)
  between operations  14.5 us (9%)
  Pallas kernels  12.4 us (8%)
  other arithmetic  12.2 us (7%)
  local copies, waits for them, and re-layouts  10.9 us (7%)
    all_gather x1, waiting for transfers between devices, gather_rows(): return lax.all_gather(block, 'seq', axis=0, tiled=True)  34.1 us
    dot_general x1, matrix products, encode(): jnp.dot(pooled_act, pw_weight, preferred_element_type=jnp.float32)  20.6 us
    ppermute x4, waiting for transfers between devices, shards(): lax.ppermute(tokens, both, [(i, n_mdl + (i + k) % n_mdl) for i in range(n...  13.5 us
    ppermute x3, starting transfers between devices, shards(): lax.ppermute(term, both, [(i, (i + k) % n_mdl) for i in range(n_mdl)])  13 us
    ppermute x4, starting transfers between devices, shards(): lax.ppermute(tokens, both, [(i, n_mdl + (i + k) % n_mdl) for i in range(n...  10.7 us
    ppermute x1, starting transfers between devices, encode(): after = lax.ppermute(gated[:margin], 'seq', down)  8.78 us
    pallas_call x1, Pallas kernels, audio_part(): pl.pallas_call(functools.partial(audio_kernel, parts=parts), grid_spec=pl...  6.57 us
    pallas_call x1, Pallas kernels, text_part(): pl.pallas_call(text_kernel, grid=(parts,), in_specs=[pl.BlockSpec((1, cou...  5.78 us
  transfers between devices with their start and end apart: 13, of which 4 were waited for; matrix products, arithmetic and copies ran while one was open for 26% of the time, Pallas kernels for 4%

profile of v1, /device:TPU:1, one launch (start us, length us, event | category | flops | bytes accessed | tf_op | source)
XLA Modules:
  0.0 163.1 jit_solution(9913836422941830530)
XLA Ops:
  6.5 1.6 pad_select_fusion
  8.2 1.4 collective-permute-start.11
  9.6 1.4 collective-permute-start.10
  11.0 1.4 collective-permute-start.9
  13.1 1.9 %convert_reduce_fusion = f32[768]{0:T(1024)S(1)} fusion(bf16[768,1280]{1,0:T(8,128)(2,1)} %param.11), kind=kLoop, calls=%fused_computation.1 | loop fusion | flops 1965312 | bytes 1969152 | tf_op jit(solution)/shard_map/reduce_sum | solution.py:190
  17.1 0.9 fusion.7
  18.0 0.9 fusion.9
  19.0 8.8 %collective-permute-start.1 = (bf16[15,320]{0,1:T(8,128)(2,1)S(1)}, bf16[15,320]{0,1:T(8,128)(2,1)}, u32[]{:S(2)}, u32[]{:S(2)}) collective-permute-start(bf16[15,320]{0,1:T(8,128)(2,1)S(1)} %get-tuple-element.47), channel_id=1, source_target_pairs={{4,0},{8,4},{12,8},{16,12},{20,16},{24,20},{28,24},{32,28},{36,32}... | collective-permute-start | bytes 28808 | tf_op jit(solution)/shard_map/ppermute | solution.py:206
  27.8 2.1 %collective-permute-start = (bf16[15,320]{0,1:T(8,128)(2,1)S(1)}, bf16[15,320]{0,1:T(8,128)(2,1)}, u32[]{:S(2)}, u32[]{:S(2)}) collective-permute-start(bf16[15,320]{0,1:T(8,128)(2,1)S(1)} %get-tuple-element.46), channel_id=1, source_target_pairs={{0,4},{4,8},{8,12},{12,16},{16,20},{20,24},{24,28},{28,32},{32,36}... | collective-permute-start | bytes 28808 | tf_op jit(solution)/shard_map/ppermute | solution.py:205
  30.1 1.4 multiply_sine_fusion
  31.8 20.6 %convolution_convert_fusion = bf16[192,1280]{1,0:T(8,128)(2,1)} fusion(bf16[320,1280]{1,0:T(8,128)(2,1)S(1)} %copy-done, bf16[768,320]{0,1:T(8,128)(2,1)} %copy-done.6, bf16[15,320]{0,1:T(8,128)(2,1)} %collective-permute-done.1, bf16[15,320]{0,1:T(8,128)(2,1)} %collective-permute-done, f32[320]{0:T(512)S(1)} %get-tuple-element.40, ...), kind=kOutput, calls=%fused_computation.36 | convolution fusion | flops 298364928 | bytes 1868032 | tf_op jit(solution)/shard_map/dot_general | solution.py:214
  52.4 6.6 %collective-permute-start.4 = (bf16[192,1280]{1,0:T(8,128)(2,1)}, bf16[192,1280]{1,0:T(8,128)(2,1)}, u32[]{:S(2)}, u32[]{:S(2)}) collective-permute-start(bf16[192,1280]{1,0:T(8,128)(2,1)} %convolution_convert_fusion), channel_id=1, source_target_pairs={{0,3},{1,0},{2,1},{3,2},{4,7},{5,4},{6,5},{7,6},{8,11},{9,8},{10,9... | collective-permute-start | bytes 1474568 | tf_op jit(solution)/shard_map/ppermute | solution.py:244
  59.1 1.9 %collective-permute-start.3 = (bf16[192,1280]{1,0:T(8,128)(2,1)}, bf16[192,1280]{1,0:T(8,128)(2,1)}, u32[]{:S(2)}, u32[]{:S(2)}) collective-permute-start(bf16[192,1280]{1,0:T(8,128)(2,1)} %convolution_convert_fusion), channel_id=1, source_target_pairs={{0,2},{1,3},{2,0},{3,1},{4,6},{5,7},{6,4},{7,5},{8,10},{9,11},{10,... | collective-permute-start | bytes 1474568 | tf_op jit(solution)/shard_map/ppermute | solution.py:244
  61.0 4.5 %collective-permute-start.2 = (bf16[192,1280]{1,0:T(8,128)(2,1)}, bf16[192,1280]{1,0:T(8,128)(2,1)}, u32[]{:S(2)}, u32[]{:S(2)}) collective-permute-start(bf16[192,1280]{1,0:T(8,128)(2,1)} %convolution_convert_fusion), channel_id=1, source_target_pairs={{0,1},{1,2},{2,3},{3,0},{4,5},{5,6},{6,7},{7,4},{8,9},{9,10},{10,1... | collective-permute-start | bytes 1474568 | tf_op jit(solution)/shard_map/ppermute | solution.py:244
  65.5 1.1 fusion.52
  66.6 1.4 pad_maximum_fusion.4
  68.0 2.5 %pad_maximum_fusion = bf16[4,192,896]{2,1,0:T(8,128)(2,1)} fusion(bf16[1,192,896]{2,1,0:T(8,128)(2,1)} %bitcast.8, bf16[1,192,896]{2,1,0:T(8,128)(2,1)} %bitcast.7, bf16[1,192,896]{2,1,0:T(8,128)(2,1)} %bitcast.6, bf16[1,192,896]{2,1,0:T(8,128)(2,1)S(1)} %bitcast.23), kind=kLoop, calls=%fused_computation.37 | loop fusion | flops 2064384 | bytes 2752512 | tf_op jit(solution)/shard_map/stack | solution.py:256
  70.5 34.1 %all-gather.2.cloned.1.call-done.w_ref.refs_5_.refs_6_ = bf16[3584,1152]{1,0:T(8,128)(2,1)} async-done(((bf16[56,1152]{1,0:T(8,128)(2,1)}), bf16[3584,1152]{1,0:T(8,128)(2,1)}) %all-gather.2.cloned.1.call-update) | async-done | bytes 8257552 | tf_op jit(solution)/shard_map/all_gather | solution.py:220
  104.6 3.6 %slice.364 = bf16[64,20,896]{2,1,0:T(8,128)(2,1)} slice(bf16[64,56,1152]{2,1,0:T(8,128)(2,1)} %bitcast.22), slice={[0:64], [0:20], [0:896]} | slice | bytes 4587520 | tf_op jit(solution)/shard_map/slice | solution.py:249
  108.2 4.8 %reshape.39 = bf16[1280,896]{1,0:T(8,128)(2,1)} reshape(bf16[64,20,896]{2,1,0:T(8,128)(2,1)} %slice.364) | data formatting | bytes 4587520 | tf_op jit(solution)/shard_map/reshape | solution.py:250
  113.0 4.2 %convolution_convert_fusion.1 = bf16[192,896]{1,0:T(8,128)(2,1)} fusion(bf16[1280,896]{1,0:T(8,128)(2,1)} %reshape.39, bf16[192,1280]{1,0:T(8,128)(2,1)} %collective-permute-done.4, bf16[192,1280]{1,0:T(8,128)(2,1)} %collective-permute-done.3, bf16[192,1280]{1,0:T(8,128)(2,1)} %collective-permute-done.2, bf16[192,1280]{1,0:T(8,128)(2,1)} %convolution_convert_fusion, ...), kind=kOutput, calls=%fused_computation.46 | convolution fusion | flops 820862976 | bytes 6576896 | tf_op jit(solution)/shard_map/dot_general | solution.py:251
  117.2 3.1 %collective-permute-start.5 = (bf16[192,896]{1,0:T(8,128)(2,1)}, bf16[192,896]{1,0:T(8,128)(2,1)S(1)}, u32[]{:S(2)}, u32[]{:S(2)}) collective-permute-start(bf16[192,896]{1,0:T(8,128)(2,1)} %convolution_convert_fusion.1), channel_id=1, source_target_pairs={{0,256},{1,257},{2,258},{3,259},{4,260},{5,261},{6,262},{7,263},{8... | collective-permute-start | bytes 1032200 | tf_op jit(solution)/shard_map/ppermute | solution.py:260
  120.3 3.5 %collective-permute-start.6 = (bf16[192,896]{1,0:T(8,128)(2,1)}, bf16[192,896]{1,0:T(8,128)(2,1)S(1)}, u32[]{:S(2)}, u32[]{:S(2)}) collective-permute-start(bf16[192,896]{1,0:T(8,128)(2,1)} %convolution_convert_fusion.1), channel_id=1, source_target_pairs={{0,257},{1,258},{2,259},{3,256},{4,261},{5,262},{6,263},{7,260},{8... | collective-permute-start | bytes 1032200 | tf_op jit(solution)/shard_map/ppermute | solution.py:260
  123.8 2.9 %collective-permute-start.7 = (bf16[192,896]{1,0:T(8,128)(2,1)}, bf16[192,896]{1,0:T(8,128)(2,1)S(1)}, u32[]{:S(2)}, u32[]{:S(2)}) collective-permute-start(bf16[192,896]{1,0:T(8,128)(2,1)} %convolution_convert_fusion.1), channel_id=1, source_target_pairs={{0,258},{1,259},{2,256},{3,257},{4,262},{5,263},{6,260},{7,261},{8... | collective-permute-start | bytes 1032200 | tf_op jit(solution)/shard_map/ppermute | solution.py:260
  126.7 1.3 collective-permute-start.8
  128.0 1.4 constant_dynamic-slice_fusion.3
  129.6 5.8 %text_part.1 = (bf16[192,896]{1,0:T(8,128)(2,1)S(1)}, bf16[192,128]{1,0:T(8,128)(2,1)S(1)}, bf16[192,128]{1,0:T(8,128)(2,1)S(1)}) custom-call(bf16[4,192,896]{2,1,0:T(8,128)(2,1)S(1)} %pad_maximum_fusion.1.x_ref, f32[4,1,896]{2,1,0:T(1,128)S(1)} %reshape.40.gain_ref.refs_4_, bf16[3584,1152]{1,0:T(8,128)(2,1)} %all-gather.2.cloned.1.call-done.w_ref.refs_5_.refs_6_, ...), custom_call_target="tpu_custom_call" | custom-call | flops 1585446912 | bytes 9633792 | tf_op jit(solution)/shard_map/text_part/pallas_call | solution.py:115
  135.4 1.4 collective-permute-done.6.refs_1_
  136.8 4.3 %collective-permute-done.7.refs_2_ = bf16[192,896]{1,0:T(8,128)(2,1)S(1)} collective-permute-done((bf16[192,896]{1,0:T(8,128)(2,1)}, bf16[192,896]{1,0:T(8,128)(2,1)S(1)}, u32[]{:S(2)}, u32[]{:S(2)}) %collective-permute-start.7) | collective-permute-done | bytes 344096 | tf_op jit(solution)/shard_map/ppermute | solution.py:260
  141.1 7.8 %collective-permute-done.8.refs_3_ = bf16[192,896]{1,0:T(8,128)(2,1)S(1)} collective-permute-done((bf16[192,896]{1,0:T(8,128)(2,1)}, bf16[192,896]{1,0:T(8,128)(2,1)S(1)}, u32[]{:S(2)}, u32[]{:S(2)}) %collective-permute-start.8) | collective-permute-done | bytes 344096 | tf_op jit(solution)/shard_map/ppermute | solution.py:260
  148.9 6.6 %audio_part.1 = bf16[192,896]{1,0:T(8,128)(2,1)S(1)} custom-call(s32[4]{0:T(128)S(1)} %and_select_fusion.order_ref, bf16[192,896]{1,0:T(8,128)(2,1)S(1)} %collective-permute-done.5.refs_0_, bf16[192,896]{1,0:T(8,128)(2,1)S(1)} %collective-permute-done.6.refs_1_, bf16[192,896]{1,0:T(8,128)(2,1)S(1)} %collective-permute-done.7.refs_2_, ...), custom_call_target="tpu_custom_call" | custom-call | flops 352321536 | bytes 3211264 | tf_op jit(solution)/shard_map/audio_part/pallas_call | solution.py:148
  155.5 0.8 select_bitcast_fusion
  (52 shorter events, 2.7 us)
Async XLA Ops:
  6.5 25.3 %copy-start = (bf16[320,1280]{1,0:T(8,128)(2,1)S(1)}, bf16[320,1280]{1,0:T(8,128)(2,1)}, u32[]{:S(2)}) copy-start(bf16[320,1280]{1,0:T(8,128)(2,1)} %param.16) | copy-start | bytes 2457604
  6.5 8.5 %copy-start.1 = (bf16[768,1280]{1,0:T(8,128)(2,1)S(1)}, bf16[768,1280]{1,0:T(8,128)(2,1)}, u32[]{:S(2)}) copy-start(bf16[768,1280]{1,0:T(8,128)(2,1)} %param.11) | copy-start | bytes 5898244
  6.5 98.1 %all-gather.2.cloned.1.call-start = ((), (), s32[]{:S(2)}) async-start(), calls=%async_computation | async-start | bytes 8386560 | tf_op jit(solution)/shard_map/all_gather | solution.py:220
  8.2 52.8 %collective-permute-start.11 = (bf16[192,896]{1,0:T(8,128)(2,1)}, bf16[192,896]{1,0:T(8,128)(2,1)}, u32[]{:S(2)}, u32[]{:S(2)}) collective-permute-start(bf16[192,896]{1,0:T(8,128)(2,1)} %param.18), channel_id=1, source_target_pairs={{256,259},{257,256},{258,257},{259,258},{260,263},{261,260},{262,2... | collective-permute-start | bytes 1032200 | tf_op jit(solution)/shard_map/ppermute | solution.py:238
  9.6 58.4 %collective-permute-start.10 = (bf16[192,896]{1,0:T(8,128)(2,1)}, bf16[192,896]{1,0:T(8,128)(2,1)}, u32[]{:S(2)}, u32[]{:S(2)}) collective-permute-start(bf16[192,896]{1,0:T(8,128)(2,1)} %param.18), channel_id=1, source_target_pairs={{256,258},{257,259},{258,256},{259,257},{260,262},{261,263},{262,2... | collective-permute-start | bytes 1032200 | tf_op jit(solution)/shard_map/ppermute | solution.py:238
  11.0 57.0 %collective-permute-start.9 = (bf16[192,896]{1,0:T(8,128)(2,1)}, bf16[192,896]{1,0:T(8,128)(2,1)}, u32[]{:S(2)}, u32[]{:S(2)}) collective-permute-start(bf16[192,896]{1,0:T(8,128)(2,1)} %param.18), channel_id=1, source_target_pairs={{256,257},{257,258},{258,259},{259,256},{260,261},{261,262},{262,2... | collective-permute-start | bytes 1032200 | tf_op jit(solution)/shard_map/ppermute | solution.py:238
  13.1 2.6 %copy-start.10 = (f32[1280]{0:T(1024)S(1)}, f32[1280]{0:T(1024)}, u32[]{:S(2)}) copy-start(f32[1280]{0:T(1024)} %param.13) | copy-start | bytes 15364
  15.7 1.4 copy-start.11
  18.0 11.9 %copy-start.7 = (f32[31,320]{1,0:T(8,128)S(1)}, f32[31,320]{1,0:T(8,128)}, u32[]{:S(2)}) copy-start(f32[31,320]{1,0:T(8,128)} %param.15) | copy-start | bytes 119044
  18.0 13.7 %copy-start.9 = (f32[1152]{0:T(1024)S(1)}, f32[1152]{0:T(1024)}, u32[]{:S(2)}) copy-start(f32[1152]{0:T(1024)} %param.21) | copy-start | bytes 13828
  18.0 13.7 %copy-start.8 = (f32[3584]{0:T(1024)S(1)}, f32[3584]{0:T(1024)}, u32[]{:S(2)}) copy-start(f32[3584]{0:T(1024)} %param.19) | copy-start | bytes 43012
  18.9 11.1 %copy-start.6 = (bf16[768,320]{0,1:T(8,128)(2,1)}, bf16[768,320]{0,1:T(8,128)(2,1)S(1)}, u32[]{:S(2)}) copy-start(bf16[768,320]{0,1:T(8,128)(2,1)S(1)} %fusion.9) | copy-start | bytes 1474564
  19.0 12.8 %collective-permute-start.1 = (bf16[15,320]{0,1:T(8,128)(2,1)S(1)}, bf16[15,320]{0,1:T(8,128)(2,1)}, u32[]{:S(2)}, u32[]{:S(2)}) collective-permute-start(bf16[15,320]{0,1:T(8,128)(2,1)S(1)} %get-tuple-element.47), channel_id=1, source_target_pairs={{4,0},{8,4},{12,8},{16,12},{20,16},{24,20},{28,24},{32,28},{36,32}... | collective-permute-start | bytes 28808 | tf_op jit(solution)/shard_map/ppermute | solution.py:206
  27.8 4.0 %collective-permute-start = (bf16[15,320]{0,1:T(8,128)(2,1)S(1)}, bf16[15,320]{0,1:T(8,128)(2,1)}, u32[]{:S(2)}, u32[]{:S(2)}) collective-permute-start(bf16[15,320]{0,1:T(8,128)(2,1)S(1)} %get-tuple-element.46), channel_id=1, source_target_pairs={{0,4},{4,8},{8,12},{12,16},{16,20},{20,24},{24,28},{28,32},{32,36}... | collective-permute-start | bytes 28808 | tf_op jit(solution)/shard_map/ppermute | solution.py:205
  31.6 33.9 %copy-start.2 = (f32[384,64]{1,0:T(8,128)}, f32[384,64]{1,0:T(8,128)S(1)}, u32[]{:S(2)}) copy-start(f32[384,64]{1,0:T(8,128)S(1)} %get-tuple-element.48) | copy-start | bytes 294916
  31.6 33.9 %copy-start.3 = (f32[384,64]{1,0:T(8,128)}, f32[384,64]{1,0:T(8,128)S(1)}, u32[]{:S(2)}) copy-start(f32[384,64]{1,0:T(8,128)S(1)} %get-tuple-element.49) | copy-start | bytes 294916
  52.4 15.6 %copy-start.5 = (bf16[192,896]{1,0:T(8,128)(2,1)S(1)}, bf16[192,896]{1,0:T(8,128)(2,1)}, u32[]{:S(2)}) copy-start(bf16[192,896]{1,0:T(8,128)(2,1)} %param.18) | copy-start | bytes 1032196
  52.4 60.6 %collective-permute-start.4 = (bf16[192,1280]{1,0:T(8,128)(2,1)}, bf16[192,1280]{1,0:T(8,128)(2,1)}, u32[]{:S(2)}, u32[]{:S(2)}) collective-permute-start(bf16[192,1280]{1,0:T(8,128)(2,1)} %convolution_convert_fusion), channel_id=1, source_target_pairs={{0,3},{1,0},{2,1},{3,2},{4,7},{5,4},{6,5},{7,6},{8,11},{9,8},{10,9... | collective-permute-start | bytes 1474568 | tf_op jit(solution)/shard_map/ppermute | solution.py:244
  59.1 54.0 %collective-permute-start.3 = (bf16[192,1280]{1,0:T(8,128)(2,1)}, bf16[192,1280]{1,0:T(8,128)(2,1)}, u32[]{:S(2)}, u32[]{:S(2)}) collective-permute-start(bf16[192,1280]{1,0:T(8,128)(2,1)} %convolution_convert_fusion), channel_id=1, source_target_pairs={{0,2},{1,3},{2,0},{3,1},{4,6},{5,7},{6,4},{7,5},{8,10},{9,11},{10,... | collective-permute-start | bytes 1474568 | tf_op jit(solution)/shard_map/ppermute | solution.py:244
  61.0 52.0 %collective-permute-start.2 = (bf16[192,1280]{1,0:T(8,128)(2,1)}, bf16[192,1280]{1,0:T(8,128)(2,1)}, u32[]{:S(2)}, u32[]{:S(2)}) collective-permute-start(bf16[192,1280]{1,0:T(8,128)(2,1)} %convolution_convert_fusion), channel_id=1, source_target_pairs={{0,1},{1,2},{2,3},{3,0},{4,5},{5,6},{6,7},{7,4},{8,9},{9,10},{10,1... | collective-permute-start | bytes 1474568 | tf_op jit(solution)/shard_map/ppermute | solution.py:244
  117.2 18.2 %collective-permute-start.5 = (bf16[192,896]{1,0:T(8,128)(2,1)}, bf16[192,896]{1,0:T(8,128)(2,1)S(1)}, u32[]{:S(2)}, u32[]{:S(2)}) collective-permute-start(bf16[192,896]{1,0:T(8,128)(2,1)} %convolution_convert_fusion.1), channel_id=1, source_target_pairs={{0,256},{1,257},{2,258},{3,259},{4,260},{5,261},{6,262},{7,263},{8... | collective-permute-start | bytes 1032200 | tf_op jit(solution)/shard_map/ppermute | solution.py:260
  120.3 16.5 %collective-permute-start.6 = (bf16[192,896]{1,0:T(8,128)(2,1)}, bf16[192,896]{1,0:T(8,128)(2,1)S(1)}, u32[]{:S(2)}, u32[]{:S(2)}) collective-permute-start(bf16[192,896]{1,0:T(8,128)(2,1)} %convolution_convert_fusion.1), channel_id=1, source_target_pairs={{0,257},{1,258},{2,259},{3,256},{4,261},{5,262},{6,263},{7,260},{8... | collective-permute-start | bytes 1032200 | tf_op jit(solution)/shard_map/ppermute | solution.py:260
  123.8 17.3 %collective-permute-start.7 = (bf16[192,896]{1,0:T(8,128)(2,1)}, bf16[192,896]{1,0:T(8,128)(2,1)S(1)}, u32[]{:S(2)}, u32[]{:S(2)}) collective-permute-start(bf16[192,896]{1,0:T(8,128)(2,1)} %convolution_convert_fusion.1), channel_id=1, source_target_pairs={{0,258},{1,259},{2,256},{3,257},{4,262},{5,263},{6,260},{7,261},{8... | collective-permute-start | bytes 1032200 | tf_op jit(solution)/shard_map/ppermute | solution.py:260
  126.7 22.2 %collective-permute-start.8 = (bf16[192,896]{1,0:T(8,128)(2,1)}, bf16[192,896]{1,0:T(8,128)(2,1)S(1)}, u32[]{:S(2)}, u32[]{:S(2)}) collective-permute-start(bf16[192,896]{1,0:T(8,128)(2,1)} %convolution_convert_fusion.1), channel_id=1, source_target_pairs={{0,259},{1,256},{2,257},{3,258},{4,263},{5,260},{6,261},{7,262},{8... | collective-permute-start | bytes 1032200 | tf_op jit(solution)/shard_map/ppermute | solution.py:260
  148.9 6.6 %copy-start.4 = (bf16[192,896]{1,0:T(8,128)(2,1)S(1)}, bf16[192,896]{1,0:T(8,128)(2,1)}, u32[]{:S(2)}) copy-start(bf16[192,896]{1,0:T(8,128)(2,1)} %convolution_convert_fusion.1) | copy-start | bytes 1032196
Sparse Core Ops, SparseCore 0:
  10.6 93.9 all-gather.1

commit v2 on v1

--- a/solution.py
+++ b/solution.py
@@ -11,6 +11,10 @@
 KV = 4
 HEAD = 128
 VMEM = 48 * 1024 * 1024
+NX = 4
+NY = 8
+ADAPT_SLOT = 48
+ADAPT_COLS = 896
 
 
 def rotary_tables(count):
@@ -25,7 +29,9 @@
     return values * cosine + pltpu.roll(values, HEAD // 2, 1) * sine
 
 
-def text_kernel(x_ref, gain_ref, w_ref, bias_ref, cos_ref, sin_ref, q_ref, k_ref, v_ref, acc, square):
+def text_kernel(order_ref, *refs, parts):
+    xs = refs[:parts]
+    gain_ref, w_ref, bias_ref, cos_ref, sin_ref, q_ref, k_ref, v_ref, acc, square = refs[parts:]
     step = pl.program_id(0)
 
     @pl.when(step == 0)
@@ -33,15 +39,19 @@
         acc[...] = jnp.zeros_like(acc)
         square[...] = jnp.zeros_like(square)
 
-    x = x_ref[0].astype(jnp.float32)
-    square[...] += jnp.sum(x * x, axis=1, keepdims=True)
-    acc[...] += jnp.dot(
-        (x * gain_ref[0]).astype(jnp.bfloat16), w_ref[...], preferred_element_type=jnp.float32
-    )
+    for i in range(parts):
+
+        @pl.when(step == i)
+        def _():
+            x = xs[i][...].astype(jnp.float32)
+            square[...] += jnp.sum(x * x, axis=1, keepdims=True)
+            acc[...] += jnp.dot(
+                (x * gain_ref[0]).astype(jnp.bfloat16), w_ref[...], preferred_element_type=jnp.float32
+            )
 
     @pl.when(step == pl.num_programs(0) - 1)
     def _():
-        scale = lax.rsqrt(square[...] / (pl.num_programs(0) * x.shape[1]) + 1e-6)
+        scale = lax.rsqrt(square[...] / (parts * xs[0].shape[1]) + 1e-6)
         cosine, sine = cos_ref[...], sin_ref[...]
         heads = q_ref.shape[1] // HEAD
         for h in range(heads + 2):
@@ -106,36 +116,40 @@
             ).astype(jnp.bfloat16)
 
 
-def text_part(x, gain, weight, bias, tables):
-    parts, count, width = x.shape
+def text_part(order, xs, gain, weight, bias, tables):
+    parts = len(xs)
+    count, width = xs[0].shape
     total = weight.shape[1]
     heads = total // HEAD - 2
     cosine, sine = tables
-    whole = lambda *shape: pl.BlockSpec(shape, lambda k: (0,) * len(shape))
-    return pl.pallas_call(
-        text_kernel,
-        grid=(parts,),
-        in_specs=[
-            pl.BlockSpec((1, count, width), lambda k: (k, 0, 0)),
-            pl.BlockSpec((1, 1, width), lambda k: (k, 0, 0)),
-            pl.BlockSpec((width, total), lambda k: (k, 0)),
-            whole(1, total),
-            pl.BlockSpec((count, HEAD), lambda k: (1, 0)),
-            pl.BlockSpec((count, HEAD), lambda k: (1, 0)),
-        ],
-        out_specs=[whole(count, heads * HEAD), whole(count, HEAD), whole(count, HEAD)],
+    whole = lambda *shape: pl.BlockSpec(shape, lambda k, o: (0,) * len(shape))
+    return pl.pallas_call(
+        functools.partial(text_kernel, parts=parts),
+        grid_spec=pltpu.PrefetchScalarGridSpec(
+            num_scalar_prefetch=1,
+            grid=(parts,),
+            in_specs=[whole(count, width)] * parts
+            + [
+                pl.BlockSpec((1, 1, width), lambda k, o: (o[k], 0, 0)),
+                pl.BlockSpec((width, total), lambda k, o: (o[k], 0)),
+                whole(1, total),
+                whole(count, HEAD),
+                whole(count, HEAD),
+            ],
+            out_specs=[whole(count, heads * HEAD), whole(count, HEAD), whole(count, HEAD)],
+            scratch_shapes=[pltpu.VMEM((count, total), jnp.float32), pltpu.VMEM((count, 1), jnp.float32)],
+        ),
         out_shape=[
             jax.ShapeDtypeStruct((count, heads * HEAD), jnp.bfloat16),
             jax.ShapeDtypeStruct((count, HEAD), jnp.bfloat16),
             jax.ShapeDtypeStruct((count, HEAD), jnp.bfloat16),
         ],
-        scratch_shapes=[pltpu.VMEM((count, total), jnp.float32), pltpu.VMEM((count, 1), jnp.float32)],
         compiler_params=pltpu.CompilerParams(vmem_limit_bytes=VMEM),
         cost_estimate=pl.CostEstimate(
             flops=2 * count * parts * width * total, bytes_accessed=2 * parts * width * (total + count), transcendentals=0
         ),
         name="text_part",
-    )(x, gain, weight, bias, cosine, sine)
+    )(order, *xs, gain, weight, bias, cosine[count:], sine[count:])
 
 
 def audio_part(order, xs, gain, weight, bias, tables, q, kt, vt):
@@ -181,43 +195,214 @@
 def pooling(rows):
     r = lax.broadcasted_iota(jnp.int32, (rows // 4, rows), 0)
     c = lax.broadcasted_iota(jnp.int32, (rows // 4, rows), 1)
-    return jnp.where(c // 4 == r, 0.25, 0.0).astype(jnp.bfloat16)
-
-
-def encode(audio, frame_count, ln_gain, glu_weight, dw_kernel, pw_weight):
-    frames_dev = audio.shape[0]
+    return jnp.where((c >= 4 * r) & (c < 4 * r + 4), 0.25, 0.0).astype(jnp.bfloat16)
+
+
+def dot_t(a, b):
+    return lax.dot_general(a, b, (((1,), (1,)), ((), ())), preferred_element_type=jnp.float32)
+
+
+def gate_kernel(count_ref, audio_ref, gain_ref, weight_ref, gated_ref, pooled_ref):
+    audio = audio_ref[...]
     rows = audio.astype(jnp.float32)
-    centred = rows - jnp.mean(rows, axis=-1, keepdims=True)
-    spread = jnp.mean(centred * centred, axis=-1, keepdims=True)
-    normed = (centred * lax.rsqrt(spread + 1e-05) * ln_gain).astype(jnp.bfloat16)
-    first_frame = lax.axis_index("seq") * frames_dev
-    valid = (first_frame + jnp.arange(frames_dev, dtype=jnp.int32) < frame_count[0]).astype(
-        jnp.float32
-    )
-    left = jnp.dot(normed, glu_weight[0], preferred_element_type=jnp.float32)
-    right = jnp.dot(normed, glu_weight[1], preferred_element_type=jnp.float32)
-    gated = (left * jax.nn.sigmoid(right) * valid[:, None]).astype(jnp.bfloat16)
-    taps = dw_kernel.shape[0]
-    margin = (taps - 1) // 2
-    count = lax.axis_size("seq")
-    up = [(i, i + 1) for i in range(count - 1)]
-    down = [(j, i) for i, j in up]
-    before = lax.ppermute(gated[frames_dev - margin :], "seq", up)
-    after = lax.ppermute(gated[:margin], "seq", down)
-    padded = jnp.concatenate([before, gated, after], axis=0)
-    conv = jnp.zeros(gated.shape, jnp.float32)
-    for offset in range(taps):
-        conv = conv + padded[offset : offset + frames_dev].astype(jnp.float32) * dw_kernel[offset]
-    act = (conv * jax.nn.sigmoid(conv)).astype(jnp.bfloat16)
-    pool = pooling(frames_dev)
-    pooled_act = jnp.dot(pool, act, preferred_element_type=jnp.float32).astype(jnp.bfloat16)
-    term = jnp.dot(pooled_act, pw_weight, preferred_element_type=jnp.float32).astype(jnp.bfloat16)
-    pooled_audio = jnp.dot(pool, audio, preferred_element_type=jnp.float32)
-    return term, pooled_audio
-
-
-def gather_rows(block):
-    return lax.all_gather(block, "seq", axis=0, tiled=True)
+    centred = rows - jnp.mean(rows, axis=1, keepdims=True)
+    spread = jnp.mean(centred * centred, axis=1, keepdims=True)
+    normed = (centred * lax.rsqrt(spread + 1e-5) * gain_ref[...]).astype(jnp.bfloat16)
+    left = dot_t(normed, weight_ref[0])
+    right = dot_t(normed, weight_ref[1])
+    frame = pl.program_id(0) * rows.shape[0] + lax.broadcasted_iota(jnp.int32, (rows.shape[0], 1), 0)
+    gated = left * (1.0 / (1.0 + jnp.exp(-right)))
+    gated_ref[...] = jnp.where(frame < count_ref[0], gated, 0.0).astype(gated_ref.dtype)
+    pooled_ref[...] = jnp.dot(pooling(rows.shape[0]), audio, preferred_element_type=jnp.float32)
+
+
+def gate(left_frames, audio, gain, weight):
+    frames, width = audio.shape
+    columns = weight.shape[1]
+    block = 256
+    return pl.pallas_call(
+        gate_kernel,
+        grid=(frames // block,),
+        in_specs=[
+            pl.BlockSpec(memory_space=pltpu.SMEM),
+            pl.BlockSpec((block, width), lambda i: (i, 0)),
+            pl.BlockSpec((1, width), lambda i: (0, 0)),
+            pl.BlockSpec((2, columns, width), lambda i: (0, 0, 0)),
+        ],
+        out_specs=[
+            pl.BlockSpec((block, columns), lambda i: (i, 0)),
+            pl.BlockSpec((block // 4, width), lambda i: (i, 0)),
+        ],
+        out_shape=[
+            jax.ShapeDtypeStruct((frames, columns), jnp.bfloat16),
+            jax.ShapeDtypeStruct((frames // 4, width), jnp.float32),
+        ],
+        compiler_params=pltpu.CompilerParams(vmem_limit_bytes=VMEM),
+        cost_estimate=pl.CostEstimate(
+            flops=4 * frames * width * columns, bytes_accessed=2 * frames * width * 4, transcendentals=frames * columns
+        ),
+        name="gate",
+    )(left_frames, audio, gain, weight)
+
+
+EDGE = 16
+
+
+def conv_kernel(before_ref, gated_ref, after_ref, taps_ref, pw_ref, *refs):
+    term_ref, padded, act = refs[-3:]
+    frames, columns = gated_ref.shape
+    taps = taps_ref.shape[0]
+    padded[:EDGE] = before_ref[...].astype(jnp.float32)
+    padded[EDGE : EDGE + frames] = gated_ref[...].astype(jnp.float32)
+    padded[EDGE + frames :] = after_ref[...].astype(jnp.float32)
+    chunk = 64
+    lead = EDGE - (taps - 1) // 2
+    for at in range(0, columns, 128):
+        lanes = slice(at, min(at + 128, columns))
+
+        def body(i, carry, lanes=lanes):
+            first = pl.multiple_of(i * chunk, chunk)
+            window = padded[pl.ds(first, chunk + 2 * EDGE), lanes]
+            total = jnp.zeros((chunk, window.shape[1]), jnp.float32)
+            for turn in range(8):
+                turned_by = window if turn == 0 else pltpu.roll(window, window.shape[0] - turn, 0)
+                for offset in range(turn, lead + taps, 8):
+                    if offset >= lead:
+                        start = offset - turn
+                        total = total + turned_by[start : start + chunk] * taps_ref[offset - lead, lanes][None]
+            value = total * (1.0 / (1.0 + jnp.exp(-total)))
+            act[pl.ds(first, chunk), lanes] = value.astype(jnp.bfloat16)
+            return carry
+
+        lax.fori_loop(0, frames // chunk, body, 0)
+    pooled = jnp.dot(pooling(frames), act[...], preferred_element_type=jnp.float32).astype(jnp.bfloat16)
+    term_ref[...] = jnp.dot(pooled, pw_ref[...], preferred_element_type=jnp.float32).astype(term_ref.dtype)
+
+
+def conv(before, gated, after, taps, pw, *after_these):
+    frames, columns = gated.shape
+    vmem = pl.BlockSpec(memory_space=pltpu.VMEM)
+    return pl.pallas_call(
+        conv_kernel,
+        in_specs=[vmem] * 5 + [pl.BlockSpec(memory_space=pl.ANY)] * len(after_these),
+        out_specs=vmem,
+        out_shape=jax.ShapeDtypeStruct((frames // 4, pw.shape[1]), jnp.bfloat16),
+        scratch_shapes=[
+            pltpu.VMEM((frames + 2 * EDGE, columns), jnp.float32),
+            pltpu.VMEM((frames, columns), jnp.bfloat16),
+        ],
+        compiler_params=pltpu.CompilerParams(vmem_limit_bytes=VMEM),
+        cost_estimate=pl.CostEstimate(
+            flops=5_000_000_000, bytes_accessed=2 * frames * columns * 4, transcendentals=frames * columns
+        ),
+        name="conv",
+    )(before, gated, after, taps, pw, *after_these)
+
+
+def place(shift_x, shift_y):
+    return [
+        ((x * NY + y) * 2 + c, ((x + shift_x) % NX * NY + (y + shift_y) % NY) * 2 + c)
+        for x in range(NX)
+        for y in range(NY)
+        for c in range(2)
+    ]
+
+
+SWAP = [(i, i ^ 1) for i in range(NX * NY * 2)]
+
+
+def of_group(group, pairs):
+    count = NX * NY * 2
+    return [(group * count + i, group * count + j) for i, j in pairs]
+
+
+def spread(block):
+    send = lambda v, dx, dy: lax.ppermute(v, "seq", place(dx, dy))
+    near = jnp.concatenate([send(block, 0, 1), block, send(block, 0, -1)], axis=0)
+    before = send(near, -1, 0)
+    behind = send(near, 1, 0)
+    far = jnp.concatenate([send(near, 0, 3), send(near[:2], 0, -3)], axis=0)
+    inner, outer = [-1, 0, 1], [-4, -3, -2, 2, 3]
+    before_far = send(far, -1, 0)
+    behind_far = send(far, 1, 0)
+    second = send(before, -1, 0)
+    groups = ("grp", "seq")
+    second_far = lax.ppermute(behind_far, groups, of_group(1, place(1, 0)))
+    direct = lax.ppermute(far[:, :ADAPT_SLOT, :ADAPT_COLS], groups, of_group(0, place(2, 0)))
+    pieces = [
+        (0, inner, near),
+        (0, outer, far),
+        (-1, inner, behind),
+        (1, inner, before),
+        (-1, outer, behind_far),
+        (1, outer, before_far),
+        (2, inner, second),
+        (2, outer, second_far),
+    ]
+    return pieces, direct
+
+
+def join_kernel(index_ref, *refs, counts):
+    ins, out, sem = refs[: len(counts)], refs[len(counts)], refs[len(counts) + 1]
+    copies = []
+    at = 0
+    for ref, count in zip(ins, counts, strict=True):
+        for j in range(count):
+            copy = pltpu.make_async_copy(ref.at[j], out.at[index_ref[at]], sem.at[at])
+            copy.start()
+            copies.append(copy)
+            at += 1
+    for copy in copies:
+        copy.wait()
+
+
+def join(index, pieces):
+    counts = [p.shape[0] for p in pieces]
+    rows, columns = pieces[0].shape[1:]
+    total = sum(counts)
+    return pl.pallas_call(
+        functools.partial(join_kernel, counts=counts),
+        in_specs=[pl.BlockSpec(memory_space=pltpu.SMEM)] + [pl.BlockSpec(memory_space=pl.ANY)] * len(pieces),
+        out_specs=pl.BlockSpec(memory_space=pl.ANY),
+        out_shape=jax.ShapeDtypeStruct((total, rows, columns), pieces[0].dtype),
+        scratch_shapes=[pltpu.SemaphoreType.DMA((total,))],
+        cost_estimate=pl.CostEstimate(flops=0, bytes_accessed=4 * total * rows * columns, transcendentals=0),
+        name="join",
+    )(index, *pieces)
+
+
+def tokens_kernel(*refs, counts):
+    pieces = refs[: len(counts)]
+    audio_ref, term_ref, other_ref, expand_ref = refs[len(counts) : len(counts) + 4]
+    out_ref, weight = refs[-2:]
+    at = 0
+    for ref, count in zip(pieces, counts, strict=True):
+        weight[at : at + count * ADAPT_SLOT] = ref[...].reshape(count * ADAPT_SLOT, ADAPT_COLS)
+        at += count * ADAPT_SLOT
+    pooled = (audio_ref[...] + term_ref[...] + other_ref[...].astype(jnp.float32)).astype(jnp.bfloat16)
+    ordered = jnp.dot(pooled, expand_ref[...], preferred_element_type=jnp.float32).astype(jnp.bfloat16)
+    out_ref[...] = jnp.dot(ordered, weight[...], preferred_element_type=jnp.float32).astype(out_ref.dtype)
+
+
+def tokens_part(pieces, pooled_audio, term, other, expand, *after_these):
+    counts = [p.shape[0] for p in pieces]
+    count = pooled_audio.shape[0]
+    whole = lambda *shape: pl.BlockSpec(shape, lambda k: (0,) * len(shape))
+    return pl.pallas_call(
+        functools.partial(tokens_kernel, counts=counts),
+        grid=(1,),
+        in_specs=[whole(n, ADAPT_SLOT, ADAPT_COLS) for n in counts]
+        + [whole(*v.shape) for v in (pooled_audio, term, other, expand)]
+        + [pl.BlockSpec(memory_space=pl.ANY)] * len(after_these),
+        out_specs=whole(count, ADAPT_COLS),
+        out_shape=jax.ShapeDtypeStruct((count, ADAPT_COLS), jnp.bfloat16),
+        scratch_shapes=[pltpu.VMEM((sum(counts) * ADAPT_SLOT, ADAPT_COLS), jnp.bfloat16)],
+        compiler_params=pltpu.CompilerParams(vmem_limit_bytes=VMEM),
+        cost_estimate=pl.CostEstimate(
+            flops=2 * count * sum(counts) * ADAPT_SLOT * (ADAPT_COLS + expand.shape[0]), bytes_accessed=8000000, transcendentals=0
+        ),
+        name="tokens_part",
+    )(*pieces, pooled_audio, term, other, expand, *after_these)
 
 
 def shards(
@@ -225,42 +410,69 @@
 ):
     grp = lax.axis_index("grp")
     mdl = lax.axis_index("mdl")
+    seq = lax.axis_index("seq")
+    core, y, x = seq % 2, seq // 2 % NY, seq // (2 * NY)
     n_mdl = lax.axis_size("mdl")
     both = ("grp", "mdl")
-    width = adapt_weight.shape[1]
-    held = jnp.pad(
-        adapt_weight,
-        ((0, qkv_weight.shape[0] - adapt_weight.shape[0]), (0, qkv_weight.shape[1] - width)),
+    rows, width = adapt_weight.shape
+    ring = lambda group, k: [(group * n_mdl + i, group * n_mdl + (i + k) % n_mdl) for i in range(n_mdl)]
+
+    twin = lax.ppermute(adapt_weight, ("grp", "seq"), of_group(0, SWAP))
+    held = jnp.where(
+        core == 0, jnp.concatenate([adapt_weight, twin]), jnp.concatenate([twin, adapt_weight])
     )
-    gathered = gather_rows(jnp.where(grp == 0, held, qkv_weight))
-
-    words = [text] + [
-        lax.ppermute(text, both, [(n_mdl + i, n_mdl + (i + k) % n_mdl) for i in range(n_mdl)])
-        for k in range(1, n_mdl)
+    held = jnp.pad(held, ((0, qkv_weight.shape[0] - 2 * rows), (0, qkv_weight.shape[1] - width)))
+    pieces, direct = spread(jnp.where(grp == 0, held, qkv_weight)[None])
+
+    behind = lax.ppermute(text, both, ring(1, 1))
+    ahead = lax.ppermute(text, both, ring(1, -1))
+    second = lax.ppermute(behind, both, ring(1, 1))
+    words = [text, ahead, second, behind]
+
+    frames = audio.shape[0]
+    gated, pooled_audio = gate(
+        frame_count - seq * frames, audio, ln_gain[None], jnp.swapaxes(glu_weight, 1, 2)
+    )
+    up = [(i, i + 1) for i in range(lax.axis_size("seq") - 1)]
+    before_edge = lax.ppermute(gated[frames - EDGE :], ("grp", "seq"), of_group(0, up))
+    after_edge = lax.ppermute(gated[:EDGE], ("grp", "seq"), of_group(0, [(j, i) for i, j in up]))
+    term = conv(before_edge, gated, after_edge, dw_kernel, pw_weight, pieces[0][2], behind, ahead)
+    term = term.astype(jnp.float32) + lax.ppermute(
+        term, both, [(0, 1), (1, 0), (2, 3), (3, 2)]
+    ).astype(jnp.float32)
+    other = lax.ppermute(term.astype(jnp.bfloat16), both, [(1, 2), (2, 1), (3, 0), (0, 3)])
+
+    chips = jnp.concatenate(
+        [
+            jnp.stack([(x + dx) % NX * NY + (y + dy) % NY for dy in steps])
+            for dx, steps, _ in pieces
+        ]
+    )
+    column = jnp.arange(chips.shape[0] * ADAPT_SLOT, dtype=jnp.int32) % ADAPT_SLOT
+    source = jnp.where(column < 2 * rows, jnp.repeat(chips, ADAPT_SLOT) * 2 * rows + column, -1)
+    expand = (jnp.arange(audio.shape[1], dtype=jnp.int32)[:, None] == source[None]).astype(jnp.bfloat16)
+    tokens = tokens_part([p for _, _, p in pieces[:-1]] + [direct], pooled_audio, term, other, expand, second)
+
+    own = [p for _, _, p in pieces]
+    swap = lambda v: lax.ppermute(v, ("grp", "seq"), of_group(1, SWAP))
+    exchanged = [
+        swap(jnp.concatenate(own[:4], axis=0)),
+        swap(jnp.concatenate(own[4:7], axis=0)),
+        swap(own[7]),
     ]
-    term, pooled_audio = encode(audio, frame_count, ln_gain, glu_weight, dw_kernel, pw_weight)
-    total = pooled_audio + term.astype(jnp.float32)
-    for k in range(1, n_mdl):
-        total = total + lax.ppermute(
-            term, both, [(i, (i + k) % n_mdl) for i in range(n_mdl)]
-        ).astype(jnp.float32)
-    pooled = total.astype(jnp.bfloat16)
-    n_seq = lax.axis_size("seq")
-    adapter = gathered.reshape(n_seq, qkv_weight.shape[0], -1)[:, : adapt_weight.shape[0], :width]
-    adapter = adapter.reshape(n_seq * adapt_weight.shape[0], width)
-    tokens = jnp.dot(pooled, adapter, preferred_element_type=jnp.float32).astype(jnp.bfloat16)
+    index = jnp.concatenate([chips * 2 + core, chips * 2 + 1 - core])
+    weight = join(index, own + exchanged).reshape(-1, qkv_weight.shape[1])
 
     tables = rotary_tables(2 * text.shape[0])
     gain = norm_gain.reshape(n_mdl, 1, width)
-    order = (mdl - jnp.arange(n_mdl, dtype=jnp.int32)) % n_mdl
-    x = jnp.stack(words)
-    x = jnp.stack([lax.dynamic_index_in_dim(x, (mdl - i) % n_mdl, 0, keepdims=False) for i in range(n_mdl)])
-    q, kt, vt = text_part(x, gain, gathered, qkv_bias[None], tables)
-    sounds = [
-        lax.ppermute(tokens, both, [(i, n_mdl + (i + k) % n_mdl) for i in range(n_mdl)])
-        for k in range(n_mdl)
-    ]
-    context = audio_part(order, sounds, gain, gathered, qkv_bias[None, -2 * HEAD :], tables, q, kt, vt)
+    order = (mdl + jnp.arange(n_mdl, dtype=jnp.int32)) % n_mdl
+    q, kt, vt = text_part(order, words, gain, weight, qkv_bias[None], tables)
+    same = lax.ppermute(tokens, both, [(i, n_mdl + i) for i in range(n_mdl)])
+    following = lax.ppermute(tokens, both, [(i, n_mdl + (i - 1) % n_mdl) for i in range(n_mdl)])
+    across = lax.ppermute(following, both, ring(1, -1))
+    last = lax.ppermute(same, both, ring(1, 1))
+    sounds = [same, following, across, last]
+    context = audio_part(order, sounds, gain, weight, qkv_bias[None, -2 * HEAD :], tables, q, kt, vt)
     return jnp.where(grp == 0, tokens, context)[None]
 
 

time: 164 us -> 425 us (2.59); the launches traced: 163 us -> 418 us
  Pallas kernels: 12.4 us -> 279 us
  starting transfers between devices: 38.9 us -> 80.6 us
  matrix products: 26.6 us -> 0 us
  waiting for transfers between devices: 47.6 us -> 34.3 us
  between operations: 14.5 us -> 1.54 us
    pallas_call x1 -> x5, Pallas kernels: 5.78 us -> 272 us  [the longest x1 253 us: join(): pl.pallas_call(functools.partial(join_kernel, counts=counts), in_specs=[p...]
    ppermute x12 -> x26, starting transfers between devices: 38.9 us -> 80.6 us  [the longest x9 29.6 us: spread(): send = lambda v, dx, dy: lax.ppermute(v, 'seq', place(dx, dy))]
    all_gather x1 -> x0, waiting for transfers between devices: 34.1 us -> none  [gather_rows(): return lax.all_gather(block, 'seq', axis=0, tiled=True)]
    dot_general x4 -> x0, matrix products: 26.6 us -> none  [the longest x1 20.6 us: encode(): jnp.dot(pooled_act, pw_weight, preferred_element_type=jnp.float32)]
    ppermute x12 -> x26, waiting for transfers between devices: 13.5 us -> 34.3 us  [the longest x9 27.6 us: spread(): send = lambda v, dx, dy: lax.ppermute(v, 'seq', place(dx, dy))]
    unnamed x24 -> x56, local copies, waits for them, and re-layouts: 0.82 us -> 11.2 us
    reshape x1 -> x0, local copies, waits for them, and re-layouts: 4.75 us -> none  [shards(): adapter = adapter.reshape(n_seq * adapt_weight.shape[0], width)]
  transfers between devices with their start and end apart: 13 -> 26, of which waited for: 4 -> 4; matrix products, arithmetic and copies ran while one was open for 26% -> 4% of each run, Pallas kernels for 4% -> 65%
where the time goes in v2:
time: 425 us; the launch traced here: 418 us
  Pallas kernels  279 us (66%)
  starting transfers between devices  80.6 us (19%)
  waiting for transfers between devices  34.3 us (8%)
  local copies, waits for them, and re-layouts  13.8 us (3%)
  other arithmetic  8.71 us (2%)
    pallas_call x1, Pallas kernels, join(): pl.pallas_call(functools.partial(join_kernel, counts=counts), in_specs=[p...  253 us
    ppermute x9, starting transfers between devices, spread(): send = lambda v, dx, dy: lax.ppermute(v, 'seq', place(dx, dy))  29.6 us
    ppermute x9, waiting for transfers between devices, spread(): send = lambda v, dx, dy: lax.ppermute(v, 'seq', place(dx, dy))  27.6 us
    unnamed x56, local copies, waits for them, and re-layouts  11.2 us
    ppermute x1, starting transfers between devices, shards(): lax.ppermute(term.astype(jnp.bfloat16), both, [(1, 2), (2, 1), (3, 0), (0...  10.9 us
    ppermute x1, starting transfers between devices, shards(): twin = lax.ppermute(adapt_weight, ('grp', 'seq'), of_group(0, SWAP))  8.79 us
  transfers between devices with their start and end apart: 26, of which 4 were waited for; matrix products, arithmetic and copies ran while one was open for 4% of the time, Pallas kernels for 65%

profile of v2, /device:TPU:1, one launch (start us, length us, event | category | flops | bytes accessed | tf_op | source)
XLA Modules:
  0.0 417.9 jit_solution(12358430102383094300)
XLA Ops:
  2.1 8.8 %collective-permute-start = (bf16[20,896]{1,0:T(8,128)(2,1)}, bf16[20,896]{1,0:T(8,128)(2,1)S(1)}, u32[]{:S(2)}, u32[]{:S(2)}) collective-permute-start(bf16[20,896]{1,0:T(8,128)(2,1)} %param.17), channel_id=1, source_target_pairs={{0,4},{4,0},{8,12},{12,8},{16,20},{20,16},{24,28},{28,24},{32,36},... | collective-permute-start | bytes 107528 | tf_op jit(solution)/shard_map/ppermute | solution.py:420
  12.2 1.5 copy-done.17
  15.2 3.8 gate.1
  20.0 2.0 collective-permute-start.11
  22.7 1.9 collective-permute-start.2
  24.7 3.4 collective-permute-start.1
  29.2 3.2 collective-permute-start.12
  32.5 1.9 collective-permute-start.3
  36.4 2.6 collective-permute-start.5
  39.0 3.9 collective-permute-start.6
  42.9 6.4 %collective-permute-start.4 = (bf16[2,56,1152]{2,1,0:T(8,128)(2,1)S(1)}, bf16[2,56,1152]{2,1,0:T(8,128)(2,1)S(1)}, u32[]{:S(2)}, u32[]{:S(2)}) collective-permute-start(bf16[2,56,1152]{2,1,0:T(8,128)(2,1)S(1)} %pad_maximum_fusion.2), channel_id=1, source_target_pairs={{0,40},{4,44},{8,48},{12,52},{16,56},{20,60},{24,0},{28,4},{32,8},... | collective-permute-start | bytes 774152 | tf_op jit(solution)/shard_map/ppermute | solution.py:320
  49.4 5.5 %conv.1 = bf16[192,1280]{1,0:T(8,128)(2,1)S(1)} custom-call(bf16[16,320]{1,0:T(8,128)(2,1)S(1)} %collective-permute-done.11.before_ref, bf16[768,320]{1,0:T(8,128)(2,1)S(1)} %get-tuple-element.11.gated_ref, bf16[16,320]{1,0:T(8,128)(2,1)S(1)} %collective-permute-done.12.after_ref, f32[31,320]{1,0:T(8,128)S(1)} %copy-done.20, ...), custom_call_target="tpu_custom_call" | custom-call | flops 5000000000 | bytes 1966080 | tf_op jit(solution)/shard_map/conv/pallas_call | solution.py:285
  54.9 3.8 collective-permute-start.15
  58.7 4.9 %collective-permute-done.3 = bf16[3,56,1152]{2,1,0:T(8,128)(2,1)S(1)} collective-permute-done((bf16[3,56,1152]{2,1,0:T(8,128)(2,1)S(1)}, bf16[3,56,1152]{2,1,0:T(8,128)(2,1)S(1)}, u32[]{:S(2)}, u32[]{:S(2)}) %collective-permute-start.3) | collective-permute-done | bytes 387104 | tf_op jit(solution)/shard_map/ppermute | solution.py:320
  65.9 1.9 collective-permute-start.7
  68.6 4.6 %collective-permute-start.8 = (bf16[5,56,1152]{2,1,0:T(8,128)(2,1)S(1)}, bf16[5,56,1152]{2,1,0:T(8,128)(2,1)S(1)}, u32[]{:S(2)}, u32[]{:S(2)}) collective-permute-start(bf16[5,56,1152]{2,1,0:T(8,128)(2,1)S(1)} %get-tuple-element.24.refs_1_), channel_id=1, source_target_pairs={{0,192},{4,196},{8,200},{12,204},{16,208},{20,212},{24,216},{28,22... | collective-permute-start | bytes 1935368 | tf_op jit(solution)/shard_map/ppermute | solution.py:320
  74.0 1.9 collective-permute-start.10
  76.7 3.1 collective-permute-start.9
  81.0 21.6 %collective-permute-done.9.refs_6_ = bf16[3,56,1152]{2,1,0:T(8,128)(2,1)S(1)} collective-permute-done((bf16[3,56,1152]{2,1,0:T(8,128)(2,1)S(1)}, bf16[3,56,1152]{2,1,0:T(8,128)(2,1)S(1)}, u32[]{:S(2)}, u32[]{:S(2)}) %collective-permute-start.9) | collective-permute-done | bytes 387104 | tf_op jit(solution)/shard_map/ppermute | solution.py:320
  102.6 1.9 collective-permute-start.23
  104.5 10.9 %collective-permute-start.16 = (bf16[192,1280]{1,0:T(8,128)(2,1)}, bf16[192,1280]{1,0:T(8,128)(2,1)}, u32[]{:S(2)}, u32[]{:S(2)}) collective-permute-start(bf16[192,1280]{1,0:T(8,128)(2,1)} %get-tuple-element.15), channel_id=1, source_target_pairs={{1,2},{2,1},{3,0},{0,3},{5,6},{6,5},{7,4},{4,7},{9,10},{10,9},{11,... | collective-permute-start | bytes 1474568 | tf_op jit(solution)/shard_map/ppermute | solution.py:443
  116.9 2.0 collective-permute-start.24
  119.6 1.5 collective-permute-start.22
  121.1 3.5 fusion.refs_11_
  124.7 1.5 collective-permute-start.25
  128.5 4.3 %tokens_part.1 = bf16[192,896]{1,0:T(8,128)(2,1)S(1)} custom-call(bf16[3,56,1152]{2,1,0:T(8,128)(2,1)S(1)} %pad_maximum_fusion.1.refs_0_, bf16[5,56,1152]{2,1,0:T(8,128)(2,1)S(1)} %get-tuple-element.24.refs_1_, bf16[3,56,1152]{2,1,0:T(8,128)(2,1)S(1)} %collective-permute-done.5.refs_2_, bf16[3,56,1152]{2,1,0:T(8,128)(2,1)S(1)} %collective-permute-done.6.refs_3_, ...), custom_call_target="tpu_custom_call" | custom-call | flops 1283457024 | bytes 8000000 | tf_op jit(solution)/shard_map/tokens_part/pallas_call | solution.py:391
  132.8 5.6 %collective-permute-start.18 = (bf16[192,896]{1,0:T(8,128)(2,1)S(1)}, bf16[192,896]{1,0:T(8,128)(2,1)S(1)}, u32[]{:S(2)}, u32[]{:S(2)}) collective-permute-start(bf16[192,896]{1,0:T(8,128)(2,1)S(1)} %tokens_part.1), channel_id=1, source_target_pairs={{0,256},{1,257},{2,258},{3,259},{4,260},{5,261},{6,262},{7,263},{8... | collective-permute-start | bytes 1032200 | tf_op jit(solution)/shard_map/ppermute | solution.py:470
  138.5 3.4 collective-permute-start.19
  142.7 6.6 %collective-permute-done.19.refs_1_ = bf16[192,896]{1,0:T(8,128)(2,1)S(1)} collective-permute-done((bf16[192,896]{1,0:T(8,128)(2,1)S(1)}, bf16[192,896]{1,0:T(8,128)(2,1)S(1)}, u32[]{:S(2)}, u32[]{:S(2)}) %collective-permute-start.19) | collective-permute-done | bytes 344096 | tf_op jit(solution)/shard_map/ppermute | solution.py:471
  151.7 252.6 %join.1 = bf16[64,56,1152]{2,1,0:T(8,128)(2,1)} custom-call(s32[64]{0:T(128)} %pad_add_fusion.index_ref, bf16[3,56,1152]{2,1,0:T(8,128)(2,1)} %copy-done.4, bf16[5,56,1152]{2,1,0:T(8,128)(2,1)} %copy-done, bf16[3,56,1152]{2,1,0:T(8,128)(2,1)} %copy-done.5, bf16[3,56,1152]{2,1,0:T(8,128)(2,1)} %copy-done.6, bf16[5,56,1152]{2,1,0:T(8,128)(2,1)} %copy-done.1, ...), custom_call_target="tpu_custom_call" | custom-call | bytes 16515072 | tf_op jit(solution)/shard_map/join/pallas_call | solution.py:363
  404.4 6.0 %text_part.1 = (bf16[192,896]{1,0:T(8,128)(2,1)S(1)}, bf16[192,128]{1,0:T(8,128)(2,1)S(1)}, bf16[192,128]{1,0:T(8,128)(2,1)S(1)}) custom-call(s32[4]{0:T(128)S(1)} %and_select_fusion.order_ref, bf16[192,896]{1,0:T(8,128)(2,1)S(1)} %copy-done.14, bf16[192,896]{1,0:T(8,128)(2,1)S(1)} %copy-done.16, bf16[192,896]{1,0:T(8,128)(2,1)S(1)} %copy-done.9, ...), custom_call_target="tpu_custom_call" | custom-call | flops 1585446912 | bytes 9633792 | tf_op jit(solution)/shard_map/text_part/pallas_call | solution.py:126
  410.5 6.6 %audio_part.1 = bf16[192,896]{1,0:T(8,128)(2,1)S(1)} custom-call(s32[4]{0:T(128)S(1)} %and_select_fusion.order_ref, bf16[192,896]{1,0:T(8,128)(2,1)S(1)} %collective-permute-done.18.refs_0_, bf16[192,896]{1,0:T(8,128)(2,1)S(1)} %collective-permute-done.19.refs_1_, bf16[192,896]{1,0:T(8,128)(2,1)S(1)} %collective-permute-done.20.refs_2_, ...), custom_call_target="tpu_custom_call" | custom-call | flops 352321536 | bytes 3211264 | tf_op jit(solution)/shard_map/audio_part/pallas_call | solution.py:162
  (108 shorter events, 22.9 us)
Async XLA Ops:
  0.0 42.9 %collective-permute-start.13 = (bf16[192,896]{1,0:T(8,128)(2,1)}, bf16[192,896]{1,0:T(8,128)(2,1)}, u32[]{:S(2)}, u32[]{:S(2)}) collective-permute-start(bf16[192,896]{1,0:T(8,128)(2,1)} %refs_0_.1), channel_id=1, source_target_pairs={{256,257},{257,258},{258,259},{259,256},{260,261},{261,262},{262,2... | collective-permute-start | bytes 1032200 | tf_op jit(solution)/shard_map/ppermute | solution.py:427
  1.4 47.9 %collective-permute-start.14 = (bf16[192,896]{1,0:T(8,128)(2,1)}, bf16[192,896]{1,0:T(8,128)(2,1)S(1)}, u32[]{:S(2)}, u32[]{:S(2)}) collective-permute-start(bf16[192,896]{1,0:T(8,128)(2,1)} %refs_0_.1), channel_id=1, source_target_pairs={{256,259},{257,256},{258,257},{259,258},{260,263},{261,260},{262,2... | collective-permute-start | bytes 1032200 | tf_op jit(solution)/shard_map/ppermute | solution.py:428
  2.1 20.5 %collective-permute-start = (bf16[20,896]{1,0:T(8,128)(2,1)}, bf16[20,896]{1,0:T(8,128)(2,1)S(1)}, u32[]{:S(2)}, u32[]{:S(2)}) collective-permute-start(bf16[20,896]{1,0:T(8,128)(2,1)} %param.17), channel_id=1, source_target_pairs={{0,4},{4,0},{8,12},{12,8},{16,20},{20,16},{24,28},{28,24},{32,36},... | collective-permute-start | bytes 107528 | tf_op jit(solution)/shard_map/ppermute | solution.py:420
  20.0 16.4 %collective-permute-start.11 = (bf16[16,320]{1,0:T(8,128)(2,1)S(1)}, bf16[16,320]{1,0:T(8,128)(2,1)S(1)}, u32[]{:S(2)}, u32[]{:S(2)}) collective-permute-start(bf16[16,320]{1,0:T(8,128)(2,1)S(1)} %get-tuple-element.18), channel_id=1, source_target_pairs={{0,4},{4,8},{8,12},{12,16},{16,20},{20,24},{24,28},{28,32},{32,36}... | collective-permute-start | bytes 30728 | tf_op jit(solution)/shard_map/ppermute | solution.py:437
  22.7 6.4 %collective-permute-start.2 = (bf16[1,56,1152]{2,1,0:T(8,128)(2,1)S(1)}, bf16[1,56,1152]{2,1,0:T(8,128)(2,1)S(1)}, u32[]{:S(2)}, u32[]{:S(2)}) collective-permute-start(bf16[1,56,1152]{2,1,0:T(8,128)(2,1)S(1)} %select_bitcast_fusion.1), channel_id=1, source_target_pairs={{0,56},{4,60},{8,0},{12,4},{16,8},{20,12},{24,16},{28,20},{32,24},... | collective-permute-start | bytes 387080 | tf_op jit(solution)/shard_map/ppermute | solution.py:320
  24.7 7.7 %collective-permute-start.1 = (bf16[1,56,1152]{2,1,0:T(8,128)(2,1)S(1)}, bf16[1,56,1152]{2,1,0:T(8,128)(2,1)S(1)}, u32[]{:S(2)}, u32[]{:S(2)}) collective-permute-start(bf16[1,56,1152]{2,1,0:T(8,128)(2,1)S(1)} %select_bitcast_fusion.1), channel_id=1, source_target_pairs={{0,8},{4,12},{8,16},{12,20},{16,24},{20,28},{24,32},{28,36},{32,40... | collective-permute-start | bytes 387080 | tf_op jit(solution)/shard_map/ppermute | solution.py:320
  29.2 9.9 %collective-permute-start.12 = (bf16[16,320]{1,0:T(8,128)(2,1)S(1)}, bf16[16,320]{1,0:T(8,128)(2,1)S(1)}, u32[]{:S(2)}, u32[]{:S(2)}) collective-permute-start(bf16[16,320]{1,0:T(8,128)(2,1)S(1)} %get-tuple-element.17), channel_id=1, source_target_pairs={{4,0},{8,4},{12,8},{16,12},{20,16},{24,20},{28,24},{32,28},{36,32}... | collective-permute-start | bytes 30728 | tf_op jit(solution)/shard_map/ppermute | solution.py:438
  32.5 93.8 %copy-start.4 = (bf16[3,56,1152]{2,1,0:T(8,128)(2,1)}, bf16[3,56,1152]{2,1,0:T(8,128)(2,1)S(1)}, u32[]{:S(2)}) copy-start(bf16[3,56,1152]{2,1,0:T(8,128)(2,1)S(1)} %pad_maximum_fusion.1.refs_0_) | copy-start | bytes 1161220
  32.5 31.1 %collective-permute-start.3 = (bf16[3,56,1152]{2,1,0:T(8,128)(2,1)S(1)}, bf16[3,56,1152]{2,1,0:T(8,128)(2,1)S(1)}, u32[]{:S(2)}, u32[]{:S(2)}) collective-permute-start(bf16[3,56,1152]{2,1,0:T(8,128)(2,1)S(1)} %pad_maximum_fusion.1.refs_0_), channel_id=1, source_target_pairs={{0,24},{4,28},{8,32},{12,36},{16,40},{20,44},{24,48},{28,52},{32,5... | collective-permute-start | bytes 1161224 | tf_op jit(solution)/shard_map/ppermute | solution.py:320
  36.4 32.2 %collective-permute-start.5 = (bf16[3,56,1152]{2,1,0:T(8,128)(2,1)S(1)}, bf16[3,56,1152]{2,1,0:T(8,128)(2,1)S(1)}, u32[]{:S(2)}, u32[]{:S(2)}) collective-permute-start(bf16[3,56,1152]{2,1,0:T(8,128)(2,1)S(1)} %pad_maximum_fusion.1.refs_0_), channel_id=1, source_target_pairs={{0,64},{4,68},{8,72},{12,76},{16,80},{20,84},{24,88},{28,92},{32,9... | collective-permute-start | bytes 1161224 | tf_op jit(solution)/shard_map/ppermute | solution.py:320
  39.0 34.9 %collective-permute-start.6 = (bf16[3,56,1152]{2,1,0:T(8,128)(2,1)S(1)}, bf16[3,56,1152]{2,1,0:T(8,128)(2,1)S(1)}, u32[]{:S(2)}, u32[]{:S(2)}) collective-permute-start(bf16[3,56,1152]{2,1,0:T(8,128)(2,1)S(1)} %pad_maximum_fusion.1.refs_0_), channel_id=1, source_target_pairs={{0,192},{4,196},{8,200},{12,204},{16,208},{20,212},{24,216},{28,22... | collective-permute-start | bytes 1161224 | tf_op jit(solution)/shard_map/ppermute | solution.py:320
  42.9 22.2 %collective-permute-start.4 = (bf16[2,56,1152]{2,1,0:T(8,128)(2,1)S(1)}, bf16[2,56,1152]{2,1,0:T(8,128)(2,1)S(1)}, u32[]{:S(2)}, u32[]{:S(2)}) collective-permute-start(bf16[2,56,1152]{2,1,0:T(8,128)(2,1)S(1)} %pad_maximum_fusion.2), channel_id=1, source_target_pairs={{0,40},{4,44},{8,48},{12,52},{16,56},{20,60},{24,0},{28,4},{32,8},... | collective-permute-start | bytes 774152 | tf_op jit(solution)/shard_map/ppermute | solution.py:320
  54.9 21.8 %collective-permute-start.15 = (bf16[192,1280]{1,0:T(8,128)(2,1)S(1)}, bf16[192,1280]{1,0:T(8,128)(2,1)S(1)}, u32[]{:S(2)}, u32[]{:S(2)}) collective-permute-start(bf16[192,1280]{1,0:T(8,128)(2,1)S(1)} %conv.1), channel_id=1, source_target_pairs={{0,1},{1,0},{2,3},{3,2},{4,5},{5,4},{6,7},{7,6},{8,9},{9,8},{10,11... | collective-permute-start | bytes 1474568 | tf_op jit(solution)/shard_map/ppermute | solution.py:440
  63.6 55.3 %collective-permute-start.17 = (bf16[192,896]{1,0:T(8,128)(2,1)}, bf16[192,896]{1,0:T(8,128)(2,1)S(1)}, u32[]{:S(2)}, u32[]{:S(2)}) collective-permute-start(bf16[192,896]{1,0:T(8,128)(2,1)} %collective-permute-done.13.refs_1_.refs_3_), channel_id=1, source_target_pairs={{256,257},{257,258},{258,259},{259,256},{260,261},{261,262},{262,2... | collective-permute-start | bytes 1032200 | tf_op jit(solution)/shard_map/ppermute | solution.py:429
  65.9 60.4 %copy-start = (bf16[5,56,1152]{2,1,0:T(8,128)(2,1)}, bf16[5,56,1152]{2,1,0:T(8,128)(2,1)S(1)}, u32[]{:S(2)}) copy-start(bf16[5,56,1152]{2,1,0:T(8,128)(2,1)S(1)} %get-tuple-element.24.refs_1_) | copy-start | bytes 1935364
  65.9 38.6 %collective-permute-start.7 = (bf16[5,56,1152]{2,1,0:T(8,128)(2,1)S(1)}, bf16[5,56,1152]{2,1,0:T(8,128)(2,1)S(1)}, u32[]{:S(2)}, u32[]{:S(2)}) collective-permute-start(bf16[5,56,1152]{2,1,0:T(8,128)(2,1)S(1)} %get-tuple-element.24.refs_1_), channel_id=1, source_target_pairs={{0,64},{4,68},{8,72},{12,76},{16,80},{20,84},{24,88},{28,92},{32,9... | collective-permute-start | bytes 1935368 | tf_op jit(solution)/shard_map/ppermute | solution.py:320
  68.6 57.6 %copy-start.5 = (bf16[3,56,1152]{2,1,0:T(8,128)(2,1)}, bf16[3,56,1152]{2,1,0:T(8,128)(2,1)S(1)}, u32[]{:S(2)}) copy-start(bf16[3,56,1152]{2,1,0:T(8,128)(2,1)S(1)} %collective-permute-done.5.refs_2_) | copy-start | bytes 1161220
  68.6 46.9 %collective-permute-start.8 = (bf16[5,56,1152]{2,1,0:T(8,128)(2,1)S(1)}, bf16[5,56,1152]{2,1,0:T(8,128)(2,1)S(1)}, u32[]{:S(2)}, u32[]{:S(2)}) collective-permute-start(bf16[5,56,1152]{2,1,0:T(8,128)(2,1)S(1)} %get-tuple-element.24.refs_1_), channel_id=1, source_target_pairs={{0,192},{4,196},{8,200},{12,204},{16,208},{20,212},{24,216},{28,22... | collective-permute-start | bytes 1935368 | tf_op jit(solution)/shard_map/ppermute | solution.py:320
  74.0 52.3 %collective-permute-start.10 = (bf16[5,48,896]{2,1,0:T(8,128)(2,1)}, bf16[5,48,896]{2,1,0:T(8,128)(2,1)}, u32[]{:S(2)}, u32[]{:S(2)}) collective-permute-start(bf16[5,48,896]{2,1,0:T(8,128)(2,1)} %slice.34), channel_id=1, source_target_pairs={{0,128},{4,132},{8,136},{12,140},{16,144},{20,148},{24,152},{28,15... | collective-permute-start | bytes 1290248 | tf_op jit(solution)/shard_map/ppermute | solution.py:331
  76.7 25.9 %collective-permute-start.9 = (bf16[3,56,1152]{2,1,0:T(8,128)(2,1)S(1)}, bf16[3,56,1152]{2,1,0:T(8,128)(2,1)S(1)}, u32[]{:S(2)}, u32[]{:S(2)}) collective-permute-start(bf16[3,56,1152]{2,1,0:T(8,128)(2,1)S(1)} %collective-permute-done.6.refs_3_), channel_id=1, source_target_pairs={{0,192},{4,196},{8,200},{12,204},{16,208},{20,212},{24,216},{28,22... | collective-permute-start | bytes 1161224 | tf_op jit(solution)/shard_map/ppermute | solution.py:320
  102.6 49.1 %collective-permute-start.23 = (bf16[14,56,1152]{2,1,0:T(8,128)(2,1)}, bf16[14,56,1152]{2,1,0:T(8,128)(2,1)}, u32[]{:S(2)}, u32[]{:S(2)}) collective-permute-start(bf16[14,56,1152]{2,1,0:T(8,128)(2,1)} %constant_dynamic-update-slice_fusion.2), channel_id=1, source_target_pairs={{256,260},{260,256},{264,268},{268,264},{272,276},{276,272},{280,2... | collective-permute-start | bytes 5419016 | tf_op jit(solution)/shard_map/ppermute | solution.py:457
  104.5 21.7 %collective-permute-start.16 = (bf16[192,1280]{1,0:T(8,128)(2,1)}, bf16[192,1280]{1,0:T(8,128)(2,1)}, u32[]{:S(2)}, u32[]{:S(2)}) collective-permute-start(bf16[192,1280]{1,0:T(8,128)(2,1)} %get-tuple-element.15), channel_id=1, source_target_pairs={{1,2},{2,1},{3,0},{0,3},{5,6},{6,5},{7,4},{4,7},{9,10},{10,9},{11,... | collective-permute-start | bytes 1474568 | tf_op jit(solution)/shard_map/ppermute | solution.py:443
  116.9 34.8 %collective-permute-start.24 = (bf16[13,56,1152]{2,1,0:T(8,128)(2,1)}, bf16[13,56,1152]{2,1,0:T(8,128)(2,1)}, u32[]{:S(2)}, u32[]{:S(2)}) collective-permute-start(bf16[13,56,1152]{2,1,0:T(8,128)(2,1)} %pad_maximum_fusion), channel_id=1, source_target_pairs={{256,260},{260,256},{264,268},{268,264},{272,276},{276,272},{280,2... | collective-permute-start | bytes 5031944 | tf_op jit(solution)/shard_map/ppermute | solution.py:457
  119.6 5.1 %collective-permute-start.22 = (bf16[5,56,1152]{2,1,0:T(8,128)(2,1)S(1)}, bf16[5,56,1152]{2,1,0:T(8,128)(2,1)}, u32[]{:S(2)}, u32[]{:S(2)}) collective-permute-start(bf16[5,56,1152]{2,1,0:T(8,128)(2,1)S(1)} %collective-permute-done.7.refs_4_), channel_id=1, source_target_pairs={{256,320},{260,324},{264,328},{268,332},{272,336},{276,340},{280,3... | collective-permute-start | bytes 1935368 | tf_op jit(solution)/shard_map/ppermute | solution.py:330
  124.7 27.0 %collective-permute-start.25 = (bf16[5,56,1152]{2,1,0:T(8,128)(2,1)}, bf16[5,56,1152]{2,1,0:T(8,128)(2,1)}, u32[]{:S(2)}, u32[]{:S(2)}) collective-permute-start(bf16[5,56,1152]{2,1,0:T(8,128)(2,1)} %collective-permute-done.22.refs_7_), channel_id=1, source_target_pairs={{256,260},{260,256},{264,268},{268,264},{272,276},{276,272},{280,2... | collective-permute-start | bytes 1935368 | tf_op jit(solution)/shard_map/ppermute | solution.py:457
  132.8 17.2 %collective-permute-start.18 = (bf16[192,896]{1,0:T(8,128)(2,1)S(1)}, bf16[192,896]{1,0:T(8,128)(2,1)S(1)}, u32[]{:S(2)}, u32[]{:S(2)}) collective-permute-start(bf16[192,896]{1,0:T(8,128)(2,1)S(1)} %tokens_part.1), channel_id=1, source_target_pairs={{0,256},{1,257},{2,258},{3,259},{4,260},{5,261},{6,262},{7,263},{8... | collective-permute-start | bytes 1032200 | tf_op jit(solution)/shard_map/ppermute | solution.py:470
  138.5 10.9 %collective-permute-start.19 = (bf16[192,896]{1,0:T(8,128)(2,1)S(1)}, bf16[192,896]{1,0:T(8,128)(2,1)S(1)}, u32[]{:S(2)}, u32[]{:S(2)}) collective-permute-start(bf16[192,896]{1,0:T(8,128)(2,1)S(1)} %tokens_part.1), channel_id=1, source_target_pairs={{0,259},{1,256},{2,257},{3,258},{4,263},{5,260},{6,261},{7,262},{8... | collective-permute-start | bytes 1032200 | tf_op jit(solution)/shard_map/ppermute | solution.py:471
  149.3 261.1 %collective-permute-start.20 = (bf16[192,896]{1,0:T(8,128)(2,1)S(1)}, bf16[192,896]{1,0:T(8,128)(2,1)S(1)}, u32[]{:S(2)}, u32[]{:S(2)}) collective-permute-start(bf16[192,896]{1,0:T(8,128)(2,1)S(1)} %collective-permute-done.19.refs_1_), channel_id=1, source_target_pairs={{256,259},{257,256},{258,257},{259,258},{260,263},{261,260},{262,2... | collective-permute-start | bytes 1032200 | tf_op jit(solution)/shard_map/ppermute | solution.py:472
  150.0 260.4 %collective-permute-start.21 = (bf16[192,896]{1,0:T(8,128)(2,1)S(1)}, bf16[192,896]{1,0:T(8,128)(2,1)S(1)}, u32[]{:S(2)}, u32[]{:S(2)}) collective-permute-start(bf16[192,896]{1,0:T(8,128)(2,1)S(1)} %collective-permute-done.18.refs_0_), channel_id=1, source_target_pairs={{256,257},{257,258},{258,259},{259,256},{260,261},{261,262},{262,2... | collective-permute-start | bytes 1032200 | tf_op jit(solution)/shard_map/ppermute | solution.py:473
  151.7 252.7 %copy-start.9 = (bf16[192,896]{1,0:T(8,128)(2,1)S(1)}, bf16[192,896]{1,0:T(8,128)(2,1)}, u32[]{:S(2)}) copy-start(bf16[192,896]{1,0:T(8,128)(2,1)} %copy-done.7) | copy-start | bytes 1032196
  151.7 252.7 %copy-start.14 = (bf16[192,896]{1,0:T(8,128)(2,1)S(1)}, bf16[192,896]{1,0:T(8,128)(2,1)}, u32[]{:S(2)}) copy-start(bf16[192,896]{1,0:T(8,128)(2,1)} %refs_0_.1) | copy-start | bytes 1032196
  151.7 252.7 %copy-start.16 = (bf16[192,896]{1,0:T(8,128)(2,1)S(1)}, bf16[192,896]{1,0:T(8,128)(2,1)}, u32[]{:S(2)}) copy-start(bf16[192,896]{1,0:T(8,128)(2,1)} %copy-done.15) | copy-start | bytes 1032196
  (19 other events, 235.3 us)

commit v3 on v2

--- a/solution.py
+++ b/solution.py
@@ -29,84 +29,63 @@
     return values * cosine + pltpu.roll(values, HEAD // 2, 1) * sine
 
 
-def text_kernel(order_ref, *refs, parts):
-    xs = refs[:parts]
-    gain_ref, w_ref, bias_ref, cos_ref, sin_ref, q_ref, k_ref, v_ref, acc, square = refs[parts:]
+def decode_kernel(order_ref, *refs, parts):
+    words, sounds = refs[:parts], refs[parts : 2 * parts]
+    gain_ref, w_ref, bias_ref, cos_ref, sin_ref, out_ref, acc, acc_kv, square, square_kv = refs[2 * parts :]
     step = pl.program_id(0)
+    count, total = acc.shape
+    heads = total // HEAD - 2
 
     @pl.when(step == 0)
     def _():
-        acc[...] = jnp.zeros_like(acc)
-        square[...] = jnp.zeros_like(square)
+        for ref in (acc, acc_kv, square, square_kv):
+            ref[...] = jnp.zeros_like(ref)
 
     for i in range(parts):
 
         @pl.when(step == i)
         def _():
-            x = xs[i][...].astype(jnp.float32)
+            x = words[i][...].astype(jnp.float32)
             square[...] += jnp.sum(x * x, axis=1, keepdims=True)
             acc[...] += jnp.dot(
                 (x * gain_ref[0]).astype(jnp.bfloat16), w_ref[...], preferred_element_type=jnp.float32
             )
+            x = sounds[i][...].astype(jnp.float32)
+            square_kv[...] += jnp.sum(x * x, axis=1, keepdims=True)
+            acc_kv[...] += jnp.dot(
+                (x * gain_ref[0]).astype(jnp.bfloat16), w_ref[:, heads * HEAD :], preferred_element_type=jnp.float32
+            )
 
     @pl.when(step == pl.num_programs(0) - 1)
     def _():
-        scale = lax.rsqrt(square[...] / (parts * xs[0].shape[1]) + 1e-6)
-        cosine, sine = cos_ref[...], sin_ref[...]
-        heads = q_ref.shape[1] // HEAD
-        for h in range(heads + 2):
-            cols = pl.ds(h * HEAD, HEAD)
-            value = acc[:, cols] * scale + bias_ref[:, cols]
-            if h < heads + 1:
-                value = turned(value, cosine, sine)
-            value = value.astype(jnp.bfloat16)
-            if h < heads:
-                q_ref[:, cols] = value
-            elif h == heads:
-                k_ref[...] = value
-            else:
-                v_ref[...] = value
-
-
-def audio_kernel(
-    order_ref, *refs, parts
-):
-    xs = refs[:parts]
-    (gain_ref, wk_ref, wv_ref, bias_ref, cos_ref, sin_ref, q_ref, kt_ref, vt_ref, out_ref, acc_k, acc_v, square) = refs[parts:]
-    step = pl.program_id(0)
-
-    @pl.when(step == 0)
-    def _():
-        acc_k[...] = jnp.zeros_like(acc_k)
-        acc_v[...] = jnp.zeros_like(acc_v)
-        square[...] = jnp.zeros_like(square)
-
-    for i in range(parts):
-
-        @pl.when(step == i)
-        def _():
-            x = xs[i][...].astype(jnp.float32)
-            square[...] += jnp.sum(x * x, axis=1, keepdims=True)
-            xg = (x * gain_ref[0]).astype(jnp.bfloat16)
-            acc_k[...] += jnp.dot(xg, wk_ref[...], preferred_element_type=jnp.float32)
-            acc_v[...] += jnp.dot(xg, wv_ref[...], preferred_element_type=jnp.float32)
-
-    @pl.when(step == pl.num_programs(0) - 1)
-    def _():
-        count = acc_k.shape[0]
-        heads = q_ref.shape[1] // HEAD
-        scale = lax.rsqrt(square[...] / (parts * xs[0].shape[1]) + 1e-6)
-        keys = turned(acc_k[...] * scale + bias_ref[:, :HEAD], cos_ref[...], sin_ref[...])
-        keys = jnp.concatenate([keys.astype(jnp.bfloat16), kt_ref[...]], axis=0)
-        values = (acc_v[...] * scale + bias_ref[:, HEAD:]).astype(jnp.bfloat16)
-        values = jnp.concatenate([values, vt_ref[...]], axis=0)
+        width = parts * words[0].shape[1]
+        scale = lax.rsqrt(square[...] / width + 1e-6)
+        scale_kv = lax.rsqrt(square_kv[...] / width + 1e-6)
+        cosine, sine = cos_ref[count:], sin_ref[count:]
+        key_cols = slice(heads * HEAD, (heads + 1) * HEAD)
+        value_cols = slice((heads + 1) * HEAD, total)
+        keys = jnp.concatenate(
+            [
+                turned(acc_kv[:, :HEAD] * scale_kv + bias_ref[:, key_cols], cos_ref[:count], sin_ref[:count]),
+                turned(acc[:, key_cols] * scale + bias_ref[:, key_cols], cosine, sine),
+            ],
+            axis=0,
+        ).astype(jnp.bfloat16)
+        values = jnp.concatenate(
+            [
+                acc_kv[:, HEAD:] * scale_kv + bias_ref[:, value_cols],
+                acc[:, value_cols] * scale + bias_ref[:, value_cols],
+            ],
+            axis=0,
+        ).astype(jnp.bfloat16)
         row = lax.broadcasted_iota(jnp.int32, (count, 2 * count), 0)
         col = lax.broadcasted_iota(jnp.int32, (count, 2 * count), 1)
         allowed = col <= row + count
         for h in range(heads):
-            cols = pl.ds(h * HEAD, HEAD)
+            cols = slice(h * HEAD, (h + 1) * HEAD)
+            query = turned(acc[:, cols] * scale + bias_ref[:, cols], cosine, sine).astype(jnp.bfloat16)
             scores = lax.dot_general(
-                q_ref[:, cols], keys, (((1,), (1,)), ((), ())), preferred_element_type=jnp.float32
+                query, keys, (((1,), (1,)), ((), ())), preferred_element_type=jnp.float32
             ) * (HEAD**-0.5)
             scores = jnp.where(allowed, scores, -1e30)
             weights = jnp.exp(scores - jnp.max(scores, axis=1, keepdims=True))
@@ -116,80 +95,40 @@
             ).astype(jnp.bfloat16)
 
 
-def text_part(order, xs, gain, weight, bias, tables):
-    parts = len(xs)
-    count, width = xs[0].shape
+def decode(order, words, sounds, gain, weight, bias, tables):
+    parts = len(words)
+    count, width = words[0].shape
     total = weight.shape[1]
-    heads = total // HEAD - 2
-    cosine, sine = tables
+    columns = total - 2 * HEAD
     whole = lambda *shape: pl.BlockSpec(shape, lambda k, o: (0,) * len(shape))
     return pl.pallas_call(
-        functools.partial(text_kernel, parts=parts),
+        functools.partial(decode_kernel, parts=parts),
         grid_spec=pltpu.PrefetchScalarGridSpec(
             num_scalar_prefetch=1,
             grid=(parts,),
-            in_specs=[whole(count, width)] * parts
+            in_specs=[whole(count, width)] * (2 * parts)
             + [
                 pl.BlockSpec((1, 1, width), lambda k, o: (o[k], 0, 0)),
                 pl.BlockSpec((width, total), lambda k, o: (o[k], 0)),
                 whole(1, total),
-                whole(count, HEAD),
-                whole(count, HEAD),
+                whole(2 * count, HEAD),
+                whole(2 * count, HEAD),
             ],
-            out_specs=[whole(count, heads * HEAD), whole(count, HEAD), whole(count, HEAD)],
-            scratch_shapes=[pltpu.VMEM((count, total), jnp.float32), pltpu.VMEM((count, 1), jnp.float32)],
-        ),
-        out_shape=[
-            jax.ShapeDtypeStruct((count, heads * HEAD), jnp.bfloat16),
-            jax.ShapeDtypeStruct((count, HEAD), jnp.bfloat16),
-            jax.ShapeDtypeStruct((count, HEAD), jnp.bfloat16),
-        ],
+            out_specs=whole(count, columns),
+            scratch_shapes=[
+                pltpu.VMEM((count, total), jnp.float32),
+                pltpu.VMEM((count, 2 * HEAD), jnp.float32),
+                pltpu.VMEM((count, 1), jnp.float32),
+                pltpu.VMEM((count, 1), jnp.float32),
+            ],
+        ),
+        out_shape=jax.ShapeDtypeStruct((count, columns), jnp.bfloat16),
         compiler_params=pltpu.CompilerParams(vmem_limit_bytes=VMEM),
         cost_estimate=pl.CostEstimate(
             flops=2 * count * parts * width * total, bytes_accessed=2 * parts * width * (total + count), transcendentals=0
         ),
-        name="text_part",
-    )(order, *xs, gain, weight, bias, cosine[count:], sine[count:])
-
-
-def audio_part(order, xs, gain, weight, bias, tables, q, kt, vt):
-    parts = len(xs)
-    count, width = xs[0].shape
-    total = weight.shape[1]
-    heads = total // HEAD - 2
-    cosine, sine = tables
-    whole = lambda *shape: pl.BlockSpec(shape, lambda k, o: (0,) * len(shape))
-    return pl.pallas_call(
-        functools.partial(audio_kernel, parts=parts),
-        grid_spec=pltpu.PrefetchScalarGridSpec(
-            num_scalar_prefetch=1,
-            grid=(parts,),
-            in_specs=[whole(count, width)] * parts
-            + [
-                pl.BlockSpec((1, 1, width), lambda k, o: (o[k], 0, 0)),
-                pl.BlockSpec((width, HEAD), lambda k, o: (o[k], heads)),
-                pl.BlockSpec((width, HEAD), lambda k, o: (o[k], heads + 1)),
-                whole(1, 2 * HEAD),
-                whole(count, HEAD),
-                whole(count, HEAD),
-                whole(count, heads * HEAD),
-                whole(count, HEAD),
-                whole(count, HEAD),
-            ],
-            out_specs=whole(count, heads * HEAD),
-            scratch_shapes=[
-                pltpu.VMEM((count, HEAD), jnp.float32),
-                pltpu.VMEM((count, HEAD), jnp.float32),
-                pltpu.VMEM((count, 1), jnp.float32),
-            ],
-        ),
-        out_shape=jax.ShapeDtypeStruct((count, heads * HEAD), jnp.bfloat16),
-        compiler_params=pltpu.CompilerParams(vmem_limit_bytes=VMEM),
-        cost_estimate=pl.CostEstimate(
-            flops=2 * count * parts * width * 2 * HEAD, bytes_accessed=2 * parts * width * (2 * HEAD + count), transcendentals=0
-        ),
-        name="audio_part",
-    )(order, *xs, gain, weight, weight, bias, cosine[:count], sine[:count], q, kt, vt)
+        name="decode",
+    )(order, *words, *sounds, gain, weight, bias, *tables)
 
 
 def pooling(rows):
@@ -317,58 +256,11 @@
 
 
 def spread(block):
-    send = lambda v, dx, dy: lax.ppermute(v, "seq", place(dx, dy))
+    send = lambda v, dx, dy: lax.ppermute(v, ("grp", "seq"), of_group(0, place(dx, dy)))
     near = jnp.concatenate([send(block, 0, 1), block, send(block, 0, -1)], axis=0)
-    before = send(near, -1, 0)
-    behind = send(near, 1, 0)
-    far = jnp.concatenate([send(near, 0, 3), send(near[:2], 0, -3)], axis=0)
-    inner, outer = [-1, 0, 1], [-4, -3, -2, 2, 3]
-    before_far = send(far, -1, 0)
-    behind_far = send(far, 1, 0)
-    second = send(before, -1, 0)
-    groups = ("grp", "seq")
-    second_far = lax.ppermute(behind_far, groups, of_group(1, place(1, 0)))
-    direct = lax.ppermute(far[:, :ADAPT_SLOT, :ADAPT_COLS], groups, of_group(0, place(2, 0)))
-    pieces = [
-        (0, inner, near),
-        (0, outer, far),
-        (-1, inner, behind),
-        (1, inner, before),
-        (-1, outer, behind_far),
-        (1, outer, before_far),
-        (2, inner, second),
-        (2, outer, second_far),
-    ]
-    return pieces, direct
-
-
-def join_kernel(index_ref, *refs, counts):
-    ins, out, sem = refs[: len(counts)], refs[len(counts)], refs[len(counts) + 1]
-    copies = []
-    at = 0
-    for ref, count in zip(ins, counts, strict=True):
-        for j in range(count):
-            copy = pltpu.make_async_copy(ref.at[j], out.at[index_ref[at]], sem.at[at])
-            copy.start()
-            copies.append(copy)
-            at += 1
-    for copy in copies:
-        copy.wait()
-
-
-def join(index, pieces):
-    counts = [p.shape[0] for p in pieces]
-    rows, columns = pieces[0].shape[1:]
-    total = sum(counts)
-    return pl.pallas_call(
-        functools.partial(join_kernel, counts=counts),
-        in_specs=[pl.BlockSpec(memory_space=pltpu.SMEM)] + [pl.BlockSpec(memory_space=pl.ANY)] * len(pieces),
-        out_specs=pl.BlockSpec(memory_space=pl.ANY),
-        out_shape=jax.ShapeDtypeStruct((total, rows, columns), pieces[0].dtype),
-        scratch_shapes=[pltpu.SemaphoreType.DMA((total,))],
-        cost_estimate=pl.CostEstimate(flops=0, bytes_accessed=4 * total * rows * columns, transcendentals=0),
-        name="join",
-    )(index, *pieces)
+    line = jnp.concatenate([near, send(near, 0, 3), send(near[:2], 0, -3)], axis=0)
+    steps = [-1, 0, 1, -4, -3, -2, 2, 3]
+    return [(0, steps, line)] + [(dx, steps, send(line, -dx, 0)) for dx in (-1, 1, 2)]
 
 
 def tokens_kernel(*refs, counts):
@@ -417,12 +309,12 @@
     rows, width = adapt_weight.shape
     ring = lambda group, k: [(group * n_mdl + i, group * n_mdl + (i + k) % n_mdl) for i in range(n_mdl)]
 
+    weight = lax.all_gather(qkv_weight, "seq", axis=0, tiled=True)
     twin = lax.ppermute(adapt_weight, ("grp", "seq"), of_group(0, SWAP))
     held = jnp.where(
         core == 0, jnp.concatenate([adapt_weight, twin]), jnp.concatenate([twin, adapt_weight])
     )
-    held = jnp.pad(held, ((0, qkv_weight.shape[0] - 2 * rows), (0, qkv_weight.shape[1] - width)))
-    pieces, direct = spread(jnp.where(grp == 0, held, qkv_weight)[None])
+    pieces = spread(jnp.pad(held, ((0, ADAPT_SLOT - 2 * rows), (0, 0)))[None])
 
     behind = lax.ppermute(text, both, ring(1, 1))
     ahead = lax.ppermute(text, both, ring(1, -1))
@@ -436,7 +328,7 @@
     up = [(i, i + 1) for i in range(lax.axis_size("seq") - 1)]
     before_edge = lax.ppermute(gated[frames - EDGE :], ("grp", "seq"), of_group(0, up))
     after_edge = lax.ppermute(gated[:EDGE], ("grp", "seq"), of_group(0, [(j, i) for i, j in up]))
-    term = conv(before_edge, gated, after_edge, dw_kernel, pw_weight, pieces[0][2], behind, ahead)
+    term = conv(before_edge, gated, after_edge, dw_kernel, pw_weight, behind, ahead)
     term = term.astype(jnp.float32) + lax.ppermute(
         term, both, [(0, 1), (1, 0), (2, 3), (3, 2)]
     ).astype(jnp.float32)
@@ -451,28 +343,17 @@
     column = jnp.arange(chips.shape[0] * ADAPT_SLOT, dtype=jnp.int32) % ADAPT_SLOT
     source = jnp.where(column < 2 * rows, jnp.repeat(chips, ADAPT_SLOT) * 2 * rows + column, -1)
     expand = (jnp.arange(audio.shape[1], dtype=jnp.int32)[:, None] == source[None]).astype(jnp.bfloat16)
-    tokens = tokens_part([p for _, _, p in pieces[:-1]] + [direct], pooled_audio, term, other, expand, second)
-
-    own = [p for _, _, p in pieces]
-    swap = lambda v: lax.ppermute(v, ("grp", "seq"), of_group(1, SWAP))
-    exchanged = [
-        swap(jnp.concatenate(own[:4], axis=0)),
-        swap(jnp.concatenate(own[4:7], axis=0)),
-        swap(own[7]),
-    ]
-    index = jnp.concatenate([chips * 2 + core, chips * 2 + 1 - core])
-    weight = join(index, own + exchanged).reshape(-1, qkv_weight.shape[1])
+    tokens = tokens_part([p for _, _, p in pieces], pooled_audio, term, other, expand, second)
 
     tables = rotary_tables(2 * text.shape[0])
     gain = norm_gain.reshape(n_mdl, 1, width)
     order = (mdl + jnp.arange(n_mdl, dtype=jnp.int32)) % n_mdl
-    q, kt, vt = text_part(order, words, gain, weight, qkv_bias[None], tables)
     same = lax.ppermute(tokens, both, [(i, n_mdl + i) for i in range(n_mdl)])
     following = lax.ppermute(tokens, both, [(i, n_mdl + (i - 1) % n_mdl) for i in range(n_mdl)])
     across = lax.ppermute(following, both, ring(1, -1))
     last = lax.ppermute(same, both, ring(1, 1))
     sounds = [same, following, across, last]
-    context = audio_part(order, sounds, gain, weight, qkv_bias[None, -2 * HEAD :], tables, q, kt, vt)
+    context = decode(order, words, sounds, gain, weight, qkv_bias[None], tables)
     return jnp.where(grp == 0, tokens, context)[None]
 
 

time: 425 us -> 166 us (0.39)
  the two profiles are of different devices: /device:TPU:1 before, /device:TPU:74 now
where the time goes in v3:
time: 166 us; the launch traced here: 165 us
  waiting for transfers between devices  82.8 us (50%)
  starting transfers between devices  34.1 us (21%)
  Pallas kernels  22.5 us (14%)
  between operations  14.8 us (9%)
  local copies, waits for them, and re-layouts  5.8 us (3%)
  other arithmetic  5.52 us (3%)
    ppermute x1, waiting for transfers between devices, shards(): lax.ppermute(tokens, both, [(i, n_mdl + (i - 1) % n_mdl) for i in range(n...  68.7 us
    pallas_call x1, Pallas kernels, decode(): pl.pallas_call(functools.partial(decode_kernel, parts=parts), grid_spec=p...  9.47 us
    ppermute x1, starting transfers between devices, shards(): last = lax.ppermute(same, both, ring(1, 1))  6.13 us
    ppermute x1, starting transfers between devices, shards(): behind = lax.ppermute(text, both, ring(1, 1))  6.09 us
    ppermute x1, starting transfers between devices, shards(): ahead = lax.ppermute(text, both, ring(1, -1))  5.87 us
    ppermute x1, waiting for transfers between devices, shards(): last = lax.ppermute(same, both, ring(1, 1))  5.7 us
    pallas_call x1, Pallas kernels, conv(): pl.pallas_call(conv_kernel, in_specs=[vmem] * 5 + [pl.BlockSpec(memory_sp...  5.48 us
    ppermute x7, starting transfers between devices, spread(): lax.ppermute(v, ('grp', 'seq'), of_group(0, place(dx, dy)))  4.8 us
  transfers between devices with their start and end apart: 20, of which 4 were waited for; matrix products, arithmetic and copies ran while one was open for 4% of the time, Pallas kernels for 8%

profile of v3, /device:TPU:74, one launch (start us, length us, event | category | flops | bytes accessed | tf_op | source)
XLA Modules:
  0.0 165.5 jit_solution(8617564964520973349)
XLA Ops:
  6.5 0.7 all-gather.2.cloned.1.call-update
  7.3 6.1 %collective-permute-start.10 = (bf16[192,896]{1,0:T(8,128)(2,1)}, bf16[192,896]{1,0:T(8,128)(2,1)S(1)}, u32[]{:S(2)}, u32[]{:S(2)}) collective-permute-start(bf16[192,896]{1,0:T(8,128)(2,1)} %refs_0_.1), channel_id=1, source_target_pairs={{256,257},{257,258},{258,259},{259,256},{260,261},{261,262},{262,2... | collective-permute-start | bytes 1032200 | tf_op jit(solution)/shard_map/ppermute | solution.py:319
  13.4 5.9 %collective-permute-start.11 = (bf16[192,896]{1,0:T(8,128)(2,1)}, bf16[192,896]{1,0:T(8,128)(2,1)S(1)}, u32[]{:S(2)}, u32[]{:S(2)}) collective-permute-start(bf16[192,896]{1,0:T(8,128)(2,1)} %refs_0_.1), channel_id=1, source_target_pairs={{256,259},{257,256},{258,257},{259,258},{260,263},{261,260},{262,2... | collective-permute-start | bytes 1032200 | tf_op jit(solution)/shard_map/ppermute | solution.py:320
  20.6 0.7 broadcast_in_dim.24.gain_ref
  21.3 1.5 copy-done.3
  22.8 1.4 copy-done.4
  24.2 3.8 %gate.1 = (bf16[768,320]{1,0:T(8,128)(2,1)S(1)}, f32[192,1280]{1,0:T(8,128)S(1)}) custom-call(s32[1]{0:T(128)S(6)} %sub.14.count_ref, bf16[768,1280]{1,0:T(8,128)(2,1)S(1)} %copy-done.3, f32[1,1280]{1,0:T(1,128)S(1)} %broadcast_in_dim.24.gain_ref, bf16[2,320,1280]{2,1,0:T(8,128)(2,1)S(1)} %bitcast.40), custom_call_target="tpu_custom_call" | custom-call | flops 1258291200 | bytes 7864320 | tf_op jit(solution)/shard_map/gate/pallas_call | solution.py:162
  29.4 0.7 collective-permute-start.1
  31.5 0.7 collective-permute-start.3
  32.2 0.7 collective-permute-start.4
  32.9 5.5 %conv.1 = bf16[192,1280]{1,0:T(8,128)(2,1)S(1)} custom-call(bf16[16,320]{1,0:T(8,128)(2,1)S(1)} %collective-permute-done.8.before_ref, bf16[768,320]{1,0:T(8,128)(2,1)S(1)} %get-tuple-element.8.gated_ref, bf16[16,320]{1,0:T(8,128)(2,1)S(1)} %collective-permute-done.9.after_ref, f32[31,320]{1,0:T(8,128)S(1)} %copy-done.6, bf16[320,1280]{1,0:T(8,128)(2,1)S(1)} %copy-done.5, ...), custom_call_target="tpu_custom_call" | custom-call | flops 5000000000 | bytes 1966080 | tf_op jit(solution)/shard_map/conv/pallas_call | solution.py:224
  38.4 0.7 collective-permute-start.12
  39.2 2.5 %collective-permute-start.14 = (bf16[192,896]{1,0:T(8,128)(2,1)S(1)}, bf16[192,896]{1,0:T(8,128)(2,1)S(1)}, u32[]{:S(2)}, u32[]{:S(2)}) collective-permute-start(bf16[192,896]{1,0:T(8,128)(2,1)S(1)} %collective-permute-done.10.refs_0_.refs_3_), channel_id=1, source_target_pairs={{256,257},{257,258},{258,259},{259,256},{260,261},{261,262},{262,2... | collective-permute-start | bytes 1032200 | tf_op jit(solution)/shard_map/ppermute | solution.py:321
  41.7 0.7 collective-permute-start.5
  42.4 0.7 collective-permute-start.6
  43.1 0.7 collective-permute-start.7
  44.0 0.7 collective-permute-start.13
  44.7 3.6 %fusion.refs_7_ = bf16[1280,1536]{1,0:T(8,128)(2,1)} fusion(s32[1536]{0:T(1024)S(1)} %add_select_fusion.1), kind=kLoop, calls=%fused_computation.1 | loop fusion | flops 3932160 | bytes 3938304 | tf_op jit(solution)/shard_map/convert_element_type | solution.py:345
  48.2 4.4 %collective-permute-done.14.refs_8_.refs_2_ = bf16[192,896]{1,0:T(8,128)(2,1)S(1)} collective-permute-done((bf16[192,896]{1,0:T(8,128)(2,1)S(1)}, bf16[192,896]{1,0:T(8,128)(2,1)S(1)}, u32[]{:S(2)}, u32[]{:S(2)}) %collective-permute-start.14) | collective-permute-done | bytes 344096 | tf_op jit(solution)/shard_map/ppermute | solution.py:321
  52.8 3.7 %tokens_part.1 = bf16[192,896]{1,0:T(8,128)(2,1)S(1)} custom-call(bf16[8,48,896]{2,1,0:T(8,128)(2,1)S(1)} %constant_dynamic-update-slice_fusion.refs_0_, bf16[8,48,896]{2,1,0:T(8,128)(2,1)S(1)} %collective-permute-done.5.refs_1_, bf16[8,48,896]{2,1,0:T(8,128)(2,1)S(1)} %collective-permute-done.6.refs_2_, ...), custom_call_target="tpu_custom_call" | custom-call | flops 1283457024 | bytes 8000000 | tf_op jit(solution)/shard_map/tokens_part/pallas_call | solution.py:283
  56.5 1.3 collective-permute-start.16
  57.8 1.3 collective-permute-start.15
  59.2 68.7 %collective-permute-done.16.refs_5_ = bf16[192,896]{1,0:T(8,128)(2,1)S(1)} collective-permute-done((bf16[192,896]{1,0:T(8,128)(2,1)S(1)}, bf16[192,896]{1,0:T(8,128)(2,1)S(1)}, u32[]{:S(2)}, u32[]{:S(2)}) %collective-permute-start.16) | collective-permute-done | bytes 344096 | tf_op jit(solution)/shard_map/ppermute | solution.py:352
  127.9 2.8 %collective-permute-start.17 = (bf16[192,896]{1,0:T(8,128)(2,1)S(1)}, bf16[192,896]{1,0:T(8,128)(2,1)S(1)}, u32[]{:S(2)}, u32[]{:S(2)}) collective-permute-start(bf16[192,896]{1,0:T(8,128)(2,1)S(1)} %collective-permute-done.16.refs_5_), channel_id=1, source_target_pairs={{256,259},{257,256},{258,257},{259,258},{260,263},{261,260},{262,2... | collective-permute-start | bytes 1032200 | tf_op jit(solution)/shard_map/ppermute | solution.py:353
  130.7 6.1 %collective-permute-start.18 = (bf16[192,896]{1,0:T(8,128)(2,1)S(1)}, bf16[192,896]{1,0:T(8,128)(2,1)S(1)}, u32[]{:S(2)}, u32[]{:S(2)}) collective-permute-start(bf16[192,896]{1,0:T(8,128)(2,1)S(1)} %collective-permute-done.15.refs_4_), channel_id=1, source_target_pairs={{256,257},{257,258},{258,259},{259,256},{260,261},{261,262},{262,2... | collective-permute-start | bytes 1032200 | tf_op jit(solution)/shard_map/ppermute | solution.py:354
  136.8 0.8 fusion.1
  137.8 3.2 %collective-permute-done.17.refs_6_ = bf16[192,896]{1,0:T(8,128)(2,1)S(1)} collective-permute-done((bf16[192,896]{1,0:T(8,128)(2,1)S(1)}, bf16[192,896]{1,0:T(8,128)(2,1)S(1)}, u32[]{:S(2)}, u32[]{:S(2)}) %collective-permute-start.17) | collective-permute-done | bytes 344096 | tf_op jit(solution)/shard_map/ppermute | solution.py:353
  140.9 5.7 %collective-permute-done.18.refs_7_ = bf16[192,896]{1,0:T(8,128)(2,1)S(1)} collective-permute-done((bf16[192,896]{1,0:T(8,128)(2,1)S(1)}, bf16[192,896]{1,0:T(8,128)(2,1)S(1)}, u32[]{:S(2)}, u32[]{:S(2)}) %collective-permute-start.18) | collective-permute-done | bytes 344096 | tf_op jit(solution)/shard_map/ppermute | solution.py:354
  146.6 0.7 copy-done.1
  147.4 1.0 copy-done.2
  148.4 9.5 %decode.1 = bf16[192,896]{1,0:T(8,128)(2,1)S(1)} custom-call(s32[4]{0:T(128)S(1)} %and_select_fusion.order_ref, bf16[192,896]{1,0:T(8,128)(2,1)S(1)} %copy-done, bf16[192,896]{1,0:T(8,128)(2,1)S(1)} %collective-permute-done.11.refs_1_, bf16[192,896]{1,0:T(8,128)(2,1)S(1)} %collective-permute-done.14.refs_8_.refs_2_, ...), custom_call_target="tpu_custom_call" | custom-call | flops 1585446912 | bytes 9633792 | tf_op jit(solution)/shard_map/decode/pallas_call | solution.py:104
  157.8 0.8 select_bitcast_fusion
  (59 shorter events, 3.5 us)
Async XLA Ops:
  6.5 22.8 %copy-start.7 = (bf16[20,896]{1,0:T(8,128)(2,1)S(1)}, bf16[20,896]{1,0:T(8,128)(2,1)}, u32[]{:S(2)}) copy-start(bf16[20,896]{1,0:T(8,128)(2,1)} %param.17) | copy-start | bytes 107524
  6.5 26.4 %copy-start.6 = (f32[31,320]{1,0:T(8,128)S(1)}, f32[31,320]{1,0:T(8,128)}, u32[]{:S(2)}) copy-start(f32[31,320]{1,0:T(8,128)} %taps_ref.1) | copy-start | bytes 119044
  6.5 140.8 %all-gather.2.cloned.1.call-start = ((), (), s32[]{:S(2)}) async-start(), calls=%async_computation | async-start | bytes 8386560 | tf_op jit(solution)/shard_map/all_gather | solution.py:312
  7.3 25.6 %collective-permute-start.10 = (bf16[192,896]{1,0:T(8,128)(2,1)}, bf16[192,896]{1,0:T(8,128)(2,1)S(1)}, u32[]{:S(2)}, u32[]{:S(2)}) collective-permute-start(bf16[192,896]{1,0:T(8,128)(2,1)} %refs_0_.1), channel_id=1, source_target_pairs={{256,257},{257,258},{258,259},{259,256},{260,261},{261,262},{262,2... | collective-permute-start | bytes 1032200 | tf_op jit(solution)/shard_map/ppermute | solution.py:319
  13.4 19.5 %collective-permute-start.11 = (bf16[192,896]{1,0:T(8,128)(2,1)}, bf16[192,896]{1,0:T(8,128)(2,1)S(1)}, u32[]{:S(2)}, u32[]{:S(2)}) collective-permute-start(bf16[192,896]{1,0:T(8,128)(2,1)} %refs_0_.1), channel_id=1, source_target_pairs={{256,259},{257,256},{258,257},{259,258},{260,263},{261,260},{262,2... | collective-permute-start | bytes 1032200 | tf_op jit(solution)/shard_map/ppermute | solution.py:320
  19.2 10.1 %collective-permute-start = (bf16[20,896]{1,0:T(8,128)(2,1)}, bf16[20,896]{1,0:T(8,128)(2,1)S(1)}, u32[]{:S(2)}, u32[]{:S(2)}) collective-permute-start(bf16[20,896]{1,0:T(8,128)(2,1)} %param.17), channel_id=1, source_target_pairs={{0,4},{4,0},{8,12},{12,8},{16,20},{20,16},{24,28},{28,24},{32,36},... | collective-permute-start | bytes 107528 | tf_op jit(solution)/shard_map/ppermute | solution.py:313
  21.3 1.5 copy-start.3
  22.8 1.4 copy-start.4
  24.2 8.7 %copy-start.5 = (bf16[320,1280]{1,0:T(8,128)(2,1)S(1)}, bf16[320,1280]{1,0:T(8,128)(2,1)}, u32[]{:S(2)}) copy-start(bf16[320,1280]{1,0:T(8,128)(2,1)} %pw_ref.1) | copy-start | bytes 2457604
  28.1 4.1 %collective-permute-start.8 = (bf16[16,320]{1,0:T(8,128)(2,1)S(1)}, bf16[16,320]{1,0:T(8,128)(2,1)S(1)}, u32[]{:S(2)}, u32[]{:S(2)}) collective-permute-start(bf16[16,320]{1,0:T(8,128)(2,1)S(1)} %get-tuple-element.12), channel_id=1, source_target_pairs={{0,4},{4,8},{8,12},{12,16},{16,20},{20,24},{24,28},{28,32},{32,36}... | collective-permute-start | bytes 30728 | tf_op jit(solution)/shard_map/ppermute | solution.py:329
  29.4 1.4 collective-permute-start.1
  30.0 1.4 collective-permute-start.2
  30.7 2.1 %collective-permute-start.9 = (bf16[16,320]{1,0:T(8,128)(2,1)S(1)}, bf16[16,320]{1,0:T(8,128)(2,1)S(1)}, u32[]{:S(2)}, u32[]{:S(2)}) collective-permute-start(bf16[16,320]{1,0:T(8,128)(2,1)S(1)} %get-tuple-element.11), channel_id=1, source_target_pairs={{4,0},{8,4},{12,8},{16,12},{20,16},{24,20},{28,24},{32,28},{36,32}... | collective-permute-start | bytes 30728 | tf_op jit(solution)/shard_map/ppermute | solution.py:330
  31.5 10.2 %collective-permute-start.3 = (bf16[3,48,896]{2,1,0:T(8,128)(2,1)S(1)}, bf16[3,48,896]{2,1,0:T(8,128)(2,1)S(1)}, u32[]{:S(2)}, u32[]{:S(2)}) collective-permute-start(bf16[3,48,896]{2,1,0:T(8,128)(2,1)S(1)} %pad_maximum_fusion), channel_id=1, source_target_pairs={{0,24},{4,28},{8,32},{12,36},{16,40},{20,44},{24,48},{28,52},{32,5... | collective-permute-start | bytes 774152 | tf_op jit(solution)/shard_map/ppermute | solution.py:259
  32.2 9.5 %collective-permute-start.4 = (bf16[2,48,896]{2,1,0:T(8,128)(2,1)S(1)}, bf16[2,48,896]{2,1,0:T(8,128)(2,1)S(1)}, u32[]{:S(2)}, u32[]{:S(2)}) collective-permute-start(bf16[2,48,896]{2,1,0:T(8,128)(2,1)S(1)} %pad_maximum_fusion.3), channel_id=1, source_target_pairs={{0,40},{4,44},{8,48},{12,52},{16,56},{20,60},{24,0},{28,4},{32,8},... | collective-permute-start | bytes 516104 | tf_op jit(solution)/shard_map/ppermute | solution.py:259
  38.4 5.4 %collective-permute-start.12 = (bf16[192,1280]{1,0:T(8,128)(2,1)S(1)}, bf16[192,1280]{1,0:T(8,128)(2,1)S(1)}, u32[]{:S(2)}, u32[]{:S(2)}) collective-permute-start(bf16[192,1280]{1,0:T(8,128)(2,1)S(1)} %conv.1), channel_id=1, source_target_pairs={{0,1},{1,0},{2,3},{3,2},{4,5},{5,4},{6,7},{7,6},{8,9},{9,8},{10,11... | collective-permute-start | bytes 1474568 | tf_op jit(solution)/shard_map/ppermute | solution.py:332
  39.2 13.5 %collective-permute-start.14 = (bf16[192,896]{1,0:T(8,128)(2,1)S(1)}, bf16[192,896]{1,0:T(8,128)(2,1)S(1)}, u32[]{:S(2)}, u32[]{:S(2)}) collective-permute-start(bf16[192,896]{1,0:T(8,128)(2,1)S(1)} %collective-permute-done.10.refs_0_.refs_3_), channel_id=1, source_target_pairs={{256,257},{257,258},{258,259},{259,256},{260,261},{261,262},{262,2... | collective-permute-start | bytes 1032200 | tf_op jit(solution)/shard_map/ppermute | solution.py:321
  41.7 11.0 %collective-permute-start.5 = (bf16[8,48,896]{2,1,0:T(8,128)(2,1)S(1)}, bf16[8,48,896]{2,1,0:T(8,128)(2,1)S(1)}, u32[]{:S(2)}, u32[]{:S(2)}) collective-permute-start(bf16[8,48,896]{2,1,0:T(8,128)(2,1)S(1)} %constant_dynamic-update-slice_fusion.refs_0_), channel_id=1, source_target_pairs={{0,64},{4,68},{8,72},{12,76},{16,80},{20,84},{24,88},{28,92},{32,9... | collective-permute-start | bytes 2064392 | tf_op jit(solution)/shard_map/ppermute | solution.py:259
  42.4 10.3 %collective-permute-start.6 = (bf16[8,48,896]{2,1,0:T(8,128)(2,1)S(1)}, bf16[8,48,896]{2,1,0:T(8,128)(2,1)S(1)}, u32[]{:S(2)}, u32[]{:S(2)}) collective-permute-start(bf16[8,48,896]{2,1,0:T(8,128)(2,1)S(1)} %constant_dynamic-update-slice_fusion.refs_0_), channel_id=1, source_target_pairs={{0,192},{4,196},{8,200},{12,204},{16,208},{20,212},{24,216},{28,22... | collective-permute-start | bytes 2064392 | tf_op jit(solution)/shard_map/ppermute | solution.py:259
  43.1 9.6 %collective-permute-start.7 = (bf16[8,48,896]{2,1,0:T(8,128)(2,1)S(1)}, bf16[8,48,896]{2,1,0:T(8,128)(2,1)S(1)}, u32[]{:S(2)}, u32[]{:S(2)}) collective-permute-start(bf16[8,48,896]{2,1,0:T(8,128)(2,1)S(1)} %constant_dynamic-update-slice_fusion.refs_0_), channel_id=1, source_target_pairs={{0,128},{4,132},{8,136},{12,140},{16,144},{20,148},{24,152},{28,15... | collective-permute-start | bytes 2064392 | tf_op jit(solution)/shard_map/ppermute | solution.py:259
  44.0 8.7 %collective-permute-start.13 = (bf16[192,1280]{1,0:T(8,128)(2,1)S(1)}, bf16[192,1280]{1,0:T(8,128)(2,1)S(1)}, u32[]{:S(2)}, u32[]{:S(2)}) collective-permute-start(bf16[192,1280]{1,0:T(8,128)(2,1)S(1)} %get-tuple-element.9), channel_id=1, source_target_pairs={{1,2},{2,1},{3,0},{0,3},{5,6},{6,5},{7,4},{4,7},{9,10},{10,9},{11,... | collective-permute-start | bytes 1474568 | tf_op jit(solution)/shard_map/ppermute | solution.py:335
  52.7 6.4 %copy-start.8 = (f32[3584]{0:T(1024)S(1)}, f32[3584]{0:T(1024)}, u32[]{:S(2)}) copy-start(f32[3584]{0:T(1024)} %param.19) | copy-start | bytes 43012
  52.7 6.4 %copy-start.9 = (f32[1152]{0:T(1024)S(1)}, f32[1152]{0:T(1024)}, u32[]{:S(2)}) copy-start(f32[1152]{0:T(1024)} %param.21) | copy-start | bytes 13828
  52.7 94.6 %copy-start = (bf16[192,896]{1,0:T(8,128)(2,1)S(1)}, bf16[192,896]{1,0:T(8,128)(2,1)}, u32[]{:S(2)}) copy-start(bf16[192,896]{1,0:T(8,128)(2,1)} %refs_0_.1) | copy-start | bytes 1032196
  56.5 71.4 %collective-permute-start.16 = (bf16[192,896]{1,0:T(8,128)(2,1)S(1)}, bf16[192,896]{1,0:T(8,128)(2,1)S(1)}, u32[]{:S(2)}, u32[]{:S(2)}) collective-permute-start(bf16[192,896]{1,0:T(8,128)(2,1)S(1)} %tokens_part.1), channel_id=1, source_target_pairs={{0,259},{1,256},{2,257},{3,258},{4,263},{5,260},{6,261},{7,262},{8... | collective-permute-start | bytes 1032200 | tf_op jit(solution)/shard_map/ppermute | solution.py:352
  57.8 72.9 %collective-permute-start.15 = (bf16[192,896]{1,0:T(8,128)(2,1)S(1)}, bf16[192,896]{1,0:T(8,128)(2,1)S(1)}, u32[]{:S(2)}, u32[]{:S(2)}) collective-permute-start(bf16[192,896]{1,0:T(8,128)(2,1)S(1)} %tokens_part.1), channel_id=1, source_target_pairs={{0,256},{1,257},{2,258},{3,259},{4,260},{5,261},{6,262},{7,263},{8... | collective-permute-start | bytes 1032200 | tf_op jit(solution)/shard_map/ppermute | solution.py:351
  127.9 13.1 %collective-permute-start.17 = (bf16[192,896]{1,0:T(8,128)(2,1)S(1)}, bf16[192,896]{1,0:T(8,128)(2,1)S(1)}, u32[]{:S(2)}, u32[]{:S(2)}) collective-permute-start(bf16[192,896]{1,0:T(8,128)(2,1)S(1)} %collective-permute-done.16.refs_5_), channel_id=1, source_target_pairs={{256,259},{257,256},{258,257},{259,258},{260,263},{261,260},{262,2... | collective-permute-start | bytes 1032200 | tf_op jit(solution)/shard_map/ppermute | solution.py:353
  130.7 16.0 %collective-permute-start.18 = (bf16[192,896]{1,0:T(8,128)(2,1)S(1)}, bf16[192,896]{1,0:T(8,128)(2,1)S(1)}, u32[]{:S(2)}, u32[]{:S(2)}) collective-permute-start(bf16[192,896]{1,0:T(8,128)(2,1)S(1)} %collective-permute-done.15.refs_4_), channel_id=1, source_target_pairs={{256,257},{257,258},{258,259},{259,256},{260,261},{261,262},{262,2... | collective-permute-start | bytes 1032200 | tf_op jit(solution)/shard_map/ppermute | solution.py:354
  146.6 0.7 copy-start.1
  147.4 1.0 copy-start.2
Sparse Core Ops, SparseCore 0:
  10.6 94.3 all-gather.1

commit v4 on v3

v4 whole, which is shorter than its diff:
```python
import functools

import jax
import jax.numpy as jnp
from jax import lax
from jax.experimental import pallas as pl
from jax.experimental.pallas import tpu as pltpu
from jax.sharding import Mesh
from jax.sharding import PartitionSpec as P

HEADS = 28
KV = 4
HEAD = 128
VMEM = 48 * 1024 * 1024
NX = 4
NY = 8
SEQ = ("x", "y", "core")


def rotary_tables(count):
    half = HEAD // 2
    freq = 1000000.0 ** (-(jnp.arange(half, dtype=jnp.float32) * 2.0 / HEAD))
    angle = jnp.arange(count, dtype=jnp.int32).astype(jnp.float32)[:, None] * freq[None, :]
    cosine, sine = jnp.cos(angle), jnp.sin(angle)
    return jnp.concatenate([cosine, cosine], 1), jnp.concatenate([-sine, sine], 1)


def turned(values, cosine, sine):
    return values * cosine + pltpu.roll(values, HEAD // 2, 1) * sine


def decode_kernel(order_ref, *refs, parts):
    words, sounds, line, halves = refs[:parts], refs[parts : 2 * parts], refs[2 * parts], refs[2 * parts + 1 : 4 * parts - 1]
    gain_ref, bias_ref, cos_ref, sin_ref, out_ref, rows, weight, acc, acc_kv, square, square_kv, sem = refs[4 * parts - 1 :]
    count, total = acc.shape
    heads = total // HEAD - 2
    depth = weight.shape[1]
    core = order_ref[2 * parts]
    copies = [[pltpu.make_async_copy(line, weight.at[0], sem.at[0])]]
    for i in range(parts - 1):
        pair = []
        for j in range(2):
            first = pl.multiple_of((core if j == 0 else 1 - core) * (depth // 2), depth // 2)
            at = 1 + 2 * i + j
            pair.append(
                pltpu.make_async_copy(halves[2 * i + j], weight.at[i + 1, pl.ds(first, depth // 2)], sem.at[at])
            )
        copies.append(pair)
    for pair in copies:
        for copy in pair:
            copy.start()
    square[...] = jnp.zeros_like(square)
    square_kv[...] = jnp.zeros_like(square_kv)
    for i in range(parts):
        block = order_ref[i]
        for ref, total_square, first in ((words[i], square, 0), (sounds[i], square_kv, count)):
            x = ref[...].astype(jnp.float32)
            total_square[...] += jnp.sum(x * x, axis=1, keepdims=True)
            rows[block, first : first + count] = (x * gain_ref[block]).astype(jnp.bfloat16)
    for i in range(parts):
        block = order_ref[parts + i]
        for copy in copies[i]:
            copy.wait()
        term = jnp.dot(rows[block, :count], weight[i], preferred_element_type=jnp.float32)
        term_kv = jnp.dot(rows[block, count:], weight[i, :, heads * HEAD :], preferred_element_type=jnp.float32)
        acc[...] = term if i == 0 else acc[...] + term
        acc_kv[...] = term_kv if i == 0 else acc_kv[...] + term_kv
    width = parts * depth
    scale = lax.rsqrt(square[...] / width + 1e-6)
    scale_kv = lax.rsqrt(square_kv[...] / width + 1e-6)
    cosine, sine = cos_ref[count:], sin_ref[count:]
    key_cols = slice(heads * HEAD, (heads + 1) * HEAD)
    value_cols = slice((heads + 1) * HEAD, total)
    keys = jnp.concatenate(
        [
            turned(acc_kv[:, :HEAD] * scale_kv + bias_ref[:, key_cols], cos_ref[:count], sin_ref[:count]),
            turned(acc[:, key_cols] * scale + bias_ref[:, key_cols], cosine, sine),
        ],
        axis=0,
    ).astype(jnp.bfloat16)
    values = jnp.concatenate(
        [
            acc_kv[:, HEAD:] * scale_kv + bias_ref[:, value_cols],
            acc[:, value_cols] * scale + bias_ref[:, value_cols],
        ],
        axis=0,
    ).astype(jnp.bfloat16)
    row = lax.broadcasted_iota(jnp.int32, (count, 2 * count), 0)
    col = lax.broadcasted_iota(jnp.int32, (count, 2 * count), 1)
    allowed = col <= row + count
    for h in range(heads):
        cols = slice(h * HEAD, (h + 1) * HEAD)
        query = turned(acc[:, cols] * scale + bias_ref[:, cols], cosine, sine).astype(jnp.bfloat16)
        scores = lax.dot_general(
            query, keys, (((1,), (1,)), ((), ())), preferred_element_type=jnp.float32
        ) * (HEAD**-0.5)
        scores = jnp.where(allowed, scores, -1e30)
        weights = jnp.exp(scores - jnp.max(scores, axis=1, keepdims=True))
        probs = weights * (1.0 / jnp.sum(weights, axis=1, keepdims=True))
        out_ref[:, cols] = jnp.dot(
            probs.astype(jnp.bfloat16), values, preferred_element_type=jnp.float32
        ).astype(jnp.bfloat16)


def decode(order, words, sounds, line, halves, gain, bias, tables):
    parts = len(words)
    count, width = words[0].shape
    total = line.shape[1]
    columns = total - 2 * HEAD
    vmem = pl.BlockSpec(memory_space=pltpu.VMEM)
    anywhere = pl.BlockSpec(memory_space=pl.ANY)
    return pl.pallas_call(
        functools.partial(decode_kernel, parts=parts),
        in_specs=[pl.BlockSpec(memory_space=pltpu.SMEM)]
        + [vmem] * (2 * parts)
        + [anywhere] * (1 + len(halves))
        + [vmem] * 4,
        out_specs=vmem,
        scratch_shapes=[
            pltpu.VMEM((parts, 2 * count, width), jnp.bfloat16),
            pltpu.VMEM((parts, width, total), jnp.bfloat16),
            pltpu.VMEM((count, total), jnp.float32),
            pltpu.VMEM((count, 2 * HEAD), jnp.float32),
            pltpu.VMEM((count, 1), jnp.float32),
            pltpu.VMEM((count, 1), jnp.float32),
            pltpu.SemaphoreType.DMA((1 + len(halves),)),
        ],
        out_shape=jax.ShapeDtypeStruct((count, columns), jnp.bfloat16),
        compiler_params=pltpu.CompilerParams(vmem_limit_bytes=VMEM),
        cost_estimate=pl.CostEstimate(
            flops=2 * count * parts * width * total, bytes_accessed=2 * parts * width * (total + count), transcendentals=0
        ),
        name="decode",
    )(order, *words, *sounds, line, *halves, gain, bias, *tables)


def pooling(rows):
    r = lax.broadcasted_iota(jnp.int32, (rows // 4, rows), 0)
    c = lax.broadcasted_iota(jnp.int32, (rows // 4, rows), 1)
    return jnp.where((c >= 4 * r) & (c < 4 * r + 4), 0.25, 0.0).astype(jnp.bfloat16)


def dot_t(a, b):
    return lax.dot_general(a, b, (((1,), (1,)), ((), ())), preferred_element_type=jnp.float32)


def gate_kernel(count_ref, audio_ref, gain_ref, weight_ref, gated_ref, pooled_ref):
    audio = audio_ref[...]
    rows = audio.astype(jnp.float32)
    centred = rows - jnp.mean(rows, axis=1, keepdims=True)
    spread = jnp.mean(centred * centred, axis=1, keepdims=True)
    normed = (centred * lax.rsqrt(spread + 1e-5) * gain_ref[...]).astype(jnp.bfloat16)
    left = dot_t(normed, weight_ref[0])
    right = dot_t(normed, weight_ref[1])
    frame = pl.program_id(0) * rows.shape[0] + lax.broadcasted_iota(jnp.int32, (rows.shape[0], 1), 0)
    gated = left * (1.0 / (1.0 + jnp.exp(-right)))
    gated_ref[...] = jnp.where(frame < count_ref[0], gated, 0.0).astype(gated_ref.dtype)
    pooled_ref[...] = jnp.dot(pooling(rows.shape[0]), audio, preferred_element_type=jnp.float32)


def gate(left_frames, audio, gain, weight):
    frames, width = audio.shape
    columns = weight.shape[1]
    block = 256
    return pl.pallas_call(
        gate_kernel,
        grid=(frames // block,),
        in_specs=[
            pl.BlockSpec(memory_space=pltpu.SMEM),
            pl.BlockSpec((block, width), lambda i: (i, 0)),
            pl.BlockSpec((1, width), lambda i: (0, 0)),
            pl.BlockSpec((2, columns, width), lambda i: (0, 0, 0)),
        ],
        out_specs=[
            pl.BlockSpec((block, columns), lambda i: (i, 0)),
            pl.BlockSpec((block // 4, width), lambda i: (i, 0)),
        ],
        out_shape=[
            jax.ShapeDtypeStruct((frames, columns), jnp.bfloat16),
            jax.ShapeDtypeStruct((frames // 4, width), jnp.float32),
        ],
        compiler_params=pltpu.CompilerParams(vmem_limit_bytes=VMEM),
        cost_estimate=pl.CostEstimate(
            flops=4 * frames * width * columns, bytes_accessed=2 * frames * width * 4, transcendentals=frames * columns
        ),
        name="gate",
    )(left_frames, audio, gain, weight)


EDGE = 16


def conv_kernel(tag_ref, before_ref, gated_ref, after_ref, taps_ref, pw_ref, *refs):
    term_ref, same_ref, padded, act = refs[-4:]
    same_ref[0] = tag_ref[0]
    frames, columns = gated_ref.shape
    taps = taps_ref.shape[0]
    padded[:EDGE] = before_ref[...].astype(jnp.float32)
    padded[EDGE : EDGE + frames] = gated_ref[...].astype(jnp.float32)
    padded[EDGE + frames :] = after_ref[...].astype(jnp.float32)
    chunk = 64
    lead = EDGE - (taps - 1) // 2
    for at in range(0, columns, 128):
        lanes = slice(at, min(at + 128, columns))

        def body(i, carry, lanes=lanes):
            first = pl.multiple_of(i * chunk, chunk)
            window = padded[pl.ds(first, chunk + 2 * EDGE), lanes]
            total = jnp.zeros((chunk, window.shape[1]), jnp.float32)
            for turn in range(8):
                turned_by = window if turn == 0 else pltpu.roll(window, window.shape[0] - turn, 0)
                for offset in range(turn, lead + taps, 8):
                    if offset >= lead:
                        start = offset - turn
                        total = total + turned_by[start : start + chunk] * taps_ref[offset - lead, lanes][None]
            value = total * (1.0 / (1.0 + jnp.exp(-total)))
            act[pl.ds(first, chunk), lanes] = value.astype(jnp.bfloat16)
            return carry

        lax.fori_loop(0, frames // chunk, body, 0)
    pooled = jnp.dot(pooling(frames), act[...], preferred_element_type=jnp.float32).astype(jnp.bfloat16)
    term_ref[...] = jnp.dot(pooled, pw_ref[...], preferred_element_type=jnp.float32).astype(term_ref.dtype)


def conv(tag, before, gated, after, taps, pw, *after_these):
    frames, columns = gated.shape
    vmem = pl.BlockSpec(memory_space=pltpu.VMEM)
    return pl.pallas_call(
        conv_kernel,
        in_specs=[pl.BlockSpec(memory_space=pltpu.SMEM)]
        + [vmem] * 5
        + [pl.BlockSpec(memory_space=pl.ANY)] * len(after_these),
        out_specs=[vmem, pl.BlockSpec(memory_space=pltpu.SMEM)],
        out_shape=[
            jax.ShapeDtypeStruct((frames // 4, pw.shape[1]), jnp.bfloat16),
            jax.ShapeDtypeStruct((1,), jnp.int32),
        ],
        scratch_shapes=[
            pltpu.VMEM((frames + 2 * EDGE, columns), jnp.float32),
            pltpu.VMEM((frames, columns), jnp.bfloat16),
        ],
        compiler_params=pltpu.CompilerParams(vmem_limit_bytes=VMEM),
        cost_estimate=pl.CostEstimate(
            flops=5_000_000_000, bytes_accessed=2 * frames * columns * 4, transcendentals=frames * columns
        ),
        name="conv",
    )(tag, before, gated, after, taps, pw, *after_these)


def place(shift_x, shift_y):
    return [
        ((x * NY + y) * 2 + c, ((x + shift_x) % NX * NY + (y + shift_y) % NY) * 2 + c)
        for x in range(NX)
        for y in range(NY)
        for c in range(2)
    ]


SWAP = [(i, i ^ 1) for i in range(NX * NY * 2)]


def of_group(group, pairs):
    count = NX * NY * 2
    return [(group * count + i, group * count + j) for i, j in pairs]


def tokens_kernel(at_ref, *refs, counts):
    pieces = refs[: len(counts)]
    audio_ref, term_ref, other_ref = refs[len(counts) : len(counts) + 3]
    out_ref, weight = refs[-2:]
    run = min(counts)
    at = 0
    for ref, count in zip(pieces, counts, strict=True):
        for first in range(0, count, run):
            weight[pl.ds(pl.multiple_of(at_ref[at] * run, run), run)] = ref[first : first + run]
            at += 1
    pooled = (audio_ref[...] + term_ref[...] + other_ref[...].astype(jnp.float32)).astype(jnp.bfloat16)
    out_ref[...] = jnp.dot(pooled, weight[...], preferred_element_type=jnp.float32).astype(out_ref.dtype)


def tokens_part(at, pieces, pooled_audio, term, other, *after_these):
    counts = [p.shape[0] for p in pieces]
    count = pooled_audio.shape[0]
    columns = pieces[0].shape[1]
    vmem = pl.BlockSpec(memory_space=pltpu.VMEM)
    return pl.pallas_call(
        functools.partial(tokens_kernel, counts=counts),
        in_specs=[pl.BlockSpec(memory_space=pltpu.SMEM)]
        + [vmem] * (len(pieces) + 3)
        + [pl.BlockSpec(memory_space=pl.ANY)] * len(after_these),
        out_specs=vmem,
        out_shape=jax.ShapeDtypeStruct((count, columns), jnp.bfloat16),
        scratch_shapes=[pltpu.VMEM((sum(counts), columns), jnp.bfloat16)],
        compiler_params=pltpu.CompilerParams(vmem_limit_bytes=VMEM),
        cost_estimate=pl.CostEstimate(
            flops=2 * count * sum(counts) * columns, bytes_accessed=8000000, transcendentals=0
        ),
        name="tokens_part",
    )(at, *pieces, pooled_audio, term, other, *after_these)


def shards(
    audio, frame_count, ln_gain, glu_weight, dw_kernel, pw_weight, adapt_weight, text, norm_gain, qkv_weight, qkv_bias
):
    grp = lax.axis_index("grp")
    mdl = lax.axis_index("mdl")
    x, core = lax.axis_index("x"), lax.axis_index("core")
    seq = lax.axis_index(SEQ)
    n_mdl = lax.axis_size("mdl")
    both = ("grp", "mdl")
    rows, width = adapt_weight.shape
    ring = lambda group, k: [(group * n_mdl + i, group * n_mdl + (i + k) % n_mdl) for i in range(n_mdl)]

    held = jnp.pad(adapt_weight, ((0, qkv_weight.shape[0] - rows), (0, qkv_weight.shape[1] - width)))
    line = lax.all_gather(jnp.where(grp == 0, held, qkv_weight), ("y", "core"), axis=0, tiled=True)
    send = lambda group, v, pairs: lax.ppermute(v, ("grp",) + SEQ, of_group(group, pairs))
    behind = lax.ppermute(text, both, ring(1, 1))
    ahead = lax.ppermute(text, both, ring(1, -1))
    second = lax.ppermute(behind, both, ring(1, 1))
    words = [text, ahead, second, behind]

    frames = audio.shape[0]
    gated, pooled_audio = gate(
        frame_count - seq * frames, audio, ln_gain[None], jnp.swapaxes(glu_weight, 1, 2)
    )
    up = [(i, i + 1) for i in range(2 * NX * NY - 1)]
    before_edge = send(0, gated[frames - EDGE :], up)
    after_edge = send(0, gated[:EDGE], [(j, i) for i, j in up])
    term, turn = conv(core[None], before_edge, gated, after_edge, dw_kernel, pw_weight, behind, ahead)
    turn = turn[0]
    adapter = line.reshape(2 * NY, -1, line.shape[1])[:, :rows, :width].reshape(2 * NY * rows, width)
    half = lax.dynamic_slice_in_dim(adapter, turn * (NY * rows), NY * rows)
    adapter_far = [send(0, half, place(-dx, 0)) for dx in (-1, 1, 2)]
    adapter_twin = send(0, jnp.concatenate(adapter_far), SWAP)

    depth = line.shape[0] // 2
    half = lax.dynamic_slice_in_dim(line, turn * depth, depth)
    from_behind = send(1, half, place(1, 0))
    from_ahead = send(1, half, place(-1, 0))
    from_across = jnp.concatenate(
        [
            send(1, from_behind[: depth // 2], place(1, 0)),
            send(1, from_ahead[depth // 2 :], place(-1, 0)),
        ]
    )
    halves = []
    for piece in (from_behind, from_ahead, from_across):
        halves += [piece, send(1, piece, SWAP)]

    term = term.astype(jnp.float32) + lax.ppermute(
        term, both, [(0, 1), (1, 0), (2, 3), (3, 2)]
    ).astype(jnp.float32)
    other = lax.ppermute(term.astype(jnp.bfloat16), both, [(1, 2), (2, 1), (3, 0), (0, 3)])

    far = [(x - 1) % NX, (x + 1) % NX, (x + 2) % NX]
    at = [2 * x, 2 * x + 1] + [2 * i + core for i in far] + [2 * i + 1 - core for i in far]
    tokens = tokens_part(
        jnp.stack(at), [adapter] + adapter_far + [adapter_twin], pooled_audio, term, other, second
    )

    tables = rotary_tables(2 * text.shape[0])
    gain = norm_gain.reshape(n_mdl, 1, width)
    order = jnp.stack([(mdl + i) % n_mdl for i in range(n_mdl)] + [x] + far + [core])
    same = lax.ppermute(tokens, both, [(i, n_mdl + i) for i in range(n_mdl)])
    following = lax.ppermute(tokens, both, [(i, n_mdl + (i - 1) % n_mdl) for i in range(n_mdl)])
    across = lax.ppermute(following, both, ring(1, -1))
    last = lax.ppermute(same, both, ring(1, 1))
    sounds = [same, following, across, last]
    context = decode(order, words, sounds, line, halves, gain, qkv_bias[None], tables)
    return jnp.where(grp == 0, tokens, context)[None]


def solution(mesh):
    mesh = Mesh(
        mesh.devices.reshape(mesh.shape["grp"], NX, NY, 2, mesh.shape["mdl"]), ("grp", *SEQ, "mdl")
    )
    in_specs = (
        P(SEQ, None),
        P(),
        P(),
        P(None, None, "mdl"),
        P(None, "mdl"),
        P("mdl", None),
        P(SEQ, "mdl"),
        P(SEQ, "mdl"),
        P(),
        P(SEQ, "mdl"),
        P("mdl"),
    )
    out_specs = P("grp", SEQ, "mdl")
    return jax.shard_map(shards, mesh=mesh, in_specs=in_specs, out_specs=out_specs, check_vma=False)
```

time: 166 us -> 174 us (1.048)
  the two profiles are of different devices: /device:TPU:74 before, /device:TPU:64 now
where the time goes in v4:
time: 174 us; the launch traced here: 173 us
  waiting for transfers between devices  60.5 us (35%)
  starting transfers between devices  54.9 us (32%)
  Pallas kernels  20.3 us (12%)
  local copies, waits for them, and re-layouts  16.2 us (9%)
  between operations  15.9 us (9%)
  other arithmetic  5.25 us (3%)
    ppermute x13, starting transfers between devices, shards(): lax.ppermute(v, ('grp',) + SEQ, of_group(group, pairs))  25.2 us
    ppermute x13, waiting for transfers between devices, shards(): lax.ppermute(v, ('grp',) + SEQ, of_group(group, pairs))  21.2 us
    all_gather x1, waiting for transfers between devices, shards(): lax.all_gather(jnp.where(grp == 0, held, qkv_weight), ('y', 'core'), axis...  19.4 us
    unnamed x39, local copies, waits for them, and re-layouts  9.75 us
    ppermute x1, waiting for transfers between devices, shards(): lax.ppermute(tokens, both, [(i, n_mdl + (i - 1) % n_mdl) for i in range(n...  9.52 us
    pallas_call x1, Pallas kernels, decode(): pl.pallas_call(functools.partial(decode_kernel, parts=parts), in_specs=[p...  8.87 us
    ppermute x1, starting transfers between devices, shards(): across = lax.ppermute(following, both, ring(1, -1))  6.88 us
    ppermute x1, waiting for transfers between devices, shards(): last = lax.ppermute(same, both, ring(1, 1))  6.24 us
  transfers between devices with their start and end apart: 23, of which 6 were waited for; matrix products, arithmetic and copies ran while one was open for 5% of the time, Pallas kernels for 7%

profile of v4, /device:TPU:64, one launch (start us, length us, event | category | flops | bytes accessed | tf_op | source)
XLA Modules:
  0.0 173.1 jit_solution(13684952246786330946)
XLA Ops:
  6.5 1.6 pad_select_fusion
  8.2 6.1 %collective-permute-start.2 = (bf16[192,896]{1,0:T(8,128)(2,1)}, bf16[192,896]{1,0:T(8,128)(2,1)}, u32[]{:S(2)}, u32[]{:S(2)}) collective-permute-start(bf16[192,896]{1,0:T(8,128)(2,1)} %refs_0_.1), channel_id=1, source_target_pairs={{256,257},{257,258},{258,259},{259,256},{260,261},{261,262},{262,2... | collective-permute-start | bytes 1032200 | tf_op jit(solution)/shard_map/ppermute | solution.py:317
  14.3 5.9 %collective-permute-start.3 = (bf16[192,896]{1,0:T(8,128)(2,1)}, bf16[192,896]{1,0:T(8,128)(2,1)S(1)}, u32[]{:S(2)}, u32[]{:S(2)}) collective-permute-start(bf16[192,896]{1,0:T(8,128)(2,1)} %refs_0_.1), channel_id=1, source_target_pairs={{256,259},{257,256},{258,257},{259,258},{260,263},{261,260},{262,2... | collective-permute-start | bytes 1032200 | tf_op jit(solution)/shard_map/ppermute | solution.py:318
  21.5 1.5 copy-done.13
  23.0 1.4 copy-done.14
  24.5 3.8 %gate.1 = (bf16[768,320]{1,0:T(8,128)(2,1)S(1)}, f32[192,1280]{1,0:T(8,128)S(1)}) custom-call(s32[1]{0:T(128)S(6)} %sub.23.count_ref, bf16[768,1280]{1,0:T(8,128)(2,1)S(1)} %copy-done.13, f32[1,1280]{1,0:T(1,128)S(1)} %broadcast_in_dim.15.gain_ref, bf16[2,320,1280]{2,1,0:T(8,128)(2,1)S(1)} %bitcast.24), custom_call_target="tpu_custom_call" | custom-call | flops 1258291200 | bytes 7864320 | tf_op jit(solution)/shard_map/gate/pallas_call | solution.py:165
  29.8 5.5 %conv.1 = (bf16[192,1280]{1,0:T(8,128)(2,1)S(1)}, s32[1]{0:T(128)}) custom-call(s32[1]{0:T(128)} %bitcast.9.tag_ref, bf16[16,320]{1,0:T(8,128)(2,1)S(1)} %collective-permute-done.before_ref, bf16[768,320]{1,0:T(8,128)(2,1)S(1)} %get-tuple-element.9.gated_ref, bf16[16,320]{1,0:T(8,128)(2,1)S(1)} %collective-permute-done.1.after_ref, ...), custom_call_target="tpu_custom_call" | custom-call | flops 5000000000 | bytes 1966080 | tf_op jit(solution)/shard_map/conv/pallas_call | solution.py:228
  35.9 19.4 %all-gather.2.cloned.1.call-done.refs_8_ = bf16[896,1152]{1,0:T(8,128)(2,1)} async-done(((bf16[56,1152]{1,0:T(8,128)(2,1)}), bf16[896,1152]{1,0:T(8,128)(2,1)}) %all-gather.2.cloned.1.call-update) | async-done | bytes 2064400 | tf_op jit(solution)/shard_map/all_gather | solution.py:315
  55.4 2.3 %constant_dynamic-slice_fusion = bf16[448,1152]{1,0:T(8,128)(2,1)} fusion(bf16[896,1152]{1,0:T(8,128)(2,1)} %all-gather.2.cloned.1.call-done.refs_8_, s32[]{:T(128)S(6)} %select_n.64), kind=kLoop, calls=%fused_computation.13 | loop fusion | bytes 2064388 | tf_op jit(solution)/shard_map/dynamic_slice | solution.py:337
  57.6 4.6 %collective-permute-start.17 = (bf16[448,1152]{1,0:T(8,128)(2,1)}, bf16[448,1152]{1,0:T(8,128)(2,1)}, u32[]{:S(2)}, u32[]{:S(2)}) collective-permute-start(bf16[448,1152]{1,0:T(8,128)(2,1)} %constant_dynamic-slice_fusion), channel_id=1, source_target_pairs={{256,448},{260,452},{264,456},{268,460},{272,464},{276,468},{280,4... | collective-permute-start | bytes 3096584 | tf_op jit(solution)/shard_map/ppermute | solution.py:316
  62.2 1.9 %collective-permute-start.15 = (bf16[448,1152]{1,0:T(8,128)(2,1)}, bf16[448,1152]{1,0:T(8,128)(2,1)S(1)}, u32[]{:S(2)}, u32[]{:S(2)}) collective-permute-start(bf16[448,1152]{1,0:T(8,128)(2,1)} %constant_dynamic-slice_fusion), channel_id=1, source_target_pairs={{256,320},{260,324},{264,328},{268,332},{272,336},{276,340},{280,3... | collective-permute-start | bytes 3096584 | tf_op jit(solution)/shard_map/ppermute | solution.py:316
  64.8 1.2 slice.20
  68.9 4.6 %collective-permute-start.10 = (bf16[192,896]{1,0:T(8,128)(2,1)}, bf16[192,896]{1,0:T(8,128)(2,1)S(1)}, u32[]{:S(2)}, u32[]{:S(2)}) collective-permute-start(bf16[192,896]{1,0:T(8,128)(2,1)} %collective-permute-done.2.refs_0_.refs_3_), channel_id=1, source_target_pairs={{256,257},{257,258},{258,259},{259,256},{260,261},{261,262},{262,2... | collective-permute-start | bytes 1032200 | tf_op jit(solution)/shard_map/ppermute | solution.py:319
  74.6 1.6 collective-permute-start.7
  76.2 8.8 %collective-permute-done.17.refs_11_ = bf16[448,1152]{1,0:T(8,128)(2,1)} collective-permute-done((bf16[448,1152]{1,0:T(8,128)(2,1)}, bf16[448,1152]{1,0:T(8,128)(2,1)}, u32[]{:S(2)}, u32[]{:S(2)}) %collective-permute-start.17) | collective-permute-done | bytes 1032224 | tf_op jit(solution)/shard_map/ppermute | solution.py:316
  85.0 1.1 slice.22
  86.1 5.6 %collective-permute-start.20 = (bf16[224,1152]{1,0:T(8,128)(2,1)S(1)}, bf16[224,1152]{1,0:T(8,128)(2,1)S(1)}, u32[]{:S(2)}, u32[]{:S(2)}) collective-permute-start(bf16[224,1152]{1,0:T(8,128)(2,1)S(1)} %slice.22), channel_id=1, source_target_pairs={{256,448},{260,452},{264,456},{268,460},{272,464},{276,468},{280,4... | collective-permute-start | bytes 1548296 | tf_op jit(solution)/shard_map/ppermute | solution.py:316
  91.8 1.9 %collective-permute-start.19 = (bf16[224,1152]{1,0:T(8,128)(2,1)S(1)}, bf16[224,1152]{1,0:T(8,128)(2,1)S(1)}, u32[]{:S(2)}, u32[]{:S(2)}) collective-permute-start(bf16[224,1152]{1,0:T(8,128)(2,1)S(1)} %slice.21), channel_id=1, source_target_pairs={{256,320},{260,324},{264,328},{268,332},{272,336},{276,340},{280,3... | collective-permute-start | bytes 1548296 | tf_op jit(solution)/shard_map/ppermute | solution.py:316
  95.3 12.4 %collective-permute-done.19 = bf16[224,1152]{1,0:T(8,128)(2,1)S(1)} collective-permute-done((bf16[224,1152]{1,0:T(8,128)(2,1)S(1)}, bf16[224,1152]{1,0:T(8,128)(2,1)S(1)}, u32[]{:S(2)}, u32[]{:S(2)}) %collective-permute-start.19) | collective-permute-done | bytes 516128 | tf_op jit(solution)/shard_map/ppermute | solution.py:316
  107.7 1.9 %collective-permute-start.18 = (bf16[448,1152]{1,0:T(8,128)(2,1)}, bf16[448,1152]{1,0:T(8,128)(2,1)}, u32[]{:S(2)}, u32[]{:S(2)}) collective-permute-start(bf16[448,1152]{1,0:T(8,128)(2,1)} %collective-permute-done.17.refs_11_), channel_id=1, source_target_pairs={{256,260},{260,256},{264,268},{268,264},{272,276},{276,272},{280,2... | collective-permute-start | bytes 3096584 | tf_op jit(solution)/shard_map/ppermute | solution.py:316
  110.5 2.4 %collective-permute-start.16 = (bf16[448,1152]{1,0:T(8,128)(2,1)S(1)}, bf16[448,1152]{1,0:T(8,128)(2,1)}, u32[]{:S(2)}, u32[]{:S(2)}) collective-permute-start(bf16[448,1152]{1,0:T(8,128)(2,1)S(1)} %collective-permute-done.15.refs_9_), channel_id=1, source_target_pairs={{256,260},{260,256},{264,268},{268,264},{272,276},{276,272},{280,2... | collective-permute-start | bytes 3096584 | tf_op jit(solution)/shard_map/ppermute | solution.py:316
  113.7 1.9 %collective-permute-start.21 = (bf16[448,1152]{1,0:T(8,128)(2,1)}, bf16[448,1152]{1,0:T(8,128)(2,1)}, u32[]{:S(2)}, u32[]{:S(2)}) collective-permute-start(bf16[448,1152]{1,0:T(8,128)(2,1)} %constant_dynamic-update-slice_fusion.refs_13_), channel_id=1, source_target_pairs={{256,260},{260,256},{264,268},{268,264},{272,276},{276,272},{280,2... | collective-permute-start | bytes 3096584 | tf_op jit(solution)/shard_map/ppermute | solution.py:316
  119.4 1.2 copy-done.7
  121.7 2.1 %tokens_part.1 = bf16[192,896]{1,0:T(8,128)(2,1)S(1)} custom-call(s32[8]{0:T(128)S(1)} %stack.63.at_ref, bf16[320,896]{1,0:T(8,128)(2,1)S(1)} %reshape.24.refs_0_, bf16[160,896]{1,0:T(8,128)(2,1)S(1)} %copy-done.5, bf16[160,896]{1,0:T(8,128)(2,1)S(1)} %copy-done.3, bf16[160,896]{1,0:T(8,128)(2,1)S(1)} %copy-done.1, ...), custom_call_target="tpu_custom_call" | custom-call | flops 440401920 | bytes 8000000 | tf_op jit(solution)/shard_map/tokens_part/pallas_call | solution.py:286
  123.8 1.4 collective-permute-start.12
  125.2 1.3 collective-permute-start.11
  126.8 9.5 %collective-permute-done.12.refs_5_ = bf16[192,896]{1,0:T(8,128)(2,1)S(1)} collective-permute-done((bf16[192,896]{1,0:T(8,128)(2,1)S(1)}, bf16[192,896]{1,0:T(8,128)(2,1)S(1)}, u32[]{:S(2)}, u32[]{:S(2)}) %collective-permute-start.12) | collective-permute-done | bytes 344096 | tf_op jit(solution)/shard_map/ppermute | solution.py:365
  136.3 6.9 %collective-permute-start.13 = (bf16[192,896]{1,0:T(8,128)(2,1)S(1)}, bf16[192,896]{1,0:T(8,128)(2,1)S(1)}, u32[]{:S(2)}, u32[]{:S(2)}) collective-permute-start(bf16[192,896]{1,0:T(8,128)(2,1)S(1)} %collective-permute-done.12.refs_5_), channel_id=1, source_target_pairs={{256,259},{257,256},{258,257},{259,258},{260,263},{261,260},{262,2... | collective-permute-start | bytes 1032200 | tf_op jit(solution)/shard_map/ppermute | solution.py:366
  143.2 2.1 %collective-permute-start.14 = (bf16[192,896]{1,0:T(8,128)(2,1)S(1)}, bf16[192,896]{1,0:T(8,128)(2,1)S(1)}, u32[]{:S(2)}, u32[]{:S(2)}) collective-permute-start(bf16[192,896]{1,0:T(8,128)(2,1)S(1)} %collective-permute-done.11.refs_4_), channel_id=1, source_target_pairs={{256,257},{257,258},{258,259},{259,256},{260,261},{261,262},{262,2... | collective-permute-start | bytes 1032200 | tf_op jit(solution)/shard_map/ppermute | solution.py:367
  146.2 4.1 %collective-permute-done.13.refs_6_ = bf16[192,896]{1,0:T(8,128)(2,1)S(1)} collective-permute-done((bf16[192,896]{1,0:T(8,128)(2,1)S(1)}, bf16[192,896]{1,0:T(8,128)(2,1)S(1)}, u32[]{:S(2)}, u32[]{:S(2)}) %collective-permute-start.13) | collective-permute-done | bytes 344096 | tf_op jit(solution)/shard_map/ppermute | solution.py:366
  150.3 6.2 %collective-permute-done.14.refs_7_ = bf16[192,896]{1,0:T(8,128)(2,1)S(1)} collective-permute-done((bf16[192,896]{1,0:T(8,128)(2,1)S(1)}, bf16[192,896]{1,0:T(8,128)(2,1)S(1)}, u32[]{:S(2)}, u32[]{:S(2)}) %collective-permute-start.14) | collective-permute-done | bytes 344096 | tf_op jit(solution)/shard_map/ppermute | solution.py:367
  156.6 8.9 %decode.1 = bf16[192,896]{1,0:T(8,128)(2,1)S(1)} custom-call(s32[9]{0:T(128)S(1)} %stack.72.order_ref, bf16[192,896]{1,0:T(8,128)(2,1)S(1)} %copy-done.10, bf16[192,896]{1,0:T(8,128)(2,1)S(1)} %copy-done.12, bf16[192,896]{1,0:T(8,128)(2,1)S(1)} %collective-permute-done.10.refs_8_.refs_2_, bf16[192,896]{1,0:T(8,128)(2,1)} %collective-permute-done.2.refs_0_.refs_3_, ...), custom_call_target="tpu_custom_call" | custom-call | flops 1585446912 | bytes 9633792 | tf_op jit(solution)/shard_map/decode/pallas_call | solution.py:112
  (79 shorter events, 16.0 us)
Async XLA Ops:
  6.5 48.8 %all-gather.2.cloned.1.call-start = ((), (), s32[]{:S(2)}) async-start(), calls=%async_computation | async-start | bytes 2193408 | tf_op jit(solution)/shard_map/all_gather | solution.py:315
  8.2 21.6 %collective-permute-start.2 = (bf16[192,896]{1,0:T(8,128)(2,1)}, bf16[192,896]{1,0:T(8,128)(2,1)}, u32[]{:S(2)}, u32[]{:S(2)}) collective-permute-start(bf16[192,896]{1,0:T(8,128)(2,1)} %refs_0_.1), channel_id=1, source_target_pairs={{256,257},{257,258},{258,259},{259,256},{260,261},{261,262},{262,2... | collective-permute-start | bytes 1032200 | tf_op jit(solution)/shard_map/ppermute | solution.py:317
  14.3 15.5 %collective-permute-start.3 = (bf16[192,896]{1,0:T(8,128)(2,1)}, bf16[192,896]{1,0:T(8,128)(2,1)S(1)}, u32[]{:S(2)}, u32[]{:S(2)}) collective-permute-start(bf16[192,896]{1,0:T(8,128)(2,1)} %refs_0_.1), channel_id=1, source_target_pairs={{256,259},{257,256},{258,257},{259,258},{260,263},{261,260},{262,2... | collective-permute-start | bytes 1032200 | tf_op jit(solution)/shard_map/ppermute | solution.py:318
  24.5 5.3 %copy-start.15 = (bf16[320,1280]{1,0:T(8,128)(2,1)S(1)}, bf16[320,1280]{1,0:T(8,128)(2,1)}, u32[]{:S(2)}) copy-start(bf16[320,1280]{1,0:T(8,128)(2,1)} %pw_ref.1) | copy-start | bytes 2457604
  24.5 5.3 %copy-start.16 = (f32[31,320]{1,0:T(8,128)S(1)}, f32[31,320]{1,0:T(8,128)}, u32[]{:S(2)}) copy-start(f32[31,320]{1,0:T(8,128)} %taps_ref.1) | copy-start | bytes 119044
  28.3 7.0 %copy-start.6 = (f32[192,1280]{1,0:T(8,128)}, f32[192,1280]{1,0:T(8,128)S(1)}, u32[]{:S(2)}) copy-start(f32[192,1280]{1,0:T(8,128)S(1)} %get-tuple-element.11.refs_5_) | copy-start | bytes 2949124
  28.4 1.3 collective-permute-start.1
  29.0 0.7 collective-permute-start
  29.7 5.6 %copy-start.11 = (bf16[192,896]{1,0:T(8,128)(2,1)}, bf16[192,896]{1,0:T(8,128)(2,1)S(1)}, u32[]{:S(2)}) copy-start(bf16[192,896]{1,0:T(8,128)(2,1)S(1)} %collective-permute-done.3.refs_1_) | copy-start | bytes 1032196
  57.6 27.4 %collective-permute-start.17 = (bf16[448,1152]{1,0:T(8,128)(2,1)}, bf16[448,1152]{1,0:T(8,128)(2,1)}, u32[]{:S(2)}, u32[]{:S(2)}) collective-permute-start(bf16[448,1152]{1,0:T(8,128)(2,1)} %constant_dynamic-slice_fusion), channel_id=1, source_target_pairs={{256,448},{260,452},{264,456},{268,460},{272,464},{276,468},{280,4... | collective-permute-start | bytes 3096584 | tf_op jit(solution)/shard_map/ppermute | solution.py:316
  62.2 29.5 %collective-permute-start.15 = (bf16[448,1152]{1,0:T(8,128)(2,1)}, bf16[448,1152]{1,0:T(8,128)(2,1)S(1)}, u32[]{:S(2)}, u32[]{:S(2)}) collective-permute-start(bf16[448,1152]{1,0:T(8,128)(2,1)} %constant_dynamic-slice_fusion), channel_id=1, source_target_pairs={{256,320},{260,324},{264,328},{268,332},{272,336},{276,340},{280,3... | collective-permute-start | bytes 3096584 | tf_op jit(solution)/shard_map/ppermute | solution.py:316
  66.1 2.1 %collective-permute-start.6 = (bf16[160,896]{1,0:T(8,128)(2,1)S(1)}, bf16[160,896]{1,0:T(8,128)(2,1)S(1)}, u32[]{:S(2)}, u32[]{:S(2)}) collective-permute-start(bf16[160,896]{1,0:T(8,128)(2,1)S(1)} %constant_dynamic-slice_fusion.1), channel_id=1, source_target_pairs={{0,128},{4,132},{8,136},{12,140},{16,144},{20,148},{24,152},{28,15... | collective-permute-start | bytes 860168 | tf_op jit(solution)/shard_map/ppermute | solution.py:316
  66.8 26.9 %collective-permute-start.8 = (bf16[192,1280]{1,0:T(8,128)(2,1)S(1)}, bf16[192,1280]{1,0:T(8,128)(2,1)S(1)}, u32[]{:S(2)}, u32[]{:S(2)}) collective-permute-start(bf16[192,1280]{1,0:T(8,128)(2,1)S(1)} %get-tuple-element.12), channel_id=1, source_target_pairs={{0,1},{1,0},{2,3},{3,2},{4,5},{5,4},{6,7},{7,6},{8,9},{9,8},{10,11... | collective-permute-start | bytes 1474568 | tf_op jit(solution)/shard_map/ppermute | solution.py:350
  67.5 1.4 collective-permute-start.5
  68.2 23.6 %copy-start = (bf16[160,896]{1,0:T(8,128)(2,1)}, bf16[160,896]{1,0:T(8,128)(2,1)S(1)}, u32[]{:S(2)}) copy-start(bf16[160,896]{1,0:T(8,128)(2,1)S(1)} %collective-permute-done.6.refs_3_) | copy-start | bytes 860164
  68.2 5.3 %collective-permute-start.4 = (bf16[160,896]{1,0:T(8,128)(2,1)S(1)}, bf16[160,896]{1,0:T(8,128)(2,1)S(1)}, u32[]{:S(2)}, u32[]{:S(2)}) collective-permute-start(bf16[160,896]{1,0:T(8,128)(2,1)S(1)} %constant_dynamic-slice_fusion.1), channel_id=1, source_target_pairs={{0,64},{4,68},{8,72},{12,76},{16,80},{20,84},{24,88},{28,92},{32,9... | collective-permute-start | bytes 860168 | tf_op jit(solution)/shard_map/ppermute | solution.py:316
  68.9 22.9 %copy-start.2 = (bf16[160,896]{1,0:T(8,128)(2,1)}, bf16[160,896]{1,0:T(8,128)(2,1)S(1)}, u32[]{:S(2)}) copy-start(bf16[160,896]{1,0:T(8,128)(2,1)S(1)} %collective-permute-done.5.refs_2_) | copy-start | bytes 860164
  68.9 44.8 %collective-permute-start.10 = (bf16[192,896]{1,0:T(8,128)(2,1)}, bf16[192,896]{1,0:T(8,128)(2,1)S(1)}, u32[]{:S(2)}, u32[]{:S(2)}) collective-permute-start(bf16[192,896]{1,0:T(8,128)(2,1)} %collective-permute-done.2.refs_0_.refs_3_), channel_id=1, source_target_pairs={{256,257},{257,258},{258,259},{259,256},{260,261},{261,262},{262,2... | collective-permute-start | bytes 1032200 | tf_op jit(solution)/shard_map/ppermute | solution.py:319
  73.6 18.2 %copy-start.4 = (bf16[160,896]{1,0:T(8,128)(2,1)}, bf16[160,896]{1,0:T(8,128)(2,1)S(1)}, u32[]{:S(2)}) copy-start(bf16[160,896]{1,0:T(8,128)(2,1)S(1)} %collective-permute-done.4.refs_1_) | copy-start | bytes 860164
  74.6 42.0 %collective-permute-start.7 = (bf16[480,896]{1,0:T(8,128)(2,1)}, bf16[480,896]{1,0:T(8,128)(2,1)}, u32[]{:S(2)}, u32[]{:S(2)}) collective-permute-start(bf16[480,896]{1,0:T(8,128)(2,1)} %pad_maximum_fusion), channel_id=1, source_target_pairs={{0,4},{4,0},{8,12},{12,8},{16,20},{20,16},{24,28},{28,24},{32,36},... | collective-permute-start | bytes 2580488 | tf_op jit(solution)/shard_map/ppermute | solution.py:316
  86.1 24.4 %collective-permute-start.20 = (bf16[224,1152]{1,0:T(8,128)(2,1)S(1)}, bf16[224,1152]{1,0:T(8,128)(2,1)S(1)}, u32[]{:S(2)}, u32[]{:S(2)}) collective-permute-start(bf16[224,1152]{1,0:T(8,128)(2,1)S(1)} %slice.22), channel_id=1, source_target_pairs={{256,448},{260,452},{264,456},{268,460},{272,464},{276,468},{280,4... | collective-permute-start | bytes 1548296 | tf_op jit(solution)/shard_map/ppermute | solution.py:316
  91.8 15.9 %collective-permute-start.19 = (bf16[224,1152]{1,0:T(8,128)(2,1)S(1)}, bf16[224,1152]{1,0:T(8,128)(2,1)S(1)}, u32[]{:S(2)}, u32[]{:S(2)}) collective-permute-start(bf16[224,1152]{1,0:T(8,128)(2,1)S(1)} %slice.21), channel_id=1, source_target_pairs={{256,320},{260,324},{264,328},{268,332},{272,336},{276,340},{280,3... | collective-permute-start | bytes 1548296 | tf_op jit(solution)/shard_map/ppermute | solution.py:316
  94.6 21.1 %collective-permute-start.9 = (bf16[192,1280]{1,0:T(8,128)(2,1)}, bf16[192,1280]{1,0:T(8,128)(2,1)S(1)}, u32[]{:S(2)}, u32[]{:S(2)}) collective-permute-start(bf16[192,1280]{1,0:T(8,128)(2,1)} %get-tuple-element.13), channel_id=1, source_target_pairs={{1,2},{2,1},{3,0},{0,3},{5,6},{6,5},{7,4},{4,7},{9,10},{10,9},{11,... | collective-permute-start | bytes 1474568 | tf_op jit(solution)/shard_map/ppermute | solution.py:353
  107.7 48.9 %collective-permute-start.18 = (bf16[448,1152]{1,0:T(8,128)(2,1)}, bf16[448,1152]{1,0:T(8,128)(2,1)}, u32[]{:S(2)}, u32[]{:S(2)}) collective-permute-start(bf16[448,1152]{1,0:T(8,128)(2,1)} %collective-permute-done.17.refs_11_), channel_id=1, source_target_pairs={{256,260},{260,256},{264,268},{268,264},{272,276},{276,272},{280,2... | collective-permute-start | bytes 3096584 | tf_op jit(solution)/shard_map/ppermute | solution.py:316
  110.5 46.1 %collective-permute-start.16 = (bf16[448,1152]{1,0:T(8,128)(2,1)S(1)}, bf16[448,1152]{1,0:T(8,128)(2,1)}, u32[]{:S(2)}, u32[]{:S(2)}) collective-permute-start(bf16[448,1152]{1,0:T(8,128)(2,1)S(1)} %collective-permute-done.15.refs_9_), channel_id=1, source_target_pairs={{256,260},{260,256},{264,268},{268,264},{272,276},{276,272},{280,2... | collective-permute-start | bytes 3096584 | tf_op jit(solution)/shard_map/ppermute | solution.py:316
  113.7 42.9 %collective-permute-start.21 = (bf16[448,1152]{1,0:T(8,128)(2,1)}, bf16[448,1152]{1,0:T(8,128)(2,1)}, u32[]{:S(2)}, u32[]{:S(2)}) collective-permute-start(bf16[448,1152]{1,0:T(8,128)(2,1)} %constant_dynamic-update-slice_fusion.refs_13_), channel_id=1, source_target_pairs={{256,260},{260,256},{264,268},{268,264},{272,276},{276,272},{280,2... | collective-permute-start | bytes 3096584 | tf_op jit(solution)/shard_map/ppermute | solution.py:316
  123.8 32.8 %copy-start.10 = (bf16[192,896]{1,0:T(8,128)(2,1)S(1)}, bf16[192,896]{1,0:T(8,128)(2,1)}, u32[]{:S(2)}) copy-start(bf16[192,896]{1,0:T(8,128)(2,1)} %refs_0_.1) | copy-start | bytes 1032196
  123.8 32.8 %copy-start.12 = (bf16[192,896]{1,0:T(8,128)(2,1)S(1)}, bf16[192,896]{1,0:T(8,128)(2,1)}, u32[]{:S(2)}) copy-start(bf16[192,896]{1,0:T(8,128)(2,1)} %copy-done.11) | copy-start | bytes 1032196
  123.8 12.5 %collective-permute-start.12 = (bf16[192,896]{1,0:T(8,128)(2,1)S(1)}, bf16[192,896]{1,0:T(8,128)(2,1)S(1)}, u32[]{:S(2)}, u32[]{:S(2)}) collective-permute-start(bf16[192,896]{1,0:T(8,128)(2,1)S(1)} %tokens_part.1), channel_id=1, source_target_pairs={{0,259},{1,256},{2,257},{3,258},{4,263},{5,260},{6,261},{7,262},{8... | collective-permute-start | bytes 1032200 | tf_op jit(solution)/shard_map/ppermute | solution.py:365
  125.2 17.9 %collective-permute-start.11 = (bf16[192,896]{1,0:T(8,128)(2,1)S(1)}, bf16[192,896]{1,0:T(8,128)(2,1)S(1)}, u32[]{:S(2)}, u32[]{:S(2)}) collective-permute-start(bf16[192,896]{1,0:T(8,128)(2,1)S(1)} %tokens_part.1), channel_id=1, source_target_pairs={{0,256},{1,257},{2,258},{3,259},{4,260},{5,261},{6,262},{7,263},{8... | collective-permute-start | bytes 1032200 | tf_op jit(solution)/shard_map/ppermute | solution.py:364
  136.3 14.1 %collective-permute-start.13 = (bf16[192,896]{1,0:T(8,128)(2,1)S(1)}, bf16[192,896]{1,0:T(8,128)(2,1)S(1)}, u32[]{:S(2)}, u32[]{:S(2)}) collective-permute-start(bf16[192,896]{1,0:T(8,128)(2,1)S(1)} %collective-permute-done.12.refs_5_), channel_id=1, source_target_pairs={{256,259},{257,256},{258,257},{259,258},{260,263},{261,260},{262,2... | collective-permute-start | bytes 1032200 | tf_op jit(solution)/shard_map/ppermute | solution.py:366
  143.2 13.4 %collective-permute-start.14 = (bf16[192,896]{1,0:T(8,128)(2,1)S(1)}, bf16[192,896]{1,0:T(8,128)(2,1)S(1)}, u32[]{:S(2)}, u32[]{:S(2)}) collective-permute-start(bf16[192,896]{1,0:T(8,128)(2,1)S(1)} %collective-permute-done.11.refs_4_), channel_id=1, source_target_pairs={{256,257},{257,258},{258,259},{259,256},{260,261},{261,262},{262,2... | collective-permute-start | bytes 1032200 | tf_op jit(solution)/shard_map/ppermute | solution.py:367
  (10 other events, 18.7 us)
Sparse Core Ops, SparseCore 0:
  9.5 45.8 all-gather.1

commit v5 on v3

--- a/solution.py
+++ b/solution.py
@@ -10,11 +10,10 @@
 HEADS = 28
 KV = 4
 HEAD = 128
-VMEM = 48 * 1024 * 1024
+MIB = 1024 * 1024
+LOG2E = 1.4426950408889634
 NX = 4
 NY = 8
-ADAPT_SLOT = 48
-ADAPT_COLS = 896
 
 
 def rotary_tables(count):
@@ -29,38 +28,60 @@
     return values * cosine + pltpu.roll(values, HEAD // 2, 1) * sine
 
 
-def decode_kernel(order_ref, *refs, parts):
-    words, sounds = refs[:parts], refs[parts : 2 * parts]
-    gain_ref, w_ref, bias_ref, cos_ref, sin_ref, out_ref, acc, acc_kv, square, square_kv = refs[2 * parts :]
+def prepare_kernel(order_ref, *refs, parts):
+    ins = refs[: 2 * parts]
+    gain_ref, rows_ref, scale_ref = refs[2 * parts : 2 * parts + 3]
+    count = ins[0].shape[0]
+    for first, blocks in ((0, ins[:parts]), (count, ins[parts:])):
+        square = jnp.zeros((count, 1), jnp.float32)
+        for i, ref in enumerate(blocks):
+            block = order_ref[i]
+            x = ref[...].astype(jnp.float32)
+            square = square + jnp.sum(x * x, axis=1, keepdims=True)
+            rows_ref[block, first : first + count] = (x * gain_ref[block]).astype(jnp.bfloat16)
+        scale_ref[first : first + count] = lax.rsqrt(square / (parts * ins[0].shape[1]) + 1e-6)
+
+
+def prepare(order, words, sounds, gain):
+    parts = len(words)
+    count, width = words[0].shape
+    vmem = pl.BlockSpec(memory_space=pltpu.VMEM)
+    return pl.pallas_call(
+        functools.partial(prepare_kernel, parts=parts),
+        in_specs=[pl.BlockSpec(memory_space=pltpu.SMEM)] + [vmem] * (2 * parts + 1),
+        out_specs=[vmem, vmem],
+        out_shape=[
+            jax.ShapeDtypeStruct((parts, 2 * count, width), jnp.bfloat16),
+            jax.ShapeDtypeStruct((2 * count, 1), jnp.float32),
+        ],
+        compiler_params=pltpu.CompilerParams(vmem_limit_bytes=16 * MIB),
+        cost_estimate=pl.CostEstimate(
+            flops=8 * count * parts * width, bytes_accessed=8 * count * parts * width, transcendentals=0
+        ),
+        name="prepare",
+    )(order, *words, *sounds, gain)
+
+
+def decode_kernel(rows_ref, scale_ref, w_ref, bias_ref, cos_ref, sin_ref, out_ref, acc, acc_kv):
     step = pl.program_id(0)
     count, total = acc.shape
     heads = total // HEAD - 2
+    text = jnp.dot(rows_ref[0, :count], w_ref[...], preferred_element_type=jnp.float32)
+    audio = jnp.dot(rows_ref[0, count:], w_ref[:, heads * HEAD :], preferred_element_type=jnp.float32)
 
     @pl.when(step == 0)
     def _():
-        for ref in (acc, acc_kv, square, square_kv):
-            ref[...] = jnp.zeros_like(ref)
-
-    for i in range(parts):
-
-        @pl.when(step == i)
-        def _():
-            x = words[i][...].astype(jnp.float32)
-            square[...] += jnp.sum(x * x, axis=1, keepdims=True)
-            acc[...] += jnp.dot(
-                (x * gain_ref[0]).astype(jnp.bfloat16), w_ref[...], preferred_element_type=jnp.float32
-            )
-            x = sounds[i][...].astype(jnp.float32)
-            square_kv[...] += jnp.sum(x * x, axis=1, keepdims=True)
-            acc_kv[...] += jnp.dot(
-                (x * gain_ref[0]).astype(jnp.bfloat16), w_ref[:, heads * HEAD :], preferred_element_type=jnp.float32
-            )
+        acc[...] = text
+        acc_kv[...] = audio
+
+    @pl.when(step > 0)
+    def _():
+        acc[...] += text
+        acc_kv[...] += audio
 
     @pl.when(step == pl.num_programs(0) - 1)
     def _():
-        width = parts * words[0].shape[1]
-        scale = lax.rsqrt(square[...] / width + 1e-6)
-        scale_kv = lax.rsqrt(square_kv[...] / width + 1e-6)
+        scale, scale_kv = scale_ref[:count], scale_ref[count:]
         cosine, sine = cos_ref[count:], sin_ref[count:]
         key_cols = slice(heads * HEAD, (heads + 1) * HEAD)
         value_cols = slice((heads + 1) * HEAD, total)
@@ -83,52 +104,45 @@
         allowed = col <= row + count
         for h in range(heads):
             cols = slice(h * HEAD, (h + 1) * HEAD)
-            query = turned(acc[:, cols] * scale + bias_ref[:, cols], cosine, sine).astype(jnp.bfloat16)
-            scores = lax.dot_general(
-                query, keys, (((1,), (1,)), ((), ())), preferred_element_type=jnp.float32
-            ) * (HEAD**-0.5)
+            query = turned(acc[:, cols] * scale + bias_ref[:, cols], cosine, sine) * (LOG2E * HEAD**-0.5)
+            scores = dot_t(query.astype(jnp.bfloat16), keys)
             scores = jnp.where(allowed, scores, -1e30)
-            weights = jnp.exp(scores - jnp.max(scores, axis=1, keepdims=True))
+            weights = jnp.exp2(scores - jnp.max(scores, axis=1, keepdims=True))
             probs = weights * (1.0 / jnp.sum(weights, axis=1, keepdims=True))
             out_ref[:, cols] = jnp.dot(
                 probs.astype(jnp.bfloat16), values, preferred_element_type=jnp.float32
             ).astype(jnp.bfloat16)
 
 
-def decode(order, words, sounds, gain, weight, bias, tables):
-    parts = len(words)
-    count, width = words[0].shape
+def decode(rows, scale, weight, bias, tables):
+    parts, count, width = rows.shape
+    count //= 2
     total = weight.shape[1]
     columns = total - 2 * HEAD
-    whole = lambda *shape: pl.BlockSpec(shape, lambda k, o: (0,) * len(shape))
-    return pl.pallas_call(
-        functools.partial(decode_kernel, parts=parts),
-        grid_spec=pltpu.PrefetchScalarGridSpec(
-            num_scalar_prefetch=1,
-            grid=(parts,),
-            in_specs=[whole(count, width)] * (2 * parts)
-            + [
-                pl.BlockSpec((1, 1, width), lambda k, o: (o[k], 0, 0)),
-                pl.BlockSpec((width, total), lambda k, o: (o[k], 0)),
-                whole(1, total),
-                whole(2 * count, HEAD),
-                whole(2 * count, HEAD),
-            ],
-            out_specs=whole(count, columns),
-            scratch_shapes=[
-                pltpu.VMEM((count, total), jnp.float32),
-                pltpu.VMEM((count, 2 * HEAD), jnp.float32),
-                pltpu.VMEM((count, 1), jnp.float32),
-                pltpu.VMEM((count, 1), jnp.float32),
-            ],
-        ),
+    whole = lambda *shape: pl.BlockSpec(shape, lambda k: (0,) * len(shape))
+    return pl.pallas_call(
+        decode_kernel,
+        grid=(parts,),
+        in_specs=[
+            pl.BlockSpec((1, 2 * count, width), lambda k: (k, 0, 0)),
+            whole(2 * count, 1),
+            pl.BlockSpec((width, total), lambda k: (k, 0)),
+            whole(1, total),
+            whole(2 * count, HEAD),
+            whole(2 * count, HEAD),
+        ],
+        out_specs=whole(count, columns),
+        scratch_shapes=[
+            pltpu.VMEM((count, total), jnp.float32),
+            pltpu.VMEM((count, 2 * HEAD), jnp.float32),
+        ],
         out_shape=jax.ShapeDtypeStruct((count, columns), jnp.bfloat16),
-        compiler_params=pltpu.CompilerParams(vmem_limit_bytes=VMEM),
+        compiler_params=pltpu.CompilerParams(vmem_limit_bytes=56 * MIB),
         cost_estimate=pl.CostEstimate(
             flops=2 * count * parts * width * total, bytes_accessed=2 * parts * width * (total + count), transcendentals=0
         ),
         name="decode",
-    )(order, *words, *sounds, gain, weight, bias, *tables)
+    )(rows, scale, weight, bias, *tables)
 
 
 def pooling(rows):
@@ -176,7 +190,7 @@
             jax.ShapeDtypeStruct((frames, columns), jnp.bfloat16),
             jax.ShapeDtypeStruct((frames // 4, width), jnp.float32),
         ],
-        compiler_params=pltpu.CompilerParams(vmem_limit_bytes=VMEM),
+        compiler_params=pltpu.CompilerParams(vmem_limit_bytes=20 * MIB),
         cost_estimate=pl.CostEstimate(
             flops=4 * frames * width * columns, bytes_accessed=2 * frames * width * 4, transcendentals=frames * columns
         ),
@@ -230,7 +244,7 @@
             pltpu.VMEM((frames + 2 * EDGE, columns), jnp.float32),
             pltpu.VMEM((frames, columns), jnp.bfloat16),
         ],
-        compiler_params=pltpu.CompilerParams(vmem_limit_bytes=VMEM),
+        compiler_params=pltpu.CompilerParams(vmem_limit_bytes=12 * MIB),
         cost_estimate=pl.CostEstimate(
             flops=5_000_000_000, bytes_accessed=2 * frames * columns * 4, transcendentals=frames * columns
         ),
@@ -257,9 +271,10 @@
 
 def spread(block):
     send = lambda v, dx, dy: lax.ppermute(v, ("grp", "seq"), of_group(0, place(dx, dy)))
+    rows = block.shape[0]
     near = jnp.concatenate([send(block, 0, 1), block, send(block, 0, -1)], axis=0)
-    line = jnp.concatenate([near, send(near, 0, 3), send(near[:2], 0, -3)], axis=0)
-    steps = [-1, 0, 1, -4, -3, -2, 2, 3]
+    line = jnp.concatenate([near, send(near, 0, -3), send(near[rows:], 0, 3)], axis=0)
+    steps = [-1, 0, 1, 2, 3, 4, -3, -2]
     return [(0, steps, line)] + [(dx, steps, send(line, -dx, 0)) for dx in (-1, 1, 2)]
 
 
@@ -269,8 +284,8 @@
     out_ref, weight = refs[-2:]
     at = 0
     for ref, count in zip(pieces, counts, strict=True):
-        weight[at : at + count * ADAPT_SLOT] = ref[...].reshape(count * ADAPT_SLOT, ADAPT_COLS)
-        at += count * ADAPT_SLOT
+        weight[at : at + count] = ref[...]
+        at += count
     pooled = (audio_ref[...] + term_ref[...] + other_ref[...].astype(jnp.float32)).astype(jnp.bfloat16)
     ordered = jnp.dot(pooled, expand_ref[...], preferred_element_type=jnp.float32).astype(jnp.bfloat16)
     out_ref[...] = jnp.dot(ordered, weight[...], preferred_element_type=jnp.float32).astype(out_ref.dtype)
@@ -279,19 +294,17 @@
 def tokens_part(pieces, pooled_audio, term, other, expand, *after_these):
     counts = [p.shape[0] for p in pieces]
     count = pooled_audio.shape[0]
-    whole = lambda *shape: pl.BlockSpec(shape, lambda k: (0,) * len(shape))
+    columns = pieces[0].shape[1]
+    vmem = pl.BlockSpec(memory_space=pltpu.VMEM)
     return pl.pallas_call(
         functools.partial(tokens_kernel, counts=counts),
-        grid=(1,),
-        in_specs=[whole(n, ADAPT_SLOT, ADAPT_COLS) for n in counts]
-        + [whole(*v.shape) for v in (pooled_audio, term, other, expand)]
-        + [pl.BlockSpec(memory_space=pl.ANY)] * len(after_these),
-        out_specs=whole(count, ADAPT_COLS),
-        out_shape=jax.ShapeDtypeStruct((count, ADAPT_COLS), jnp.bfloat16),
-        scratch_shapes=[pltpu.VMEM((sum(counts) * ADAPT_SLOT, ADAPT_COLS), jnp.bfloat16)],
-        compiler_params=pltpu.CompilerParams(vmem_limit_bytes=VMEM),
-        cost_estimate=pl.CostEstimate(
-            flops=2 * count * sum(counts) * ADAPT_SLOT * (ADAPT_COLS + expand.shape[0]), bytes_accessed=8000000, transcendentals=0
+        in_specs=[vmem] * (len(pieces) + 4) + [pl.BlockSpec(memory_space=pl.ANY)] * len(after_these),
+        out_specs=vmem,
+        out_shape=jax.ShapeDtypeStruct((count, columns), jnp.bfloat16),
+        scratch_shapes=[pltpu.VMEM((sum(counts), columns), jnp.bfloat16)],
+        compiler_params=pltpu.CompilerParams(vmem_limit_bytes=20 * MIB),
+        cost_estimate=pl.CostEstimate(
+            flops=4 * count * sum(counts) * columns, bytes_accessed=8000000, transcendentals=0
         ),
         name="tokens_part",
     )(*pieces, pooled_audio, term, other, expand, *after_these)
@@ -310,11 +323,10 @@
     ring = lambda group, k: [(group * n_mdl + i, group * n_mdl + (i + k) % n_mdl) for i in range(n_mdl)]
 
     weight = lax.all_gather(qkv_weight, "seq", axis=0, tiled=True)
-    twin = lax.ppermute(adapt_weight, ("grp", "seq"), of_group(0, SWAP))
-    held = jnp.where(
-        core == 0, jnp.concatenate([adapt_weight, twin]), jnp.concatenate([twin, adapt_weight])
-    )
-    pieces = spread(jnp.pad(held, ((0, ADAPT_SLOT - 2 * rows), (0, 0)))[None])
+    pieces = spread(adapt_weight)
+    swap = lambda v: lax.ppermute(v, ("grp", "seq"), of_group(0, SWAP))
+    adapter = [p for _, _, p in pieces]
+    adapter += [swap(adapter[0]), swap(jnp.concatenate(adapter[1:], axis=0))]
 
     behind = lax.ppermute(text, both, ring(1, 1))
     ahead = lax.ppermute(text, both, ring(1, -1))
@@ -340,10 +352,10 @@
             for dx, steps, _ in pieces
         ]
     )
-    column = jnp.arange(chips.shape[0] * ADAPT_SLOT, dtype=jnp.int32) % ADAPT_SLOT
-    source = jnp.where(column < 2 * rows, jnp.repeat(chips, ADAPT_SLOT) * 2 * rows + column, -1)
+    device = jnp.concatenate([2 * chips + core, 2 * chips + 1 - core])
+    source = (device[:, None] * rows + jnp.arange(rows, dtype=jnp.int32)[None]).reshape(-1)
     expand = (jnp.arange(audio.shape[1], dtype=jnp.int32)[:, None] == source[None]).astype(jnp.bfloat16)
-    tokens = tokens_part([p for _, _, p in pieces], pooled_audio, term, other, expand, second)
+    tokens = tokens_part(adapter, pooled_audio, term, other, expand, second)
 
     tables = rotary_tables(2 * text.shape[0])
     gain = norm_gain.reshape(n_mdl, 1, width)
@@ -353,7 +365,8 @@
     across = lax.ppermute(following, both, ring(1, -1))
     last = lax.ppermute(same, both, ring(1, 1))
     sounds = [same, following, across, last]
-    context = decode(order, words, sounds, gain, weight, qkv_bias[None], tables)
+    prepared, scale = prepare(order, words, sounds, gain)
+    context = decode(prepared, scale, weight, qkv_bias[None], tables)
     return jnp.where(grp == 0, tokens, context)[None]
 
 

time: 166 us -> 147 us (0.89)
  the two profiles are of different devices: /device:TPU:74 before, /device:TPU:122 now
where the time goes in v5:
time: 147 us
  waiting for transfers between devices  59.3 us (40%)
  starting transfers between devices  34.2 us (23%)
  Pallas kernels  22.5 us (15%)
  between operations  14.7 us (10%)
  local copies, waits for them, and re-layouts  9.54 us (6%)
  other arithmetic  6.28 us (4%)
    ppermute x1, waiting for transfers between devices, shards(): lax.ppermute(tokens, both, [(i, n_mdl + (i - 1) % n_mdl) for i in range(n...  44.1 us
    pallas_call x1, Pallas kernels, decode(): pl.pallas_call(decode_kernel, grid=(parts,), in_specs=[pl.BlockSpec((1, 2...  10.3 us
    unnamed x28, local copies, waits for them, and re-layouts  7.48 us
    ppermute x1, waiting for transfers between devices, shards(): second = lax.ppermute(behind, both, ring(1, 1))  7.06 us
    ppermute x1, starting transfers between devices, shards(): behind = lax.ppermute(text, both, ring(1, 1))  6.09 us
    ppermute x1, starting transfers between devices, shards(): ahead = lax.ppermute(text, both, ring(1, -1))  5.87 us
    pallas_call x1, Pallas kernels, conv(): pl.pallas_call(conv_kernel, in_specs=[vmem] * 5 + [pl.BlockSpec(memory_sp...  5.49 us
    ppermute x7, starting transfers between devices, spread(): lax.ppermute(v, ('grp', 'seq'), of_group(0, place(dx, dy)))  4.7 us
  transfers between devices with their start and end apart: 21, of which 4 were waited for; matrix products, arithmetic and copies ran while one was open for 4% of the time, Pallas kernels for 8%

profile of v5, /device:TPU:122, one launch (start us, length us, event | category | flops | bytes accessed | tf_op | source)
XLA Modules:
  0.0 146.6 jit_solution(16927586375709017036)
XLA Ops:
  6.5 0.7 all-gather.2.cloned.1.call-update
  7.3 6.1 %collective-permute-start.11 = (bf16[192,896]{1,0:T(8,128)(2,1)}, bf16[192,896]{1,0:T(8,128)(2,1)S(1)}, u32[]{:S(2)}, u32[]{:S(2)}) collective-permute-start(bf16[192,896]{1,0:T(8,128)(2,1)} %refs_0_.1), channel_id=1, source_target_pairs={{256,257},{257,258},{258,259},{259,256},{260,261},{261,262},{262,2... | collective-permute-start | bytes 1032200 | tf_op jit(solution)/shard_map/ppermute | solution.py:331
  13.4 5.9 %collective-permute-start.12 = (bf16[192,896]{1,0:T(8,128)(2,1)}, bf16[192,896]{1,0:T(8,128)(2,1)S(1)}, u32[]{:S(2)}, u32[]{:S(2)}) collective-permute-start(bf16[192,896]{1,0:T(8,128)(2,1)} %refs_0_.1), channel_id=1, source_target_pairs={{256,259},{257,256},{258,257},{259,258},{260,263},{261,260},{262,2... | collective-permute-start | bytes 1032200 | tf_op jit(solution)/shard_map/ppermute | solution.py:332
  21.2 0.7 broadcast_in_dim.6.gain_ref
  21.9 1.5 %copy-done.7 = bf16[768,1280]{1,0:T(8,128)(2,1)S(1)} copy-done((bf16[768,1280]{1,0:T(8,128)(2,1)S(1)}, bf16[768,1280]{1,0:T(8,128)(2,1)}, u32[]{:S(2)}) %copy-start.7) | copy-done | bytes 1966104
  23.5 1.4 copy-done.8
  24.9 3.8 %gate.1 = (bf16[768,320]{1,0:T(8,128)(2,1)S(1)}, f32[192,1280]{1,0:T(8,128)S(1)}) custom-call(s32[1]{0:T(128)S(6)} %sub.20.count_ref, bf16[768,1280]{1,0:T(8,128)(2,1)S(1)} %copy-done.7, f32[1,1280]{1,0:T(1,128)S(1)} %broadcast_in_dim.6.gain_ref, bf16[2,320,1280]{2,1,0:T(8,128)(2,1)S(1)} %bitcast.36), custom_call_target="tpu_custom_call" | custom-call | flops 1258291200 | bytes 7864320 | tf_op jit(solution)/shard_map/gate/pallas_call | solution.py:176
  32.0 1.2 copy-done.9
  33.2 5.5 %conv.1 = bf16[192,1280]{1,0:T(8,128)(2,1)S(1)} custom-call(bf16[16,320]{1,0:T(8,128)(2,1)S(1)} %collective-permute-done.9.before_ref, bf16[768,320]{1,0:T(8,128)(2,1)S(1)} %get-tuple-element.10.gated_ref, bf16[16,320]{1,0:T(8,128)(2,1)S(1)} %collective-permute-done.10.after_ref, f32[31,320]{1,0:T(8,128)S(1)} %copy-done.10, bf16[320,1280]{1,0:T(8,128)(2,1)S(1)} %copy-done.9, ...), custom_call_target="tpu_custom_call" | custom-call | flops 5000000000 | bytes 1966080 | tf_op jit(solution)/shard_map/conv/pallas_call | solution.py:238
  38.8 1.5 %collective-permute-start.13 = (bf16[192,1280]{1,0:T(8,128)(2,1)S(1)}, bf16[192,1280]{1,0:T(8,128)(2,1)}, u32[]{:S(2)}, u32[]{:S(2)}) collective-permute-start(bf16[192,1280]{1,0:T(8,128)(2,1)S(1)} %conv.1), channel_id=1, source_target_pairs={{0,1},{1,0},{2,3},{3,2},{4,5},{5,4},{6,7},{7,6},{8,9},{9,8},{10,11... | collective-permute-start | bytes 1474568 | tf_op jit(solution)/shard_map/ppermute | solution.py:344
  40.8 0.7 collective-permute-start.4
  43.8 2.5 %collective-permute-start.15 = (bf16[192,896]{1,0:T(8,128)(2,1)S(1)}, bf16[192,896]{1,0:T(8,128)(2,1)S(1)}, u32[]{:S(2)}, u32[]{:S(2)}) collective-permute-start(bf16[192,896]{1,0:T(8,128)(2,1)S(1)} %collective-permute-done.11.refs_0_.refs_3_), channel_id=1, source_target_pairs={{256,257},{257,258},{258,259},{259,256},{260,261},{261,262},{262,2... | collective-permute-start | bytes 1032200 | tf_op jit(solution)/shard_map/ppermute | solution.py:333
  46.4 0.7 collective-permute-start.8
  47.1 1.2 fusion.3
  48.3 0.7 collective-permute-start.14
  49.0 1.4 fusion.refs_9_
  50.4 7.1 %collective-permute-done.15.refs_10_.refs_2_ = bf16[192,896]{1,0:T(8,128)(2,1)S(1)} collective-permute-done((bf16[192,896]{1,0:T(8,128)(2,1)S(1)}, bf16[192,896]{1,0:T(8,128)(2,1)S(1)}, u32[]{:S(2)}, u32[]{:S(2)}) %collective-permute-start.15) | collective-permute-done | bytes 344096 | tf_op jit(solution)/shard_map/ppermute | solution.py:333
  57.5 1.5 %tokens_part.1 = bf16[192,896]{1,0:T(8,128)(2,1)S(1)} custom-call(bf16[160,896]{1,0:T(8,128)(2,1)S(1)} %concatenate.99.refs_0_, bf16[160,896]{1,0:T(8,128)(2,1)S(1)} %collective-permute-done.4.refs_1_, bf16[160,896]{1,0:T(8,128)(2,1)S(1)} %collective-permute-done.5.refs_2_, bf16[160,896]{1,0:T(8,128)(2,1)S(1)} %collective-permute-done.6.refs_3_, ...), custom_call_target="tpu_custom_call" | custom-call | flops 880803840 | bytes 8000000 | tf_op jit(solution)/shard_map/tokens_part/pallas_call | solution.py:299
  59.0 1.3 collective-permute-start.17
  60.3 1.3 collective-permute-start.16
  62.3 44.1 %collective-permute-done.17.refs_5_ = bf16[192,896]{1,0:T(8,128)(2,1)S(1)} collective-permute-done((bf16[192,896]{1,0:T(8,128)(2,1)S(1)}, bf16[192,896]{1,0:T(8,128)(2,1)S(1)}, u32[]{:S(2)}, u32[]{:S(2)}) %collective-permute-start.17) | collective-permute-done | bytes 344096 | tf_op jit(solution)/shard_map/ppermute | solution.py:364
  106.3 3.6 %collective-permute-start.18 = (bf16[192,896]{1,0:T(8,128)(2,1)S(1)}, bf16[192,896]{1,0:T(8,128)(2,1)S(1)}, u32[]{:S(2)}, u32[]{:S(2)}) collective-permute-start(bf16[192,896]{1,0:T(8,128)(2,1)S(1)} %collective-permute-done.17.refs_5_), channel_id=1, source_target_pairs={{256,259},{257,256},{258,257},{259,258},{260,263},{261,260},{262,2... | collective-permute-start | bytes 1032200 | tf_op jit(solution)/shard_map/ppermute | solution.py:365
  110.0 4.0 %collective-permute-start.19 = (bf16[192,896]{1,0:T(8,128)(2,1)S(1)}, bf16[192,896]{1,0:T(8,128)(2,1)S(1)}, u32[]{:S(2)}, u32[]{:S(2)}) collective-permute-start(bf16[192,896]{1,0:T(8,128)(2,1)S(1)} %collective-permute-done.16.refs_4_), channel_id=1, source_target_pairs={{256,257},{257,258},{258,259},{259,256},{260,261},{261,262},{262,2... | collective-permute-start | bytes 1032200 | tf_op jit(solution)/shard_map/ppermute | solution.py:366
  114.0 0.8 fusion.1
  114.8 0.9 pad_maximum_fusion.1
  115.7 3.6 %collective-permute-done.18.refs_6_ = bf16[192,896]{1,0:T(8,128)(2,1)S(1)} collective-permute-done((bf16[192,896]{1,0:T(8,128)(2,1)S(1)}, bf16[192,896]{1,0:T(8,128)(2,1)S(1)}, u32[]{:S(2)}, u32[]{:S(2)}) %collective-permute-start.18) | collective-permute-done | bytes 344096 | tf_op jit(solution)/shard_map/ppermute | solution.py:365
  119.2 3.8 %collective-permute-done.19.refs_7_ = bf16[192,896]{1,0:T(8,128)(2,1)S(1)} collective-permute-done((bf16[192,896]{1,0:T(8,128)(2,1)S(1)}, bf16[192,896]{1,0:T(8,128)(2,1)S(1)}, u32[]{:S(2)}, u32[]{:S(2)}) %collective-permute-start.19) | collective-permute-done | bytes 344096 | tf_op jit(solution)/shard_map/ppermute | solution.py:366
  123.1 1.0 copy-done.5
  124.1 1.4 prepare.1
  125.5 1.6 %copy-done = bf16[4,384,896]{2,1,0:T(8,128)(2,1)} copy-done((bf16[4,384,896]{2,1,0:T(8,128)(2,1)}, bf16[4,384,896]{2,1,0:T(8,128)(2,1)S(1)}, u32[]{:S(2)}) %copy-start) | copy-done | bytes 2752536
  127.7 10.3 %decode.1 = bf16[192,896]{1,0:T(8,128)(2,1)} custom-call(bf16[4,384,896]{2,1,0:T(8,128)(2,1)} %copy-done, f32[384,1]{1,0:T(8,128)} %copy-done.6, bf16[3584,1152]{1,0:T(8,128)(2,1)} %all-gather.2.cloned.1.call-done.w_ref, f32[1,1152]{1,0:T(1,128)} %broadcast_in_dim.7.bias_ref, f32[384,128]{1,0:T(8,128)} %get-tuple-element.22.cos_ref, ...), custom_call_target="tpu_custom_call" | custom-call | flops 1585446912 | bytes 9633792 | tf_op jit(solution)/shard_map/decode/pallas_call | solution.py:123
  138.0 1.7 %select_bitcast_fusion = bf16[1,192,896]{2,1,0:T(8,128)(2,1)} fusion(bf16[192,896]{1,0:T(8,128)(2,1)S(1)} %tokens_part.1, bf16[192,896]{1,0:T(8,128)(2,1)} %decode.1, pred[]{:T(512)S(6)} %eq.85), kind=kLoop, calls=%fused_computation.4 | loop fusion | flops 172032 | bytes 1032193 | tf_op jit(solution)/shard_map/broadcast_in_dim | solution.py:370
  (65 shorter events, 8.4 us)
Async XLA Ops:
  6.5 121.2 %all-gather.2.cloned.1.call-start = ((), (), s32[]{:S(2)}) async-start(), calls=%async_computation | async-start | bytes 8386560 | tf_op jit(solution)/shard_map/all_gather | solution.py:325
  7.3 24.7 %collective-permute-start.11 = (bf16[192,896]{1,0:T(8,128)(2,1)}, bf16[192,896]{1,0:T(8,128)(2,1)S(1)}, u32[]{:S(2)}, u32[]{:S(2)}) collective-permute-start(bf16[192,896]{1,0:T(8,128)(2,1)} %refs_0_.1), channel_id=1, source_target_pairs={{256,257},{257,258},{258,259},{259,256},{260,261},{261,262},{262,2... | collective-permute-start | bytes 1032200 | tf_op jit(solution)/shard_map/ppermute | solution.py:331
  13.4 18.6 %collective-permute-start.12 = (bf16[192,896]{1,0:T(8,128)(2,1)}, bf16[192,896]{1,0:T(8,128)(2,1)S(1)}, u32[]{:S(2)}, u32[]{:S(2)}) collective-permute-start(bf16[192,896]{1,0:T(8,128)(2,1)} %refs_0_.1), channel_id=1, source_target_pairs={{256,259},{257,256},{258,257},{259,258},{260,263},{261,260},{262,2... | collective-permute-start | bytes 1032200 | tf_op jit(solution)/shard_map/ppermute | solution.py:332
  19.2 10.6 %collective-permute-start.1 = (bf16[20,896]{1,0:T(8,128)(2,1)}, bf16[20,896]{1,0:T(8,128)(2,1)S(1)}, u32[]{:S(2)}, u32[]{:S(2)}) collective-permute-start(bf16[20,896]{1,0:T(8,128)(2,1)} %param.17), channel_id=1, source_target_pairs={{0,56},{4,60},{8,0},{12,4},{16,8},{20,12},{24,16},{28,20},{32,24},... | collective-permute-start | bytes 107528 | tf_op jit(solution)/shard_map/ppermute | solution.py:273
  19.9 10.6 %collective-permute-start = (bf16[20,896]{1,0:T(8,128)(2,1)}, bf16[20,896]{1,0:T(8,128)(2,1)S(1)}, u32[]{:S(2)}, u32[]{:S(2)}) collective-permute-start(bf16[20,896]{1,0:T(8,128)(2,1)} %param.17), channel_id=1, source_target_pairs={{0,8},{4,12},{8,16},{12,20},{16,24},{20,28},{24,32},{28,36},{32,40... | collective-permute-start | bytes 107528 | tf_op jit(solution)/shard_map/ppermute | solution.py:273
  21.9 1.5 %copy-start.7 = (bf16[768,1280]{1,0:T(8,128)(2,1)S(1)}, bf16[768,1280]{1,0:T(8,128)(2,1)}, u32[]{:S(2)}) copy-start(bf16[768,1280]{1,0:T(8,128)(2,1)} %audio_ref.1) | copy-start | bytes 5898244
  23.5 1.4 copy-start.8
  24.9 5.6 %copy-start.11 = (bf16[20,896]{1,0:T(8,128)(2,1)S(1)}, bf16[20,896]{1,0:T(8,128)(2,1)}, u32[]{:S(2)}) copy-start(bf16[20,896]{1,0:T(8,128)(2,1)} %param.17) | copy-start | bytes 107524
  24.9 7.1 %copy-start.10 = (f32[31,320]{1,0:T(8,128)S(1)}, f32[31,320]{1,0:T(8,128)}, u32[]{:S(2)}) copy-start(f32[31,320]{1,0:T(8,128)} %taps_ref.1) | copy-start | bytes 119044
  28.8 2.5 %collective-permute-start.10 = (bf16[16,320]{1,0:T(8,128)(2,1)S(1)}, bf16[16,320]{1,0:T(8,128)(2,1)S(1)}, u32[]{:S(2)}, u32[]{:S(2)}) collective-permute-start(bf16[16,320]{1,0:T(8,128)(2,1)S(1)} %get-tuple-element.15), channel_id=1, source_target_pairs={{4,0},{8,4},{12,8},{16,12},{20,16},{24,20},{28,24},{32,28},{36,32}... | collective-permute-start | bytes 30728 | tf_op jit(solution)/shard_map/ppermute | solution.py:342
  29.8 2.1 %collective-permute-start.9 = (bf16[16,320]{1,0:T(8,128)(2,1)S(1)}, bf16[16,320]{1,0:T(8,128)(2,1)S(1)}, u32[]{:S(2)}, u32[]{:S(2)}) collective-permute-start(bf16[16,320]{1,0:T(8,128)(2,1)S(1)} %get-tuple-element.16), channel_id=1, source_target_pairs={{0,4},{4,8},{8,12},{12,16},{16,20},{20,24},{24,28},{28,32},{32,36}... | collective-permute-start | bytes 30728 | tf_op jit(solution)/shard_map/ppermute | solution.py:341
  30.5 9.7 %collective-permute-start.2 = (bf16[60,896]{1,0:T(8,128)(2,1)S(1)}, bf16[60,896]{1,0:T(8,128)(2,1)S(1)}, u32[]{:S(2)}, u32[]{:S(2)}) collective-permute-start(bf16[60,896]{1,0:T(8,128)(2,1)S(1)} %pad_maximum_fusion.3), channel_id=1, source_target_pairs={{0,40},{4,44},{8,48},{12,52},{16,56},{20,60},{24,0},{28,4},{32,8},... | collective-permute-start | bytes 322568 | tf_op jit(solution)/shard_map/ppermute | solution.py:273
  31.3 9.0 %collective-permute-start.3 = (bf16[40,896]{1,0:T(8,128)(2,1)S(1)}, bf16[40,896]{1,0:T(8,128)(2,1)S(1)}, u32[]{:S(2)}, u32[]{:S(2)}) collective-permute-start(bf16[40,896]{1,0:T(8,128)(2,1)S(1)} %pad_maximum_fusion.4), channel_id=1, source_target_pairs={{0,24},{4,28},{8,32},{12,36},{16,40},{20,44},{24,48},{28,52},{32,5... | collective-permute-start | bytes 215048 | tf_op jit(solution)/shard_map/ppermute | solution.py:273
  31.9 11.9 %copy-start.2 = (bf16[192,896]{1,0:T(8,128)(2,1)}, bf16[192,896]{1,0:T(8,128)(2,1)S(1)}, u32[]{:S(2)}) copy-start(bf16[192,896]{1,0:T(8,128)(2,1)S(1)} %collective-permute-done.11.refs_0_.refs_3_) | copy-start | bytes 1032196
  33.2 5.5 %copy-start.4 = (bf16[192,896]{1,0:T(8,128)(2,1)}, bf16[192,896]{1,0:T(8,128)(2,1)S(1)}, u32[]{:S(2)}) copy-start(bf16[192,896]{1,0:T(8,128)(2,1)S(1)} %collective-permute-done.12.refs_1_) | copy-start | bytes 1032196
  38.8 8.4 %collective-permute-start.13 = (bf16[192,1280]{1,0:T(8,128)(2,1)S(1)}, bf16[192,1280]{1,0:T(8,128)(2,1)}, u32[]{:S(2)}, u32[]{:S(2)}) collective-permute-start(bf16[192,1280]{1,0:T(8,128)(2,1)S(1)} %conv.1), channel_id=1, source_target_pairs={{0,1},{1,0},{2,3},{3,2},{4,5},{5,4},{6,7},{7,6},{8,9},{9,8},{10,11... | collective-permute-start | bytes 1474568 | tf_op jit(solution)/shard_map/ppermute | solution.py:344
  40.8 3.0 %collective-permute-start.4 = (bf16[160,896]{1,0:T(8,128)(2,1)S(1)}, bf16[160,896]{1,0:T(8,128)(2,1)S(1)}, u32[]{:S(2)}, u32[]{:S(2)}) collective-permute-start(bf16[160,896]{1,0:T(8,128)(2,1)S(1)} %concatenate.99.refs_0_), channel_id=1, source_target_pairs={{0,64},{4,68},{8,72},{12,76},{16,80},{20,84},{24,88},{28,92},{32,9... | collective-permute-start | bytes 860168 | tf_op jit(solution)/shard_map/ppermute | solution.py:273
  41.5 4.8 %collective-permute-start.5 = (bf16[160,896]{1,0:T(8,128)(2,1)S(1)}, bf16[160,896]{1,0:T(8,128)(2,1)S(1)}, u32[]{:S(2)}, u32[]{:S(2)}) collective-permute-start(bf16[160,896]{1,0:T(8,128)(2,1)S(1)} %concatenate.99.refs_0_), channel_id=1, source_target_pairs={{0,192},{4,196},{8,200},{12,204},{16,208},{20,212},{24,216},{28,22... | collective-permute-start | bytes 860168 | tf_op jit(solution)/shard_map/ppermute | solution.py:273
  42.2 4.1 %collective-permute-start.6 = (bf16[160,896]{1,0:T(8,128)(2,1)S(1)}, bf16[160,896]{1,0:T(8,128)(2,1)S(1)}, u32[]{:S(2)}, u32[]{:S(2)}) collective-permute-start(bf16[160,896]{1,0:T(8,128)(2,1)S(1)} %concatenate.99.refs_0_), channel_id=1, source_target_pairs={{0,128},{4,132},{8,136},{12,140},{16,144},{20,148},{24,152},{28,15... | collective-permute-start | bytes 860168 | tf_op jit(solution)/shard_map/ppermute | solution.py:273
  43.1 7.3 %collective-permute-start.7 = (bf16[160,896]{1,0:T(8,128)(2,1)S(1)}, bf16[160,896]{1,0:T(8,128)(2,1)S(1)}, u32[]{:S(2)}, u32[]{:S(2)}) collective-permute-start(bf16[160,896]{1,0:T(8,128)(2,1)S(1)} %concatenate.99.refs_0_), channel_id=1, source_target_pairs={{0,4},{4,0},{8,12},{12,8},{16,20},{20,16},{24,28},{28,24},{32,36},... | collective-permute-start | bytes 860168 | tf_op jit(solution)/shard_map/ppermute | solution.py:327
  43.8 13.6 %collective-permute-start.15 = (bf16[192,896]{1,0:T(8,128)(2,1)S(1)}, bf16[192,896]{1,0:T(8,128)(2,1)S(1)}, u32[]{:S(2)}, u32[]{:S(2)}) collective-permute-start(bf16[192,896]{1,0:T(8,128)(2,1)S(1)} %collective-permute-done.11.refs_0_.refs_3_), channel_id=1, source_target_pairs={{256,257},{257,258},{258,259},{259,256},{260,261},{261,262},{262,2... | collective-permute-start | bytes 1032200 | tf_op jit(solution)/shard_map/ppermute | solution.py:333
  46.4 11.1 %collective-permute-start.8 = (bf16[480,896]{1,0:T(8,128)(2,1)S(1)}, bf16[480,896]{1,0:T(8,128)(2,1)S(1)}, u32[]{:S(2)}, u32[]{:S(2)}) collective-permute-start(bf16[480,896]{1,0:T(8,128)(2,1)S(1)} %pad_maximum_fusion), channel_id=1, source_target_pairs={{0,4},{4,0},{8,12},{12,8},{16,20},{20,16},{24,28},{28,24},{32,36},... | collective-permute-start | bytes 2580488 | tf_op jit(solution)/shard_map/ppermute | solution.py:327
  48.3 9.2 %collective-permute-start.14 = (bf16[192,1280]{1,0:T(8,128)(2,1)S(1)}, bf16[192,1280]{1,0:T(8,128)(2,1)S(1)}, u32[]{:S(2)}, u32[]{:S(2)}) collective-permute-start(bf16[192,1280]{1,0:T(8,128)(2,1)S(1)} %get-tuple-element.13), channel_id=1, source_target_pairs={{1,2},{2,1},{3,0},{0,3},{5,6},{6,5},{7,4},{4,7},{9,10},{10,9},{11,... | collective-permute-start | bytes 1474568 | tf_op jit(solution)/shard_map/ppermute | solution.py:347
  57.5 4.1 %copy-start.12 = (f32[3584]{0:T(1024)S(1)}, f32[3584]{0:T(1024)}, u32[]{:S(2)}) copy-start(f32[3584]{0:T(1024)} %param.19) | copy-start | bytes 43012
  57.5 4.2 %copy-start.13 = (f32[1152]{0:T(1024)S(1)}, f32[1152]{0:T(1024)}, u32[]{:S(2)}) copy-start(f32[1152]{0:T(1024)} %param.21) | copy-start | bytes 13828
  57.5 65.6 %copy-start.1 = (bf16[192,896]{1,0:T(8,128)(2,1)S(1)}, bf16[192,896]{1,0:T(8,128)(2,1)}, u32[]{:S(2)}) copy-start(bf16[192,896]{1,0:T(8,128)(2,1)} %refs_0_.1) | copy-start | bytes 1032196
  57.5 65.6 %copy-start.3 = (bf16[192,896]{1,0:T(8,128)(2,1)S(1)}, bf16[192,896]{1,0:T(8,128)(2,1)}, u32[]{:S(2)}) copy-start(bf16[192,896]{1,0:T(8,128)(2,1)} %copy-done.2) | copy-start | bytes 1032196
  59.0 47.3 %collective-permute-start.17 = (bf16[192,896]{1,0:T(8,128)(2,1)S(1)}, bf16[192,896]{1,0:T(8,128)(2,1)S(1)}, u32[]{:S(2)}, u32[]{:S(2)}) collective-permute-start(bf16[192,896]{1,0:T(8,128)(2,1)S(1)} %tokens_part.1), channel_id=1, source_target_pairs={{0,259},{1,256},{2,257},{3,258},{4,263},{5,260},{6,261},{7,262},{8... | collective-permute-start | bytes 1032200 | tf_op jit(solution)/shard_map/ppermute | solution.py:364
  60.3 49.7 %collective-permute-start.16 = (bf16[192,896]{1,0:T(8,128)(2,1)S(1)}, bf16[192,896]{1,0:T(8,128)(2,1)S(1)}, u32[]{:S(2)}, u32[]{:S(2)}) collective-permute-start(bf16[192,896]{1,0:T(8,128)(2,1)S(1)} %tokens_part.1), channel_id=1, source_target_pairs={{0,256},{1,257},{2,258},{3,259},{4,260},{5,261},{6,262},{7,263},{8... | collective-permute-start | bytes 1032200 | tf_op jit(solution)/shard_map/ppermute | solution.py:363
  106.3 12.9 %collective-permute-start.18 = (bf16[192,896]{1,0:T(8,128)(2,1)S(1)}, bf16[192,896]{1,0:T(8,128)(2,1)S(1)}, u32[]{:S(2)}, u32[]{:S(2)}) collective-permute-start(bf16[192,896]{1,0:T(8,128)(2,1)S(1)} %collective-permute-done.17.refs_5_), channel_id=1, source_target_pairs={{256,259},{257,256},{258,257},{259,258},{260,263},{261,260},{262,2... | collective-permute-start | bytes 1032200 | tf_op jit(solution)/shard_map/ppermute | solution.py:365
  110.0 13.1 %collective-permute-start.19 = (bf16[192,896]{1,0:T(8,128)(2,1)S(1)}, bf16[192,896]{1,0:T(8,128)(2,1)S(1)}, u32[]{:S(2)}, u32[]{:S(2)}) collective-permute-start(bf16[192,896]{1,0:T(8,128)(2,1)S(1)} %collective-permute-done.16.refs_4_), channel_id=1, source_target_pairs={{256,257},{257,258},{258,259},{259,256},{260,261},{261,262},{262,2... | collective-permute-start | bytes 1032200 | tf_op jit(solution)/shard_map/ppermute | solution.py:366
  125.5 1.6 %copy-start = (bf16[4,384,896]{2,1,0:T(8,128)(2,1)}, bf16[4,384,896]{2,1,0:T(8,128)(2,1)S(1)}, u32[]{:S(2)}) copy-start(bf16[4,384,896]{2,1,0:T(8,128)(2,1)S(1)} %get-tuple-element.11.rows_ref) | copy-start | bytes 8257540
  (3 other events, 2.9 us)
Sparse Core Ops, SparseCore 0:
  10.6 91.8 all-gather.1

commit v6 on v5

--- a/solution.py
+++ b/solution.py
@@ -28,46 +28,33 @@
     return values * cosine + pltpu.roll(values, HEAD // 2, 1) * sine
 
 
-def prepare_kernel(order_ref, *refs, parts):
+def decode_kernel(
+    order_ref, *refs, parts
+):
     ins = refs[: 2 * parts]
-    gain_ref, rows_ref, scale_ref = refs[2 * parts : 2 * parts + 3]
-    count = ins[0].shape[0]
-    for first, blocks in ((0, ins[:parts]), (count, ins[parts:])):
-        square = jnp.zeros((count, 1), jnp.float32)
-        for i, ref in enumerate(blocks):
-            block = order_ref[i]
-            x = ref[...].astype(jnp.float32)
-            square = square + jnp.sum(x * x, axis=1, keepdims=True)
-            rows_ref[block, first : first + count] = (x * gain_ref[block]).astype(jnp.bfloat16)
-        scale_ref[first : first + count] = lax.rsqrt(square / (parts * ins[0].shape[1]) + 1e-6)
-
-
-def prepare(order, words, sounds, gain):
-    parts = len(words)
-    count, width = words[0].shape
-    vmem = pl.BlockSpec(memory_space=pltpu.VMEM)
-    return pl.pallas_call(
-        functools.partial(prepare_kernel, parts=parts),
-        in_specs=[pl.BlockSpec(memory_space=pltpu.SMEM)] + [vmem] * (2 * parts + 1),
-        out_specs=[vmem, vmem],
-        out_shape=[
-            jax.ShapeDtypeStruct((parts, 2 * count, width), jnp.bfloat16),
-            jax.ShapeDtypeStruct((2 * count, 1), jnp.float32),
-        ],
-        compiler_params=pltpu.CompilerParams(vmem_limit_bytes=16 * MIB),
-        cost_estimate=pl.CostEstimate(
-            flops=8 * count * parts * width, bytes_accessed=8 * count * parts * width, transcendentals=0
-        ),
-        name="prepare",
-    )(order, *words, *sounds, gain)
-
-
-def decode_kernel(rows_ref, scale_ref, w_ref, bias_ref, cos_ref, sin_ref, out_ref, acc, acc_kv):
+    gain_ref, w_ref, bias_ref, cos_ref, sin_ref, out_ref, held, rows, scales, acc, acc_kv, sem = refs[2 * parts :]
     step = pl.program_id(0)
     count, total = acc.shape
     heads = total // HEAD - 2
-    text = jnp.dot(rows_ref[0, :count], w_ref[...], preferred_element_type=jnp.float32)
-    audio = jnp.dot(rows_ref[0, count:], w_ref[:, heads * HEAD :], preferred_element_type=jnp.float32)
+    width = held.shape[2]
+
+    @pl.when(step == 0)
+    def _():
+        copies = [pltpu.make_async_copy(ref, held.at[i], sem.at[i]) for i, ref in enumerate(ins)]
+        for copy in copies:
+            copy.start()
+        for first, side in ((0, 0), (count, parts)):
+            square = jnp.zeros((count, 1), jnp.float32)
+            for i in range(parts):
+                copies[side + i].wait()
+                block = order_ref[i]
+                x = held[side + i].astype(jnp.float32)
+                square = square + jnp.sum(x * x, axis=1, keepdims=True)
+                rows[block, first : first + count] = (x * gain_ref[block]).astype(jnp.bfloat16)
+            scales[first : first + count] = lax.rsqrt(square / (parts * width) + 1e-6)
+
+    text = jnp.dot(rows[step, :count], w_ref[...], preferred_element_type=jnp.float32)
+    audio = jnp.dot(rows[step, count:], w_ref[:, heads * HEAD :], preferred_element_type=jnp.float32)
 
     @pl.when(step == 0)
     def _():
@@ -81,7 +68,7 @@
 
     @pl.when(step == pl.num_programs(0) - 1)
     def _():
-        scale, scale_kv = scale_ref[:count], scale_ref[count:]
+        scale, scale_kv = scales[:count], scales[count:]
         cosine, sine = cos_ref[count:], sin_ref[count:]
         key_cols = slice(heads * HEAD, (heads + 1) * HEAD)
         value_cols = slice((heads + 1) * HEAD, total)
@@ -114,18 +101,19 @@
             ).astype(jnp.bfloat16)
 
 
-def decode(rows, scale, weight, bias, tables):
-    parts, count, width = rows.shape
-    count //= 2
+def decode(order, words, sounds, gain, weight, bias, tables):
+    parts = len(words)
+    count, width = words[0].shape
     total = weight.shape[1]
     columns = total - 2 * HEAD
     whole = lambda *shape: pl.BlockSpec(shape, lambda k: (0,) * len(shape))
     return pl.pallas_call(
-        decode_kernel,
+        functools.partial(decode_kernel, parts=parts),
         grid=(parts,),
-        in_specs=[
-            pl.BlockSpec((1, 2 * count, width), lambda k: (k, 0, 0)),
-            whole(2 * count, 1),
+        in_specs=[pl.BlockSpec(memory_space=pltpu.SMEM)]
+        + [pl.BlockSpec(memory_space=pl.ANY)] * (2 * parts)
+        + [
+            whole(parts, 1, width),
             pl.BlockSpec((width, total), lambda k: (k, 0)),
             whole(1, total),
             whole(2 * count, HEAD),
@@ -133,8 +121,12 @@
         ],
         out_specs=whole(count, columns),
         scratch_shapes=[
+            pltpu.VMEM((2 * parts, count, width), jnp.bfloat16),
+            pltpu.VMEM((parts, 2 * count, width), jnp.bfloat16),
+            pltpu.VMEM((2 * count, 1), jnp.float32),
             pltpu.VMEM((count, total), jnp.float32),
             pltpu.VMEM((count, 2 * HEAD), jnp.float32),
+            pltpu.SemaphoreType.DMA((2 * parts,)),
         ],
         out_shape=jax.ShapeDtypeStruct((count, columns), jnp.bfloat16),
         compiler_params=pltpu.CompilerParams(vmem_limit_bytes=56 * MIB),
@@ -142,7 +134,7 @@
             flops=2 * count * parts * width * total, bytes_accessed=2 * parts * width * (total + count), transcendentals=0
         ),
         name="decode",
-    )(rows, scale, weight, bias, *tables)
+    )(order, *words, *sounds, gain, weight, bias, *tables)
 
 
 def pooling(rows):
@@ -252,6 +244,29 @@
     )(before, gated, after, taps, pw, *after_these)
 
 
+def add_kernel(tag_ref, a_ref, b_ref, total_ref, sent_ref, same_ref):
+    same_ref[0] = tag_ref[0]
+    total = a_ref[...].astype(jnp.float32) + b_ref[...].astype(jnp.float32)
+    total_ref[...] = total
+    sent_ref[...] = total.astype(sent_ref.dtype)
+
+
+def add(tag, a, b):
+    vmem, smem = pl.BlockSpec(memory_space=pltpu.VMEM), pl.BlockSpec(memory_space=pltpu.SMEM)
+    return pl.pallas_call(
+        add_kernel,
+        in_specs=[smem, vmem, vmem],
+        out_specs=[vmem, vmem, smem],
+        out_shape=[
+            jax.ShapeDtypeStruct(a.shape, jnp.float32),
+            jax.ShapeDtypeStruct(a.shape, jnp.bfloat16),
+            jax.ShapeDtypeStruct((1,), jnp.int32),
+        ],
+        compiler_params=pltpu.CompilerParams(vmem_limit_bytes=8 * MIB),
+        name="add",
+    )(tag, a, b)
+
+
 def place(shift_x, shift_y):
     return [
         ((x * NY + y) * 2 + c, ((x + shift_x) % NX * NY + (y + shift_y) % NY) * 2 + c)
@@ -278,36 +293,61 @@
     return [(0, steps, line)] + [(dx, steps, send(line, -dx, 0)) for dx in (-1, 1, 2)]
 
 
+def pooled_kernel(audio_ref, term_ref, other_ref, expand_ref, out_ref):
+    pooled = (audio_ref[...] + term_ref[...] + other_ref[...].astype(jnp.float32)).astype(jnp.bfloat16)
+    out_ref[...] = jnp.dot(pooled, expand_ref[...], preferred_element_type=jnp.float32).astype(jnp.bfloat16)
+
+
+def pooled_part(pooled_audio, term, other, expand):
+    vmem = pl.BlockSpec(memory_space=pltpu.VMEM)
+    return pl.pallas_call(
+        pooled_kernel,
+        in_specs=[vmem] * 4,
+        out_specs=vmem,
+        out_shape=jax.ShapeDtypeStruct((pooled_audio.shape[0], expand.shape[1]), jnp.bfloat16),
+        compiler_params=pltpu.CompilerParams(vmem_limit_bytes=12 * MIB),
+        cost_estimate=pl.CostEstimate(flops=5_000_000_000, bytes_accessed=8000000, transcendentals=0),
+        name="pooled_part",
+    )(pooled_audio, term, other, expand)
+
+
 def tokens_kernel(*refs, counts):
     pieces = refs[: len(counts)]
-    audio_ref, term_ref, other_ref, expand_ref = refs[len(counts) : len(counts) + 4]
-    out_ref, weight = refs[-2:]
+    pooled_ref = refs[len(counts)]
+    out_ref, weight, sem = refs[-3:]
+    copies = []
     at = 0
-    for ref, count in zip(pieces, counts, strict=True):
-        weight[at : at + count] = ref[...]
+    for i, (ref, count) in enumerate(zip(pieces, counts, strict=True)):
+        copies.append(pltpu.make_async_copy(ref, weight.at[at : at + count], sem.at[i]))
         at += count
-    pooled = (audio_ref[...] + term_ref[...] + other_ref[...].astype(jnp.float32)).astype(jnp.bfloat16)
-    ordered = jnp.dot(pooled, expand_ref[...], preferred_element_type=jnp.float32).astype(jnp.bfloat16)
-    out_ref[...] = jnp.dot(ordered, weight[...], preferred_element_type=jnp.float32).astype(out_ref.dtype)
-
-
-def tokens_part(pieces, pooled_audio, term, other, expand, *after_these):
+    for copy in copies:
+        copy.start()
+    for copy in copies:
+        copy.wait()
+    out_ref[...] = jnp.dot(pooled_ref[...], weight[...], preferred_element_type=jnp.float32).astype(out_ref.dtype)
+
+
+def tokens_part(pieces, pooled, *after_these):
     counts = [p.shape[0] for p in pieces]
-    count = pooled_audio.shape[0]
+    count = pooled.shape[0]
     columns = pieces[0].shape[1]
+    anywhere = pl.BlockSpec(memory_space=pl.ANY)
     vmem = pl.BlockSpec(memory_space=pltpu.VMEM)
     return pl.pallas_call(
         functools.partial(tokens_kernel, counts=counts),
-        in_specs=[vmem] * (len(pieces) + 4) + [pl.BlockSpec(memory_space=pl.ANY)] * len(after_these),
+        in_specs=[anywhere] * len(pieces) + [vmem] + [anywhere] * len(after_these),
         out_specs=vmem,
         out_shape=jax.ShapeDtypeStruct((count, columns), jnp.bfloat16),
-        scratch_shapes=[pltpu.VMEM((sum(counts), columns), jnp.bfloat16)],
-        compiler_params=pltpu.CompilerParams(vmem_limit_bytes=20 * MIB),
+        scratch_shapes=[
+            pltpu.VMEM((sum(counts), columns), jnp.bfloat16),
+            pltpu.SemaphoreType.DMA((len(pieces),)),
+        ],
+        compiler_params=pltpu.CompilerParams(vmem_limit_bytes=60 * MIB),
         cost_estimate=pl.CostEstimate(
             flops=4 * count * sum(counts) * columns, bytes_accessed=8000000, transcendentals=0
         ),
         name="tokens_part",
-    )(*pieces, pooled_audio, term, other, expand, *after_these)
+    )(*pieces, pooled, *after_these)
 
 
 def shards(
@@ -326,7 +366,7 @@
     pieces = spread(adapt_weight)
     swap = lambda v: lax.ppermute(v, ("grp", "seq"), of_group(0, SWAP))
     adapter = [p for _, _, p in pieces]
-    adapter += [swap(adapter[0]), swap(jnp.concatenate(adapter[1:], axis=0))]
+    adapter += [swap(adapter[0])]
 
     behind = lax.ppermute(text, both, ring(1, 1))
     ahead = lax.ppermute(text, both, ring(1, -1))
@@ -341,10 +381,10 @@
     before_edge = lax.ppermute(gated[frames - EDGE :], ("grp", "seq"), of_group(0, up))
     after_edge = lax.ppermute(gated[:EDGE], ("grp", "seq"), of_group(0, [(j, i) for i, j in up]))
     term = conv(before_edge, gated, after_edge, dw_kernel, pw_weight, behind, ahead)
-    term = term.astype(jnp.float32) + lax.ppermute(
-        term, both, [(0, 1), (1, 0), (2, 3), (3, 2)]
-    ).astype(jnp.float32)
-    other = lax.ppermute(term.astype(jnp.bfloat16), both, [(1, 2), (2, 1), (3, 0), (0, 3)])
+    neighbour = lax.ppermute(term, both, [(0, 1), (1, 0), (2, 3), (3, 2)])
+    term, rounded, tag = add(core[None], term, neighbour)
+    other = lax.ppermute(rounded, both, [(1, 2), (2, 1), (3, 0), (0, 3)])
+    adapter += [swap(jnp.where(tag[0] >= 0, jnp.concatenate(adapter[1:4], axis=0), 0))]
 
     chips = jnp.concatenate(
         [
@@ -355,18 +395,17 @@
     device = jnp.concatenate([2 * chips + core, 2 * chips + 1 - core])
     source = (device[:, None] * rows + jnp.arange(rows, dtype=jnp.int32)[None]).reshape(-1)
     expand = (jnp.arange(audio.shape[1], dtype=jnp.int32)[:, None] == source[None]).astype(jnp.bfloat16)
-    tokens = tokens_part(adapter, pooled_audio, term, other, expand, second)
+    tokens = tokens_part(adapter, pooled_part(pooled_audio, term, other, expand), second)
 
     tables = rotary_tables(2 * text.shape[0])
     gain = norm_gain.reshape(n_mdl, 1, width)
     order = (mdl + jnp.arange(n_mdl, dtype=jnp.int32)) % n_mdl
-    same = lax.ppermute(tokens, both, [(i, n_mdl + i) for i in range(n_mdl)])
-    following = lax.ppermute(tokens, both, [(i, n_mdl + (i - 1) % n_mdl) for i in range(n_mdl)])
-    across = lax.ppermute(following, both, ring(1, -1))
-    last = lax.ppermute(same, both, ring(1, 1))
-    sounds = [same, following, across, last]
-    prepared, scale = prepare(order, words, sounds, gain)
-    context = decode(prepared, scale, weight, qkv_bias[None], tables)
+    order_of = (2, -1, 0, 1)
+    sent = {
+        k: lax.ppermute(tokens, both, [(i, n_mdl + (i + k) % n_mdl) for i in range(n_mdl)]) for k in order_of
+    }
+    sounds = [sent[0], sent[-1], sent[2], sent[1]]
+    context = decode(order, words, sounds, gain, weight, qkv_bias[None], tables)
     return jnp.where(grp == 0, tokens, context)[None]
 
 

time: 147 us -> 154 us (1.048)
  the two profiles are of different devices: /device:TPU:122 before, /device:TPU:80 now
where the time goes in v6:
time: 154 us; the launch traced here: 153 us
  waiting for transfers between devices  58.1 us (38%)
  starting transfers between devices  30.2 us (20%)
  Pallas kernels  28.7 us (19%)
  between operations  15.4 us (10%)
  local copies, waits for them, and re-layouts  13.7 us (9%)
  other arithmetic  6.88 us (4%)
    ppermute x4, waiting for transfers between devices, shards(): lax.ppermute(tokens, both, [(i, n_mdl + (i + k) % n_mdl) for i in range(n...  51 us
    pallas_call x1, Pallas kernels, decode(): pl.pallas_call(functools.partial(decode_kernel, parts=parts), grid=(parts...  12.5 us
    unnamed x50, local copies, waits for them, and re-layouts  11.1 us
    ppermute x1, waiting for transfers between devices, shards(): second = lax.ppermute(behind, both, ring(1, 1))  6.29 us
    ppermute x1, starting transfers between devices, shards(): behind = lax.ppermute(text, both, ring(1, 1))  6.09 us
    ppermute x1, starting transfers between devices, shards(): ahead = lax.ppermute(text, both, ring(1, -1))  5.87 us
    pallas_call x1, Pallas kernels, conv(): pl.pallas_call(conv_kernel, in_specs=[vmem] * 5 + [pl.BlockSpec(memory_sp...  5.48 us
    ppermute x4, starting transfers between devices, shards(): lax.ppermute(tokens, both, [(i, n_mdl + (i + k) % n_mdl) for i in range(n...  5.35 us
  transfers between devices with their start and end apart: 21, of which 4 were waited for; matrix products, arithmetic and copies ran while one was open for 5% of the time, Pallas kernels for 11%

profile of v6, /device:TPU:80, one launch (start us, length us, event | category | flops | bytes accessed | tf_op | source)
XLA Modules:
  0.0 152.8 jit_solution(13432447826243500121)
XLA Ops:
  7.3 6.1 %collective-permute-start.10 = (bf16[192,896]{1,0:T(8,128)(2,1)}, bf16[192,896]{1,0:T(8,128)(2,1)S(1)}, u32[]{:S(2)}, u32[]{:S(2)}) collective-permute-start(bf16[192,896]{1,0:T(8,128)(2,1)} %refs_0_.1), channel_id=1, source_target_pairs={{256,257},{257,258},{258,259},{259,256},{260,261},{261,262},{262,2... | collective-permute-start | bytes 1032200 | tf_op jit(solution)/shard_map/ppermute | solution.py:371
  13.4 5.9 %collective-permute-start.11 = (bf16[192,896]{1,0:T(8,128)(2,1)}, bf16[192,896]{1,0:T(8,128)(2,1)S(1)}, u32[]{:S(2)}, u32[]{:S(2)}) collective-permute-start(bf16[192,896]{1,0:T(8,128)(2,1)} %refs_0_.1), channel_id=1, source_target_pairs={{256,259},{257,256},{258,257},{259,258},{260,263},{261,260},{262,2... | collective-permute-start | bytes 1032200 | tf_op jit(solution)/shard_map/ppermute | solution.py:372
  21.9 1.5 %copy-done.3 = bf16[768,1280]{1,0:T(8,128)(2,1)S(1)} copy-done((bf16[768,1280]{1,0:T(8,128)(2,1)S(1)}, bf16[768,1280]{1,0:T(8,128)(2,1)}, u32[]{:S(2)}) %copy-start.3) | copy-done | bytes 1966104
  23.5 1.4 copy-done.4
  24.9 3.8 %gate.1 = (bf16[768,320]{1,0:T(8,128)(2,1)S(1)}, f32[192,1280]{1,0:T(8,128)S(1)}) custom-call(s32[1]{0:T(128)S(6)} %sub.20.count_ref, bf16[768,1280]{1,0:T(8,128)(2,1)S(1)} %copy-done.3, f32[1,1280]{1,0:T(1,128)S(1)} %broadcast_in_dim.22.gain_ref, bf16[2,320,1280]{2,1,0:T(8,128)(2,1)S(1)} %bitcast.38), custom_call_target="tpu_custom_call" | custom-call | flops 1258291200 | bytes 7864320 | tf_op jit(solution)/shard_map/gate/pallas_call | solution.py:168
  28.7 0.9 copy-done.9
  32.9 5.5 %conv.1.a_ref = bf16[192,1280]{1,0:T(8,128)(2,1)S(1)} custom-call(bf16[16,320]{1,0:T(8,128)(2,1)S(1)} %collective-permute-done.8.before_ref, bf16[768,320]{1,0:T(8,128)(2,1)S(1)} %get-tuple-element.10.gated_ref, bf16[16,320]{1,0:T(8,128)(2,1)S(1)} %collective-permute-done.9.after_ref, f32[31,320]{1,0:T(8,128)S(1)} %copy-done.8, ...), custom_call_target="tpu_custom_call" | custom-call | flops 5000000000 | bytes 1966080 | tf_op jit(solution)/shard_map/conv/pallas_call | solution.py:230
  38.4 0.7 copy-done.1
  43.4 0.9 add.394
  44.3 1.0 copy-done.5
  45.3 1.5 collective-permute-start.14
  47.4 1.2 maximum_select_fusion
  48.6 1.6 %collective-permute-start.13 = (bf16[480,896]{1,0:T(8,128)(2,1)}, bf16[480,896]{1,0:T(8,128)(2,1)}, u32[]{:S(2)}, u32[]{:S(2)}) collective-permute-start(bf16[480,896]{1,0:T(8,128)(2,1)} %maximum_select_fusion), channel_id=1, source_target_pairs={{0,4},{4,0},{8,12},{12,8},{16,20},{20,16},{24,28},{28,24},{32,36},... | collective-permute-start | bytes 2580488 | tf_op jit(solution)/shard_map/ppermute | solution.py:367
  50.2 1.4 fusion.expand_ref
  54.1 2.5 %collective-permute-start.15 = (bf16[192,896]{1,0:T(8,128)(2,1)}, bf16[192,896]{1,0:T(8,128)(2,1)S(1)}, u32[]{:S(2)}, u32[]{:S(2)}) collective-permute-start(bf16[192,896]{1,0:T(8,128)(2,1)} %copy-done.1), channel_id=1, source_target_pairs={{256,257},{257,258},{258,259},{259,256},{260,261},{261,262},{262,2... | collective-permute-start | bytes 1032200 | tf_op jit(solution)/shard_map/ppermute | solution.py:373
  56.6 1.2 copy-done.6
  57.8 1.2 copy-done.10
  59.0 1.8 %pooled_part.1.refs_6_ = bf16[192,1280]{1,0:T(8,128)(2,1)S(1)} custom-call(f32[192,1280]{1,0:T(8,128)S(1)} %copy-done.10, f32[192,1280]{1,0:T(8,128)S(1)} %copy-done.6, bf16[192,1280]{1,0:T(8,128)(2,1)} %collective-permute-done.14.other_ref, bf16[1280,1280]{1,0:T(8,128)(2,1)S(1)} %fusion.expand_ref), custom_call_target="tpu_custom_call" | custom-call | flops 5000000000 | bytes 8000000 | tf_op jit(solution)/shard_map/pooled_part/pallas_call | solution.py:303
  60.9 0.8 copy-done
  61.7 6.3 %collective-permute-done.15.refs_7_.refs_2_ = bf16[192,896]{1,0:T(8,128)(2,1)S(1)} collective-permute-done((bf16[192,896]{1,0:T(8,128)(2,1)}, bf16[192,896]{1,0:T(8,128)(2,1)S(1)}, u32[]{:S(2)}, u32[]{:S(2)}) %collective-permute-start.15) | collective-permute-done | bytes 344096 | tf_op jit(solution)/shard_map/ppermute | solution.py:373
  68.0 0.7 copy-done.11
  68.7 4.1 %tokens_part.1 = bf16[192,896]{1,0:T(8,128)(2,1)} custom-call(bf16[160,896]{1,0:T(8,128)(2,1)} %copy-done.16, bf16[160,896]{1,0:T(8,128)(2,1)} %copy-done.13, bf16[160,896]{1,0:T(8,128)(2,1)} %copy-done.14, bf16[160,896]{1,0:T(8,128)(2,1)} %copy-done.15, bf16[160,896]{1,0:T(8,128)(2,1)} %copy-done.22, bf16[480,896]{1,0:T(8,128)(2,1)} %collective-permute-done.13.refs_5_, ...), custom_call_target="tpu_custom_call" | custom-call | flops 880803840 | bytes 8000000 | tf_op jit(solution)/shard_map/tokens_part/pallas_call | solution.py:336
  72.8 1.3 collective-permute-start.16
  74.1 1.3 collective-permute-start.17
  75.4 1.3 collective-permute-start.18
  76.7 1.5 collective-permute-start.19
  78.2 0.8 fusion.1
  79.0 0.9 pad_maximum_fusion
  79.9 34.8 %collective-permute-done.16.refs_4_ = bf16[192,896]{1,0:T(8,128)(2,1)S(1)} collective-permute-done((bf16[192,896]{1,0:T(8,128)(2,1)}, bf16[192,896]{1,0:T(8,128)(2,1)S(1)}, u32[]{:S(2)}, u32[]{:S(2)}) %collective-permute-start.16) | collective-permute-done | bytes 344096 | tf_op jit(solution)/shard_map/ppermute | solution.py:405
  114.8 15.6 %collective-permute-done.18.refs_6_ = bf16[192,896]{1,0:T(8,128)(2,1)S(1)} collective-permute-done((bf16[192,896]{1,0:T(8,128)(2,1)}, bf16[192,896]{1,0:T(8,128)(2,1)S(1)}, u32[]{:S(2)}, u32[]{:S(2)}) %collective-permute-start.18) | collective-permute-done | bytes 344096 | tf_op jit(solution)/shard_map/ppermute | solution.py:405
  131.7 12.5 %decode.1 = bf16[192,896]{1,0:T(8,128)(2,1)} custom-call(s32[4]{0:T(128)} %and_select_fusion.order_ref, bf16[192,896]{1,0:T(8,128)(2,1)} %refs_0_.1, bf16[192,896]{1,0:T(8,128)(2,1)} %copy-done.2, bf16[192,896]{1,0:T(8,128)(2,1)} %copy-done.11, bf16[192,896]{1,0:T(8,128)(2,1)} %copy-done.1, bf16[192,896]{1,0:T(8,128)(2,1)} %copy-done.18, ...), custom_call_target="tpu_custom_call" | custom-call | flops 1585446912 | bytes 9633792 | tf_op jit(solution)/shard_map/decode/pallas_call | solution.py:110
  144.2 1.8 %select_bitcast_fusion = bf16[1,192,896]{2,1,0:T(8,128)(2,1)} fusion(bf16[192,896]{1,0:T(8,128)(2,1)S(1)} %copy-done.12, bf16[192,896]{1,0:T(8,128)(2,1)} %decode.1, pred[]{:T(512)S(6)} %eq.85), kind=kLoop, calls=%fused_computation.3 | loop fusion | flops 172032 | bytes 1032193 | tf_op jit(solution)/shard_map/broadcast_in_dim | solution.py:409
  (87 shorter events, 13.7 us)
Async XLA Ops:
  6.5 124.4 %all-gather.2.cloned.1.call-start = ((), (), s32[]{:S(2)}) async-start(), calls=%async_computation | async-start | bytes 8386560 | tf_op jit(solution)/shard_map/all_gather | solution.py:365
  7.3 25.6 %collective-permute-start.10 = (bf16[192,896]{1,0:T(8,128)(2,1)}, bf16[192,896]{1,0:T(8,128)(2,1)S(1)}, u32[]{:S(2)}, u32[]{:S(2)}) collective-permute-start(bf16[192,896]{1,0:T(8,128)(2,1)} %refs_0_.1), channel_id=1, source_target_pairs={{256,257},{257,258},{258,259},{259,256},{260,261},{261,262},{262,2... | collective-permute-start | bytes 1032200 | tf_op jit(solution)/shard_map/ppermute | solution.py:371
  13.4 19.5 %collective-permute-start.11 = (bf16[192,896]{1,0:T(8,128)(2,1)}, bf16[192,896]{1,0:T(8,128)(2,1)S(1)}, u32[]{:S(2)}, u32[]{:S(2)}) collective-permute-start(bf16[192,896]{1,0:T(8,128)(2,1)} %refs_0_.1), channel_id=1, source_target_pairs={{256,259},{257,256},{258,257},{259,258},{260,263},{261,260},{262,2... | collective-permute-start | bytes 1032200 | tf_op jit(solution)/shard_map/ppermute | solution.py:372
  19.2 11.5 %collective-permute-start.1 = (bf16[20,896]{1,0:T(8,128)(2,1)}, bf16[20,896]{1,0:T(8,128)(2,1)S(1)}, u32[]{:S(2)}, u32[]{:S(2)}) collective-permute-start(bf16[20,896]{1,0:T(8,128)(2,1)} %param.17), channel_id=1, source_target_pairs={{0,56},{4,60},{8,0},{12,4},{16,8},{20,12},{24,16},{28,20},{32,24},... | collective-permute-start | bytes 107528 | tf_op jit(solution)/shard_map/ppermute | solution.py:288
  19.9 11.5 %collective-permute-start = (bf16[20,896]{1,0:T(8,128)(2,1)}, bf16[20,896]{1,0:T(8,128)(2,1)S(1)}, u32[]{:S(2)}, u32[]{:S(2)}) collective-permute-start(bf16[20,896]{1,0:T(8,128)(2,1)} %param.17), channel_id=1, source_target_pairs={{0,8},{4,12},{8,16},{12,20},{16,24},{20,28},{24,32},{28,36},{32,40... | collective-permute-start | bytes 107528 | tf_op jit(solution)/shard_map/ppermute | solution.py:288
  21.9 1.5 %copy-start.3 = (bf16[768,1280]{1,0:T(8,128)(2,1)S(1)}, bf16[768,1280]{1,0:T(8,128)(2,1)}, u32[]{:S(2)}) copy-start(bf16[768,1280]{1,0:T(8,128)(2,1)} %audio_ref.1) | copy-start | bytes 5898244
  24.9 6.5 %copy-start.17 = (bf16[20,896]{1,0:T(8,128)(2,1)S(1)}, bf16[20,896]{1,0:T(8,128)(2,1)}, u32[]{:S(2)}) copy-start(bf16[20,896]{1,0:T(8,128)(2,1)} %param.17) | copy-start | bytes 107524
  24.9 7.9 %copy-start.7 = (bf16[320,1280]{1,0:T(8,128)(2,1)S(1)}, bf16[320,1280]{1,0:T(8,128)(2,1)}, u32[]{:S(2)}) copy-start(bf16[320,1280]{1,0:T(8,128)(2,1)} %pw_ref.1) | copy-start | bytes 2457604
  24.9 7.9 %copy-start.8 = (f32[31,320]{1,0:T(8,128)S(1)}, f32[31,320]{1,0:T(8,128)}, u32[]{:S(2)}) copy-start(f32[31,320]{1,0:T(8,128)} %taps_ref.1) | copy-start | bytes 119044
  29.7 2.5 %collective-permute-start.8 = (bf16[16,320]{1,0:T(8,128)(2,1)S(1)}, bf16[16,320]{1,0:T(8,128)(2,1)S(1)}, u32[]{:S(2)}, u32[]{:S(2)}) collective-permute-start(bf16[16,320]{1,0:T(8,128)(2,1)S(1)} %get-tuple-element.16), channel_id=1, source_target_pairs={{0,4},{4,8},{8,12},{12,16},{16,20},{20,24},{24,28},{28,32},{32,36}... | collective-permute-start | bytes 30728 | tf_op jit(solution)/shard_map/ppermute | solution.py:381
  30.7 2.1 %collective-permute-start.9 = (bf16[16,320]{1,0:T(8,128)(2,1)S(1)}, bf16[16,320]{1,0:T(8,128)(2,1)S(1)}, u32[]{:S(2)}, u32[]{:S(2)}) collective-permute-start(bf16[16,320]{1,0:T(8,128)(2,1)S(1)} %get-tuple-element.15), channel_id=1, source_target_pairs={{4,0},{8,4},{12,8},{16,12},{20,16},{24,20},{28,24},{32,28},{36,32}... | collective-permute-start | bytes 30728 | tf_op jit(solution)/shard_map/ppermute | solution.py:382
  31.4 9.1 %collective-permute-start.2 = (bf16[60,896]{1,0:T(8,128)(2,1)S(1)}, bf16[60,896]{1,0:T(8,128)(2,1)S(1)}, u32[]{:S(2)}, u32[]{:S(2)}) collective-permute-start(bf16[60,896]{1,0:T(8,128)(2,1)S(1)} %pad_maximum_fusion.2), channel_id=1, source_target_pairs={{0,40},{4,44},{8,48},{12,52},{16,56},{20,60},{24,0},{28,4},{32,8},... | collective-permute-start | bytes 322568 | tf_op jit(solution)/shard_map/ppermute | solution.py:288
  32.1 8.4 %collective-permute-start.3 = (bf16[40,896]{1,0:T(8,128)(2,1)S(1)}, bf16[40,896]{1,0:T(8,128)(2,1)S(1)}, u32[]{:S(2)}, u32[]{:S(2)}) collective-permute-start(bf16[40,896]{1,0:T(8,128)(2,1)S(1)} %pad_maximum_fusion.3), channel_id=1, source_target_pairs={{0,24},{4,28},{8,32},{12,36},{16,40},{20,44},{24,48},{28,52},{32,5... | collective-permute-start | bytes 215048 | tf_op jit(solution)/shard_map/ppermute | solution.py:288
  39.8 3.6 %collective-permute-start.12 = (bf16[192,1280]{1,0:T(8,128)(2,1)S(1)}, bf16[192,1280]{1,0:T(8,128)(2,1)S(1)}, u32[]{:S(2)}, u32[]{:S(2)}) collective-permute-start(bf16[192,1280]{1,0:T(8,128)(2,1)S(1)} %conv.1.a_ref), channel_id=1, source_target_pairs={{0,1},{1,0},{2,3},{3,2},{4,5},{5,4},{6,7},{7,6},{8,9},{9,8},{10,11... | collective-permute-start | bytes 1474568 | tf_op jit(solution)/shard_map/ppermute | solution.py:384
  41.0 7.6 %copy-start.16 = (bf16[160,896]{1,0:T(8,128)(2,1)}, bf16[160,896]{1,0:T(8,128)(2,1)S(1)}, u32[]{:S(2)}) copy-start(bf16[160,896]{1,0:T(8,128)(2,1)S(1)} %concatenate.99.refs_0_) | copy-start | bytes 860164
  41.0 6.3 %collective-permute-start.4 = (bf16[160,896]{1,0:T(8,128)(2,1)S(1)}, bf16[160,896]{1,0:T(8,128)(2,1)S(1)}, u32[]{:S(2)}, u32[]{:S(2)}) collective-permute-start(bf16[160,896]{1,0:T(8,128)(2,1)S(1)} %concatenate.99.refs_0_), channel_id=1, source_target_pairs={{0,64},{4,68},{8,72},{12,76},{16,80},{20,84},{24,88},{28,92},{32,9... | collective-permute-start | bytes 860168 | tf_op jit(solution)/shard_map/ppermute | solution.py:288
  41.7 5.6 %collective-permute-start.5 = (bf16[160,896]{1,0:T(8,128)(2,1)S(1)}, bf16[160,896]{1,0:T(8,128)(2,1)S(1)}, u32[]{:S(2)}, u32[]{:S(2)}) collective-permute-start(bf16[160,896]{1,0:T(8,128)(2,1)S(1)} %concatenate.99.refs_0_), channel_id=1, source_target_pairs={{0,192},{4,196},{8,200},{12,204},{16,208},{20,212},{24,216},{28,22... | collective-permute-start | bytes 860168 | tf_op jit(solution)/shard_map/ppermute | solution.py:288
  42.4 4.9 %collective-permute-start.6 = (bf16[160,896]{1,0:T(8,128)(2,1)S(1)}, bf16[160,896]{1,0:T(8,128)(2,1)S(1)}, u32[]{:S(2)}, u32[]{:S(2)}) collective-permute-start(bf16[160,896]{1,0:T(8,128)(2,1)S(1)} %concatenate.99.refs_0_), channel_id=1, source_target_pairs={{0,128},{4,132},{8,136},{12,140},{16,144},{20,148},{24,152},{28,15... | collective-permute-start | bytes 860168 | tf_op jit(solution)/shard_map/ppermute | solution.py:288
  45.3 11.3 %collective-permute-start.14 = (bf16[192,1280]{1,0:T(8,128)(2,1)}, bf16[192,1280]{1,0:T(8,128)(2,1)}, u32[]{:S(2)}, u32[]{:S(2)}) collective-permute-start(bf16[192,1280]{1,0:T(8,128)(2,1)} %get-tuple-element.14), channel_id=1, source_target_pairs={{1,2},{2,1},{3,0},{0,3},{5,6},{6,5},{7,4},{4,7},{9,10},{10,9},{11,... | collective-permute-start | bytes 1474568 | tf_op jit(solution)/shard_map/ppermute | solution.py:386
  48.6 3.0 %copy-start.23 = (f32[3584]{0:T(1024)S(1)}, f32[3584]{0:T(1024)}, u32[]{:S(2)}) copy-start(f32[3584]{0:T(1024)} %param.19) | copy-start | bytes 43012
  48.6 3.6 %copy-start.24 = (f32[1152]{0:T(1024)S(1)}, f32[1152]{0:T(1024)}, u32[]{:S(2)}) copy-start(f32[1152]{0:T(1024)} %param.21) | copy-start | bytes 13828
  48.6 19.4 %collective-permute-start.13 = (bf16[480,896]{1,0:T(8,128)(2,1)}, bf16[480,896]{1,0:T(8,128)(2,1)}, u32[]{:S(2)}, u32[]{:S(2)}) collective-permute-start(bf16[480,896]{1,0:T(8,128)(2,1)} %maximum_select_fusion), channel_id=1, source_target_pairs={{0,4},{4,0},{8,12},{12,8},{16,20},{20,16},{24,28},{28,24},{32,36},... | collective-permute-start | bytes 2580488 | tf_op jit(solution)/shard_map/ppermute | solution.py:367
  53.5 8.2 %collective-permute-start.7 = (bf16[160,896]{1,0:T(8,128)(2,1)}, bf16[160,896]{1,0:T(8,128)(2,1)S(1)}, u32[]{:S(2)}, u32[]{:S(2)}) collective-permute-start(bf16[160,896]{1,0:T(8,128)(2,1)} %copy-done.16), channel_id=1, source_target_pairs={{0,4},{4,0},{8,12},{12,8},{16,20},{20,16},{24,28},{28,24},{32,36},... | collective-permute-start | bytes 860168 | tf_op jit(solution)/shard_map/ppermute | solution.py:367
  54.1 13.8 %collective-permute-start.15 = (bf16[192,896]{1,0:T(8,128)(2,1)}, bf16[192,896]{1,0:T(8,128)(2,1)S(1)}, u32[]{:S(2)}, u32[]{:S(2)}) collective-permute-start(bf16[192,896]{1,0:T(8,128)(2,1)} %copy-done.1), channel_id=1, source_target_pairs={{256,257},{257,258},{258,259},{259,256},{260,261},{261,262},{262,2... | collective-permute-start | bytes 1032200 | tf_op jit(solution)/shard_map/ppermute | solution.py:373
  61.7 6.3 %copy-start.22 = (bf16[160,896]{1,0:T(8,128)(2,1)}, bf16[160,896]{1,0:T(8,128)(2,1)S(1)}, u32[]{:S(2)}) copy-start(bf16[160,896]{1,0:T(8,128)(2,1)S(1)} %collective-permute-done.7.refs_4_) | copy-start | bytes 860164
  72.8 41.9 %collective-permute-start.16 = (bf16[192,896]{1,0:T(8,128)(2,1)}, bf16[192,896]{1,0:T(8,128)(2,1)S(1)}, u32[]{:S(2)}, u32[]{:S(2)}) collective-permute-start(bf16[192,896]{1,0:T(8,128)(2,1)} %tokens_part.1), channel_id=1, source_target_pairs={{0,256},{1,257},{2,258},{3,259},{4,260},{5,261},{6,262},{7,263},{8... | collective-permute-start | bytes 1032200 | tf_op jit(solution)/shard_map/ppermute | solution.py:405
  74.1 40.6 %collective-permute-start.17 = (bf16[192,896]{1,0:T(8,128)(2,1)}, bf16[192,896]{1,0:T(8,128)(2,1)S(1)}, u32[]{:S(2)}, u32[]{:S(2)}) collective-permute-start(bf16[192,896]{1,0:T(8,128)(2,1)} %tokens_part.1), channel_id=1, source_target_pairs={{0,259},{1,256},{2,257},{3,258},{4,263},{5,260},{6,261},{7,262},{8... | collective-permute-start | bytes 1032200 | tf_op jit(solution)/shard_map/ppermute | solution.py:405
  75.4 54.9 %collective-permute-start.18 = (bf16[192,896]{1,0:T(8,128)(2,1)}, bf16[192,896]{1,0:T(8,128)(2,1)S(1)}, u32[]{:S(2)}, u32[]{:S(2)}) collective-permute-start(bf16[192,896]{1,0:T(8,128)(2,1)} %tokens_part.1), channel_id=1, source_target_pairs={{0,258},{1,259},{2,256},{3,257},{4,262},{5,263},{6,260},{7,261},{8... | collective-permute-start | bytes 1032200 | tf_op jit(solution)/shard_map/ppermute | solution.py:405
  76.7 54.2 %collective-permute-start.19 = (bf16[192,896]{1,0:T(8,128)(2,1)}, bf16[192,896]{1,0:T(8,128)(2,1)S(1)}, u32[]{:S(2)}, u32[]{:S(2)}) collective-permute-start(bf16[192,896]{1,0:T(8,128)(2,1)} %tokens_part.1), channel_id=1, source_target_pairs={{0,257},{1,258},{2,259},{3,256},{4,261},{5,262},{6,263},{7,260},{8... | collective-permute-start | bytes 1032200 | tf_op jit(solution)/shard_map/ppermute | solution.py:405
  114.8 16.2 %copy-start.18 = (bf16[192,896]{1,0:T(8,128)(2,1)}, bf16[192,896]{1,0:T(8,128)(2,1)S(1)}, u32[]{:S(2)}) copy-start(bf16[192,896]{1,0:T(8,128)(2,1)S(1)} %collective-permute-done.16.refs_4_) | copy-start | bytes 1032196
  114.8 16.2 %copy-start.19 = (bf16[192,896]{1,0:T(8,128)(2,1)}, bf16[192,896]{1,0:T(8,128)(2,1)S(1)}, u32[]{:S(2)}) copy-start(bf16[192,896]{1,0:T(8,128)(2,1)S(1)} %collective-permute-done.17.refs_5_) | copy-start | bytes 1032196
  131.7 12.5 %copy-start.12 = (bf16[192,896]{1,0:T(8,128)(2,1)S(1)}, bf16[192,896]{1,0:T(8,128)(2,1)}, u32[]{:S(2)}) copy-start(bf16[192,896]{1,0:T(8,128)(2,1)} %tokens_part.1) | copy-start | bytes 1032196
  (14 other events, 14.0 us)
Sparse Core Ops, SparseCore 0:
  10.6 92.6 all-gather.1

commit v7 on v5

--- a/solution.py
+++ b/solution.py
@@ -28,46 +28,33 @@
     return values * cosine + pltpu.roll(values, HEAD // 2, 1) * sine
 
 
-def prepare_kernel(order_ref, *refs, parts):
+def decode_kernel(
+    order_ref, *refs, parts
+):
     ins = refs[: 2 * parts]
-    gain_ref, rows_ref, scale_ref = refs[2 * parts : 2 * parts + 3]
-    count = ins[0].shape[0]
-    for first, blocks in ((0, ins[:parts]), (count, ins[parts:])):
-        square = jnp.zeros((count, 1), jnp.float32)
-        for i, ref in enumerate(blocks):
-            block = order_ref[i]
-            x = ref[...].astype(jnp.float32)
-            square = square + jnp.sum(x * x, axis=1, keepdims=True)
-            rows_ref[block, first : first + count] = (x * gain_ref[block]).astype(jnp.bfloat16)
-        scale_ref[first : first + count] = lax.rsqrt(square / (parts * ins[0].shape[1]) + 1e-6)
-
-
-def prepare(order, words, sounds, gain):
-    parts = len(words)
-    count, width = words[0].shape
-    vmem = pl.BlockSpec(memory_space=pltpu.VMEM)
-    return pl.pallas_call(
-        functools.partial(prepare_kernel, parts=parts),
-        in_specs=[pl.BlockSpec(memory_space=pltpu.SMEM)] + [vmem] * (2 * parts + 1),
-        out_specs=[vmem, vmem],
-        out_shape=[
-            jax.ShapeDtypeStruct((parts, 2 * count, width), jnp.bfloat16),
-            jax.ShapeDtypeStruct((2 * count, 1), jnp.float32),
-        ],
-        compiler_params=pltpu.CompilerParams(vmem_limit_bytes=16 * MIB),
-        cost_estimate=pl.CostEstimate(
-            flops=8 * count * parts * width, bytes_accessed=8 * count * parts * width, transcendentals=0
-        ),
-        name="prepare",
-    )(order, *words, *sounds, gain)
-
-
-def decode_kernel(rows_ref, scale_ref, w_ref, bias_ref, cos_ref, sin_ref, out_ref, acc, acc_kv):
+    gain_ref, w_ref, bias_ref, cos_ref, sin_ref, out_ref, held, rows, scales, acc, acc_kv, sem = refs[2 * parts :]
     step = pl.program_id(0)
     count, total = acc.shape
     heads = total // HEAD - 2
-    text = jnp.dot(rows_ref[0, :count], w_ref[...], preferred_element_type=jnp.float32)
-    audio = jnp.dot(rows_ref[0, count:], w_ref[:, heads * HEAD :], preferred_element_type=jnp.float32)
+    width = held.shape[2]
+
+    @pl.when(step == 0)
+    def _():
+        copies = [pltpu.make_async_copy(ref, held.at[i], sem.at[i]) for i, ref in enumerate(ins)]
+        for copy in copies:
+            copy.start()
+        for first, side in ((0, 0), (count, parts)):
+            square = jnp.zeros((count, 1), jnp.float32)
+            for i in range(parts):
+                copies[side + i].wait()
+                block = order_ref[i]
+                x = held[side + i].astype(jnp.float32)
+                square = square + jnp.sum(x * x, axis=1, keepdims=True)
+                rows[block, first : first + count] = (x * gain_ref[block]).astype(jnp.bfloat16)
+            scales[first : first + count] = lax.rsqrt(square / (parts * width) + 1e-6)
+
+    text = jnp.dot(rows[step, :count], w_ref[...], preferred_element_type=jnp.float32)
+    audio = jnp.dot(rows[step, count:], w_ref[:, heads * HEAD :], preferred_element_type=jnp.float32)
 
     @pl.when(step == 0)
     def _():
@@ -81,7 +68,7 @@
 
     @pl.when(step == pl.num_programs(0) - 1)
     def _():
-        scale, scale_kv = scale_ref[:count], scale_ref[count:]
+        scale, scale_kv = scales[:count], scales[count:]
         cosine, sine = cos_ref[count:], sin_ref[count:]
         key_cols = slice(heads * HEAD, (heads + 1) * HEAD)
         value_cols = slice((heads + 1) * HEAD, total)
@@ -114,18 +101,19 @@
             ).astype(jnp.bfloat16)
 
 
-def decode(rows, scale, weight, bias, tables):
-    parts, count, width = rows.shape
-    count //= 2
+def decode(order, words, sounds, gain, weight, bias, tables):
+    parts = len(words)
+    count, width = words[0].shape
     total = weight.shape[1]
     columns = total - 2 * HEAD
     whole = lambda *shape: pl.BlockSpec(shape, lambda k: (0,) * len(shape))
     return pl.pallas_call(
-        decode_kernel,
+        functools.partial(decode_kernel, parts=parts),
         grid=(parts,),
-        in_specs=[
-            pl.BlockSpec((1, 2 * count, width), lambda k: (k, 0, 0)),
-            whole(2 * count, 1),
+        in_specs=[pl.BlockSpec(memory_space=pltpu.SMEM)]
+        + [pl.BlockSpec(memory_space=pl.ANY)] * (2 * parts)
+        + [
+            whole(parts, 1, width),
             pl.BlockSpec((width, total), lambda k: (k, 0)),
             whole(1, total),
             whole(2 * count, HEAD),
@@ -133,8 +121,12 @@
         ],
         out_specs=whole(count, columns),
         scratch_shapes=[
+            pltpu.VMEM((2 * parts, count, width), jnp.bfloat16),
+            pltpu.VMEM((parts, 2 * count, width), jnp.bfloat16),
+            pltpu.VMEM((2 * count, 1), jnp.float32),
             pltpu.VMEM((count, total), jnp.float32),
             pltpu.VMEM((count, 2 * HEAD), jnp.float32),
+            pltpu.SemaphoreType.DMA((2 * parts,)),
         ],
         out_shape=jax.ShapeDtypeStruct((count, columns), jnp.bfloat16),
         compiler_params=pltpu.CompilerParams(vmem_limit_bytes=56 * MIB),
@@ -142,7 +134,7 @@
             flops=2 * count * parts * width * total, bytes_accessed=2 * parts * width * (total + count), transcendentals=0
         ),
         name="decode",
-    )(rows, scale, weight, bias, *tables)
+    )(order, *words, *sounds, gain, weight, bias, *tables)
 
 
 def pooling(rows):
@@ -365,8 +357,7 @@
     across = lax.ppermute(following, both, ring(1, -1))
     last = lax.ppermute(same, both, ring(1, 1))
     sounds = [same, following, across, last]
-    prepared, scale = prepare(order, words, sounds, gain)
-    context = decode(prepared, scale, weight, qkv_bias[None], tables)
+    context = decode(order, words, sounds, gain, weight, qkv_bias[None], tables)
     return jnp.where(grp == 0, tokens, context)[None]
 
 

time: 147 us -> 146 us (level)
  the two profiles are of different devices: /device:TPU:122 before, /device:TPU:90 now
where the time goes in v7:
time: 146 us; the launch traced here: 145 us
  waiting for transfers between devices  58.1 us (40%)
  starting transfers between devices  34.2 us (23%)
  Pallas kernels  23.3 us (16%)
  between operations  14.7 us (10%)
  local copies, waits for them, and re-layouts  7.67 us (5%)
  other arithmetic  6.87 us (5%)
    ppermute x1, waiting for transfers between devices, shards(): lax.ppermute(tokens, both, [(i, n_mdl + (i - 1) % n_mdl) for i in range(n...  43 us
    pallas_call x1, Pallas kernels, decode(): pl.pallas_call(functools.partial(decode_kernel, parts=parts), grid=(parts...  12.4 us
    ppermute x1, waiting for transfers between devices, shards(): second = lax.ppermute(behind, both, ring(1, 1))  7.04 us
    ppermute x1, starting transfers between devices, shards(): behind = lax.ppermute(text, both, ring(1, 1))  6.09 us
    ppermute x1, starting transfers between devices, shards(): ahead = lax.ppermute(text, both, ring(1, -1))  5.87 us
    pallas_call x1, Pallas kernels, conv(): pl.pallas_call(conv_kernel, in_specs=[vmem] * 5 + [pl.BlockSpec(memory_sp...  5.53 us
    unnamed x28, local copies, waits for them, and re-layouts  5.02 us
    ppermute x7, starting transfers between devices, spread(): lax.ppermute(v, ('grp', 'seq'), of_group(0, place(dx, dy)))  4.7 us
  transfers between devices with their start and end apart: 21, of which 4 were waited for; matrix products, arithmetic and copies ran while one was open for 5% of the time, Pallas kernels for 7%

profile of v7, /device:TPU:90, one launch (start us, length us, event | category | flops | bytes accessed | tf_op | source)
XLA Modules:
  0.0 144.9 jit_solution(5192286580106978652)
XLA Ops:
  6.5 0.7 all-gather.2.cloned.1.call-update
  7.3 6.1 %collective-permute-start.11 = (bf16[192,896]{1,0:T(8,128)(2,1)}, bf16[192,896]{1,0:T(8,128)(2,1)S(1)}, u32[]{:S(2)}, u32[]{:S(2)}) collective-permute-start(bf16[192,896]{1,0:T(8,128)(2,1)} %refs_0_.1), channel_id=1, source_target_pairs={{256,257},{257,258},{258,259},{259,256},{260,261},{261,262},{262,2... | collective-permute-start | bytes 1032200 | tf_op jit(solution)/shard_map/ppermute | solution.py:323
  13.4 5.9 %collective-permute-start.12 = (bf16[192,896]{1,0:T(8,128)(2,1)}, bf16[192,896]{1,0:T(8,128)(2,1)S(1)}, u32[]{:S(2)}, u32[]{:S(2)}) collective-permute-start(bf16[192,896]{1,0:T(8,128)(2,1)} %refs_0_.1), channel_id=1, source_target_pairs={{256,259},{257,256},{258,257},{259,258},{260,263},{261,260},{262,2... | collective-permute-start | bytes 1032200 | tf_op jit(solution)/shard_map/ppermute | solution.py:324
  21.2 0.7 broadcast_in_dim.6.gain_ref
  21.9 1.5 %copy-done.3 = bf16[768,1280]{1,0:T(8,128)(2,1)S(1)} copy-done((bf16[768,1280]{1,0:T(8,128)(2,1)S(1)}, bf16[768,1280]{1,0:T(8,128)(2,1)}, u32[]{:S(2)}) %copy-start.3) | copy-done | bytes 1966104
  23.5 1.4 copy-done.4
  24.9 3.8 %gate.1 = (bf16[768,320]{1,0:T(8,128)(2,1)S(1)}, f32[192,1280]{1,0:T(8,128)S(1)}) custom-call(s32[1]{0:T(128)S(6)} %sub.20.count_ref, bf16[768,1280]{1,0:T(8,128)(2,1)S(1)} %copy-done.3, f32[1,1280]{1,0:T(1,128)S(1)} %broadcast_in_dim.6.gain_ref, bf16[2,320,1280]{2,1,0:T(8,128)(2,1)S(1)} %bitcast.36), custom_call_target="tpu_custom_call" | custom-call | flops 1258291200 | bytes 7864320 | tf_op jit(solution)/shard_map/gate/pallas_call | solution.py:168
  32.0 1.3 copy-done.5
  33.2 5.5 %conv.1 = bf16[192,1280]{1,0:T(8,128)(2,1)S(1)} custom-call(bf16[16,320]{1,0:T(8,128)(2,1)S(1)} %collective-permute-done.9.before_ref, bf16[768,320]{1,0:T(8,128)(2,1)S(1)} %get-tuple-element.8.gated_ref, bf16[16,320]{1,0:T(8,128)(2,1)S(1)} %collective-permute-done.10.after_ref, f32[31,320]{1,0:T(8,128)S(1)} %copy-done.6, bf16[320,1280]{1,0:T(8,128)(2,1)S(1)} %copy-done.5, ...), custom_call_target="tpu_custom_call" | custom-call | flops 5000000000 | bytes 1966080 | tf_op jit(solution)/shard_map/conv/pallas_call | solution.py:230
  38.8 1.5 %collective-permute-start.13 = (bf16[192,1280]{1,0:T(8,128)(2,1)S(1)}, bf16[192,1280]{1,0:T(8,128)(2,1)}, u32[]{:S(2)}, u32[]{:S(2)}) collective-permute-start(bf16[192,1280]{1,0:T(8,128)(2,1)S(1)} %conv.1), channel_id=1, source_target_pairs={{0,1},{1,0},{2,3},{3,2},{4,5},{5,4},{6,7},{7,6},{8,9},{9,8},{10,11... | collective-permute-start | bytes 1474568 | tf_op jit(solution)/shard_map/ppermute | solution.py:336
  40.8 0.7 collective-permute-start.4
  41.5 0.7 collective-permute-start.5
  42.2 0.7 collective-permute-start.6
  43.8 2.5 %collective-permute-start.15 = (bf16[192,896]{1,0:T(8,128)(2,1)S(1)}, bf16[192,896]{1,0:T(8,128)(2,1)S(1)}, u32[]{:S(2)}, u32[]{:S(2)}) collective-permute-start(bf16[192,896]{1,0:T(8,128)(2,1)S(1)} %collective-permute-done.11.refs_0_.refs_3_), channel_id=1, source_target_pairs={{256,257},{257,258},{258,259},{259,256},{260,261},{261,262},{262,2... | collective-permute-start | bytes 1032200 | tf_op jit(solution)/shard_map/ppermute | solution.py:325
  46.4 0.7 collective-permute-start.8
  47.1 1.1 fusion.3
  48.3 0.7 collective-permute-start.14
  49.0 1.4 fusion.refs_9_
  50.4 7.0 %collective-permute-done.15.refs_10_.refs_2_ = bf16[192,896]{1,0:T(8,128)(2,1)S(1)} collective-permute-done((bf16[192,896]{1,0:T(8,128)(2,1)S(1)}, bf16[192,896]{1,0:T(8,128)(2,1)S(1)}, u32[]{:S(2)}, u32[]{:S(2)}) %collective-permute-start.15) | collective-permute-done | bytes 344096 | tf_op jit(solution)/shard_map/ppermute | solution.py:325
  57.5 1.5 %tokens_part.1 = bf16[192,896]{1,0:T(8,128)(2,1)S(1)} custom-call(bf16[160,896]{1,0:T(8,128)(2,1)S(1)} %concatenate.99.refs_0_, bf16[160,896]{1,0:T(8,128)(2,1)S(1)} %collective-permute-done.4.refs_1_, bf16[160,896]{1,0:T(8,128)(2,1)S(1)} %collective-permute-done.5.refs_2_, bf16[160,896]{1,0:T(8,128)(2,1)S(1)} %collective-permute-done.6.refs_3_, ...), custom_call_target="tpu_custom_call" | custom-call | flops 880803840 | bytes 8000000 | tf_op jit(solution)/shard_map/tokens_part/pallas_call | solution.py:291
  59.0 1.3 collective-permute-start.17
  60.3 1.3 collective-permute-start.16
  63.4 43.0 %collective-permute-done.17.refs_5_ = bf16[192,896]{1,0:T(8,128)(2,1)S(1)} collective-permute-done((bf16[192,896]{1,0:T(8,128)(2,1)S(1)}, bf16[192,896]{1,0:T(8,128)(2,1)S(1)}, u32[]{:S(2)}, u32[]{:S(2)}) %collective-permute-start.17) | collective-permute-done | bytes 344096 | tf_op jit(solution)/shard_map/ppermute | solution.py:356
  106.4 3.6 %collective-permute-start.18 = (bf16[192,896]{1,0:T(8,128)(2,1)S(1)}, bf16[192,896]{1,0:T(8,128)(2,1)S(1)}, u32[]{:S(2)}, u32[]{:S(2)}) collective-permute-start(bf16[192,896]{1,0:T(8,128)(2,1)S(1)} %collective-permute-done.17.refs_5_), channel_id=1, source_target_pairs={{256,259},{257,256},{258,257},{259,258},{260,263},{261,260},{262,2... | collective-permute-start | bytes 1032200 | tf_op jit(solution)/shard_map/ppermute | solution.py:357
  110.0 4.0 %collective-permute-start.19 = (bf16[192,896]{1,0:T(8,128)(2,1)S(1)}, bf16[192,896]{1,0:T(8,128)(2,1)S(1)}, u32[]{:S(2)}, u32[]{:S(2)}) collective-permute-start(bf16[192,896]{1,0:T(8,128)(2,1)S(1)} %collective-permute-done.16.refs_4_), channel_id=1, source_target_pairs={{256,257},{257,258},{258,259},{259,256},{260,261},{261,262},{262,2... | collective-permute-start | bytes 1032200 | tf_op jit(solution)/shard_map/ppermute | solution.py:358
  114.1 0.8 fusion.1
  114.8 0.9 pad_maximum_fusion.1
  115.8 3.6 %collective-permute-done.18.refs_6_ = bf16[192,896]{1,0:T(8,128)(2,1)S(1)} collective-permute-done((bf16[192,896]{1,0:T(8,128)(2,1)S(1)}, bf16[192,896]{1,0:T(8,128)(2,1)S(1)}, u32[]{:S(2)}, u32[]{:S(2)}) %collective-permute-start.18) | collective-permute-done | bytes 344096 | tf_op jit(solution)/shard_map/ppermute | solution.py:357
  119.3 3.8 %collective-permute-done.19.refs_7_ = bf16[192,896]{1,0:T(8,128)(2,1)S(1)} collective-permute-done((bf16[192,896]{1,0:T(8,128)(2,1)S(1)}, bf16[192,896]{1,0:T(8,128)(2,1)S(1)}, u32[]{:S(2)}, u32[]{:S(2)}) %collective-permute-start.19) | collective-permute-done | bytes 344096 | tf_op jit(solution)/shard_map/ppermute | solution.py:358
  123.1 0.7 copy-done.11
  123.9 12.4 %decode.1 = bf16[192,896]{1,0:T(8,128)(2,1)} custom-call(s32[4]{0:T(128)} %and_select_fusion.order_ref, bf16[192,896]{1,0:T(8,128)(2,1)} %refs_0_.1, bf16[192,896]{1,0:T(8,128)(2,1)} %copy-done.2, bf16[192,896]{1,0:T(8,128)(2,1)} %copy-done, bf16[192,896]{1,0:T(8,128)(2,1)} %copy-done.1, bf16[192,896]{1,0:T(8,128)(2,1)} %copy-done.9, ...), custom_call_target="tpu_custom_call" | custom-call | flops 1585446912 | bytes 9633792 | tf_op jit(solution)/shard_map/decode/pallas_call | solution.py:110
  136.3 1.8 %select_bitcast_fusion = bf16[1,192,896]{2,1,0:T(8,128)(2,1)} fusion(bf16[192,896]{1,0:T(8,128)(2,1)S(1)} %tokens_part.1, bf16[192,896]{1,0:T(8,128)(2,1)} %decode.1, pred[]{:T(512)S(6)} %eq.85), kind=kLoop, calls=%fused_computation.4 | loop fusion | flops 172032 | bytes 1032193 | tf_op jit(solution)/shard_map/broadcast_in_dim | solution.py:361
  (64 shorter events, 7.6 us)
Async XLA Ops:
  6.5 116.6 %all-gather.2.cloned.1.call-start = ((), (), s32[]{:S(2)}) async-start(), calls=%async_computation | async-start | bytes 8386560 | tf_op jit(solution)/shard_map/all_gather | solution.py:317
  7.3 24.7 %collective-permute-start.11 = (bf16[192,896]{1,0:T(8,128)(2,1)}, bf16[192,896]{1,0:T(8,128)(2,1)S(1)}, u32[]{:S(2)}, u32[]{:S(2)}) collective-permute-start(bf16[192,896]{1,0:T(8,128)(2,1)} %refs_0_.1), channel_id=1, source_target_pairs={{256,257},{257,258},{258,259},{259,256},{260,261},{261,262},{262,2... | collective-permute-start | bytes 1032200 | tf_op jit(solution)/shard_map/ppermute | solution.py:323
  13.4 18.6 %collective-permute-start.12 = (bf16[192,896]{1,0:T(8,128)(2,1)}, bf16[192,896]{1,0:T(8,128)(2,1)S(1)}, u32[]{:S(2)}, u32[]{:S(2)}) collective-permute-start(bf16[192,896]{1,0:T(8,128)(2,1)} %refs_0_.1), channel_id=1, source_target_pairs={{256,259},{257,256},{258,257},{259,258},{260,263},{261,260},{262,2... | collective-permute-start | bytes 1032200 | tf_op jit(solution)/shard_map/ppermute | solution.py:324
  19.2 10.6 %collective-permute-start.1 = (bf16[20,896]{1,0:T(8,128)(2,1)}, bf16[20,896]{1,0:T(8,128)(2,1)S(1)}, u32[]{:S(2)}, u32[]{:S(2)}) collective-permute-start(bf16[20,896]{1,0:T(8,128)(2,1)} %param.17), channel_id=1, source_target_pairs={{0,56},{4,60},{8,0},{12,4},{16,8},{20,12},{24,16},{28,20},{32,24},... | collective-permute-start | bytes 107528 | tf_op jit(solution)/shard_map/ppermute | solution.py:265
  19.9 10.6 %collective-permute-start = (bf16[20,896]{1,0:T(8,128)(2,1)}, bf16[20,896]{1,0:T(8,128)(2,1)S(1)}, u32[]{:S(2)}, u32[]{:S(2)}) collective-permute-start(bf16[20,896]{1,0:T(8,128)(2,1)} %param.17), channel_id=1, source_target_pairs={{0,8},{4,12},{8,16},{12,20},{16,24},{20,28},{24,32},{28,36},{32,40... | collective-permute-start | bytes 107528 | tf_op jit(solution)/shard_map/ppermute | solution.py:265
  21.9 1.5 %copy-start.3 = (bf16[768,1280]{1,0:T(8,128)(2,1)S(1)}, bf16[768,1280]{1,0:T(8,128)(2,1)}, u32[]{:S(2)}) copy-start(bf16[768,1280]{1,0:T(8,128)(2,1)} %audio_ref.1) | copy-start | bytes 5898244
  24.9 5.6 %copy-start.7 = (bf16[20,896]{1,0:T(8,128)(2,1)S(1)}, bf16[20,896]{1,0:T(8,128)(2,1)}, u32[]{:S(2)}) copy-start(bf16[20,896]{1,0:T(8,128)(2,1)} %param.17) | copy-start | bytes 107524
  24.9 7.1 %copy-start.6 = (f32[31,320]{1,0:T(8,128)S(1)}, f32[31,320]{1,0:T(8,128)}, u32[]{:S(2)}) copy-start(f32[31,320]{1,0:T(8,128)} %taps_ref.1) | copy-start | bytes 119044
  28.8 2.5 %collective-permute-start.10 = (bf16[16,320]{1,0:T(8,128)(2,1)S(1)}, bf16[16,320]{1,0:T(8,128)(2,1)S(1)}, u32[]{:S(2)}, u32[]{:S(2)}) collective-permute-start(bf16[16,320]{1,0:T(8,128)(2,1)S(1)} %get-tuple-element.11), channel_id=1, source_target_pairs={{4,0},{8,4},{12,8},{16,12},{20,16},{24,20},{28,24},{32,28},{36,32}... | collective-permute-start | bytes 30728 | tf_op jit(solution)/shard_map/ppermute | solution.py:334
  29.8 2.1 %collective-permute-start.9 = (bf16[16,320]{1,0:T(8,128)(2,1)S(1)}, bf16[16,320]{1,0:T(8,128)(2,1)S(1)}, u32[]{:S(2)}, u32[]{:S(2)}) collective-permute-start(bf16[16,320]{1,0:T(8,128)(2,1)S(1)} %get-tuple-element.12), channel_id=1, source_target_pairs={{0,4},{4,8},{8,12},{12,16},{16,20},{20,24},{24,28},{28,32},{32,36}... | collective-permute-start | bytes 30728 | tf_op jit(solution)/shard_map/ppermute | solution.py:333
  30.5 9.7 %collective-permute-start.2 = (bf16[60,896]{1,0:T(8,128)(2,1)S(1)}, bf16[60,896]{1,0:T(8,128)(2,1)S(1)}, u32[]{:S(2)}, u32[]{:S(2)}) collective-permute-start(bf16[60,896]{1,0:T(8,128)(2,1)S(1)} %pad_maximum_fusion.3), channel_id=1, source_target_pairs={{0,40},{4,44},{8,48},{12,52},{16,56},{20,60},{24,0},{28,4},{32,8},... | collective-permute-start | bytes 322568 | tf_op jit(solution)/shard_map/ppermute | solution.py:265
  31.3 9.0 %collective-permute-start.3 = (bf16[40,896]{1,0:T(8,128)(2,1)S(1)}, bf16[40,896]{1,0:T(8,128)(2,1)S(1)}, u32[]{:S(2)}, u32[]{:S(2)}) collective-permute-start(bf16[40,896]{1,0:T(8,128)(2,1)S(1)} %pad_maximum_fusion.4), channel_id=1, source_target_pairs={{0,24},{4,28},{8,32},{12,36},{16,40},{20,44},{24,48},{28,52},{32,5... | collective-permute-start | bytes 215048 | tf_op jit(solution)/shard_map/ppermute | solution.py:265
  31.9 11.9 %copy-start.1 = (bf16[192,896]{1,0:T(8,128)(2,1)}, bf16[192,896]{1,0:T(8,128)(2,1)S(1)}, u32[]{:S(2)}) copy-start(bf16[192,896]{1,0:T(8,128)(2,1)S(1)} %collective-permute-done.11.refs_0_.refs_3_) | copy-start | bytes 1032196
  33.2 5.5 %copy-start.2 = (bf16[192,896]{1,0:T(8,128)(2,1)}, bf16[192,896]{1,0:T(8,128)(2,1)S(1)}, u32[]{:S(2)}) copy-start(bf16[192,896]{1,0:T(8,128)(2,1)S(1)} %collective-permute-done.12.refs_1_) | copy-start | bytes 1032196
  38.8 8.3 %collective-permute-start.13 = (bf16[192,1280]{1,0:T(8,128)(2,1)S(1)}, bf16[192,1280]{1,0:T(8,128)(2,1)}, u32[]{:S(2)}, u32[]{:S(2)}) collective-permute-start(bf16[192,1280]{1,0:T(8,128)(2,1)S(1)} %conv.1), channel_id=1, source_target_pairs={{0,1},{1,0},{2,3},{3,2},{4,5},{5,4},{6,7},{7,6},{8,9},{9,8},{10,11... | collective-permute-start | bytes 1474568 | tf_op jit(solution)/shard_map/ppermute | solution.py:336
  40.8 3.0 %collective-permute-start.4 = (bf16[160,896]{1,0:T(8,128)(2,1)S(1)}, bf16[160,896]{1,0:T(8,128)(2,1)S(1)}, u32[]{:S(2)}, u32[]{:S(2)}) collective-permute-start(bf16[160,896]{1,0:T(8,128)(2,1)S(1)} %concatenate.99.refs_0_), channel_id=1, source_target_pairs={{0,64},{4,68},{8,72},{12,76},{16,80},{20,84},{24,88},{28,92},{32,9... | collective-permute-start | bytes 860168 | tf_op jit(solution)/shard_map/ppermute | solution.py:265
  41.5 4.8 %collective-permute-start.5 = (bf16[160,896]{1,0:T(8,128)(2,1)S(1)}, bf16[160,896]{1,0:T(8,128)(2,1)S(1)}, u32[]{:S(2)}, u32[]{:S(2)}) collective-permute-start(bf16[160,896]{1,0:T(8,128)(2,1)S(1)} %concatenate.99.refs_0_), channel_id=1, source_target_pairs={{0,192},{4,196},{8,200},{12,204},{16,208},{20,212},{24,216},{28,22... | collective-permute-start | bytes 860168 | tf_op jit(solution)/shard_map/ppermute | solution.py:265
  42.2 4.1 %collective-permute-start.6 = (bf16[160,896]{1,0:T(8,128)(2,1)S(1)}, bf16[160,896]{1,0:T(8,128)(2,1)S(1)}, u32[]{:S(2)}, u32[]{:S(2)}) collective-permute-start(bf16[160,896]{1,0:T(8,128)(2,1)S(1)} %concatenate.99.refs_0_), channel_id=1, source_target_pairs={{0,128},{4,132},{8,136},{12,140},{16,144},{20,148},{24,152},{28,15... | collective-permute-start | bytes 860168 | tf_op jit(solution)/shard_map/ppermute | solution.py:265
  43.1 7.3 %collective-permute-start.7 = (bf16[160,896]{1,0:T(8,128)(2,1)S(1)}, bf16[160,896]{1,0:T(8,128)(2,1)S(1)}, u32[]{:S(2)}, u32[]{:S(2)}) collective-permute-start(bf16[160,896]{1,0:T(8,128)(2,1)S(1)} %concatenate.99.refs_0_), channel_id=1, source_target_pairs={{0,4},{4,0},{8,12},{12,8},{16,20},{20,16},{24,28},{28,24},{32,36},... | collective-permute-start | bytes 860168 | tf_op jit(solution)/shard_map/ppermute | solution.py:319
  43.8 13.6 %collective-permute-start.15 = (bf16[192,896]{1,0:T(8,128)(2,1)S(1)}, bf16[192,896]{1,0:T(8,128)(2,1)S(1)}, u32[]{:S(2)}, u32[]{:S(2)}) collective-permute-start(bf16[192,896]{1,0:T(8,128)(2,1)S(1)} %collective-permute-done.11.refs_0_.refs_3_), channel_id=1, source_target_pairs={{256,257},{257,258},{258,259},{259,256},{260,261},{261,262},{262,2... | collective-permute-start | bytes 1032200 | tf_op jit(solution)/shard_map/ppermute | solution.py:325
  46.4 11.0 %collective-permute-start.8 = (bf16[480,896]{1,0:T(8,128)(2,1)S(1)}, bf16[480,896]{1,0:T(8,128)(2,1)S(1)}, u32[]{:S(2)}, u32[]{:S(2)}) collective-permute-start(bf16[480,896]{1,0:T(8,128)(2,1)S(1)} %pad_maximum_fusion), channel_id=1, source_target_pairs={{0,4},{4,0},{8,12},{12,8},{16,20},{20,16},{24,28},{28,24},{32,36},... | collective-permute-start | bytes 2580488 | tf_op jit(solution)/shard_map/ppermute | solution.py:319
  48.3 9.2 %collective-permute-start.14 = (bf16[192,1280]{1,0:T(8,128)(2,1)S(1)}, bf16[192,1280]{1,0:T(8,128)(2,1)S(1)}, u32[]{:S(2)}, u32[]{:S(2)}) collective-permute-start(bf16[192,1280]{1,0:T(8,128)(2,1)S(1)} %get-tuple-element.9), channel_id=1, source_target_pairs={{1,2},{2,1},{3,0},{0,3},{5,6},{6,5},{7,4},{4,7},{9,10},{10,9},{11,... | collective-permute-start | bytes 1474568 | tf_op jit(solution)/shard_map/ppermute | solution.py:339
  57.5 1.5 %copy-start = (bf16[192,896]{1,0:T(8,128)(2,1)}, bf16[192,896]{1,0:T(8,128)(2,1)S(1)}, u32[]{:S(2)}) copy-start(bf16[192,896]{1,0:T(8,128)(2,1)S(1)} %collective-permute-done.15.refs_10_.refs_2_) | copy-start | bytes 1032196
  57.5 4.1 %copy-start.12 = (f32[3584]{0:T(1024)S(1)}, f32[3584]{0:T(1024)}, u32[]{:S(2)}) copy-start(f32[3584]{0:T(1024)} %param.19) | copy-start | bytes 43012
  57.5 4.7 %copy-start.13 = (f32[1152]{0:T(1024)S(1)}, f32[1152]{0:T(1024)}, u32[]{:S(2)}) copy-start(f32[1152]{0:T(1024)} %param.21) | copy-start | bytes 13828
  59.0 47.4 %collective-permute-start.17 = (bf16[192,896]{1,0:T(8,128)(2,1)S(1)}, bf16[192,896]{1,0:T(8,128)(2,1)S(1)}, u32[]{:S(2)}, u32[]{:S(2)}) collective-permute-start(bf16[192,896]{1,0:T(8,128)(2,1)S(1)} %tokens_part.1), channel_id=1, source_target_pairs={{0,259},{1,256},{2,257},{3,258},{4,263},{5,260},{6,261},{7,262},{8... | collective-permute-start | bytes 1032200 | tf_op jit(solution)/shard_map/ppermute | solution.py:356
  60.3 49.7 %collective-permute-start.16 = (bf16[192,896]{1,0:T(8,128)(2,1)S(1)}, bf16[192,896]{1,0:T(8,128)(2,1)S(1)}, u32[]{:S(2)}, u32[]{:S(2)}) collective-permute-start(bf16[192,896]{1,0:T(8,128)(2,1)S(1)} %tokens_part.1), channel_id=1, source_target_pairs={{0,256},{1,257},{2,258},{3,259},{4,260},{5,261},{6,262},{7,263},{8... | collective-permute-start | bytes 1032200 | tf_op jit(solution)/shard_map/ppermute | solution.py:355
  106.4 16.7 %copy-start.8 = (bf16[192,896]{1,0:T(8,128)(2,1)}, bf16[192,896]{1,0:T(8,128)(2,1)S(1)}, u32[]{:S(2)}) copy-start(bf16[192,896]{1,0:T(8,128)(2,1)S(1)} %collective-permute-done.17.refs_5_) | copy-start | bytes 1032196
  106.4 12.9 %collective-permute-start.18 = (bf16[192,896]{1,0:T(8,128)(2,1)S(1)}, bf16[192,896]{1,0:T(8,128)(2,1)S(1)}, u32[]{:S(2)}, u32[]{:S(2)}) collective-permute-start(bf16[192,896]{1,0:T(8,128)(2,1)S(1)} %collective-permute-done.17.refs_5_), channel_id=1, source_target_pairs={{256,259},{257,256},{258,257},{259,258},{260,263},{261,260},{262,2... | collective-permute-start | bytes 1032200 | tf_op jit(solution)/shard_map/ppermute | solution.py:357
  110.0 13.1 %copy-start.9 = (bf16[192,896]{1,0:T(8,128)(2,1)}, bf16[192,896]{1,0:T(8,128)(2,1)S(1)}, u32[]{:S(2)}) copy-start(bf16[192,896]{1,0:T(8,128)(2,1)S(1)} %collective-permute-done.16.refs_4_) | copy-start | bytes 1032196
  110.0 13.1 %collective-permute-start.19 = (bf16[192,896]{1,0:T(8,128)(2,1)S(1)}, bf16[192,896]{1,0:T(8,128)(2,1)S(1)}, u32[]{:S(2)}, u32[]{:S(2)}) collective-permute-start(bf16[192,896]{1,0:T(8,128)(2,1)S(1)} %collective-permute-done.16.refs_4_), channel_id=1, source_target_pairs={{256,257},{257,258},{258,259},{259,256},{260,261},{261,262},{262,2... | collective-permute-start | bytes 1032200 | tf_op jit(solution)/shard_map/ppermute | solution.py:358
  119.3 3.8 %copy-start.10 = (bf16[192,896]{1,0:T(8,128)(2,1)}, bf16[192,896]{1,0:T(8,128)(2,1)S(1)}, u32[]{:S(2)}) copy-start(bf16[192,896]{1,0:T(8,128)(2,1)S(1)} %collective-permute-done.18.refs_6_) | copy-start | bytes 1032196
  (3 other events, 3.5 us)
Sparse Core Ops, SparseCore 0:
  10.6 92.4 all-gather.1

commit v8 on v7

--- a/solution.py
+++ b/solution.py
@@ -86,6 +86,7 @@
             ],
             axis=0,
         ).astype(jnp.bfloat16)
+        values = jnp.concatenate([values, jnp.ones_like(values)], axis=1)
         row = lax.broadcasted_iota(jnp.int32, (count, 2 * count), 0)
         col = lax.broadcasted_iota(jnp.int32, (count, 2 * count), 1)
         allowed = col <= row + count
@@ -95,10 +96,8 @@
             scores = dot_t(query.astype(jnp.bfloat16), keys)
             scores = jnp.where(allowed, scores, -1e30)
             weights = jnp.exp2(scores - jnp.max(scores, axis=1, keepdims=True))
-            probs = weights * (1.0 / jnp.sum(weights, axis=1, keepdims=True))
-            out_ref[:, cols] = jnp.dot(
-                probs.astype(jnp.bfloat16), values, preferred_element_type=jnp.float32
-            ).astype(jnp.bfloat16)
+            context = jnp.dot(weights.astype(jnp.bfloat16), values, preferred_element_type=jnp.float32)
+            out_ref[:, cols] = (context[:, :HEAD] * (1.0 / context[:, HEAD:])).astype(jnp.bfloat16)
 
 
 def decode(order, words, sounds, gain, weight, bias, tables):

time: 146 us -> 144 us (0.986)
  the two profiles are of different devices: /device:TPU:90 before, /device:TPU:122 now
where the time goes in v8:
time: 144 us
  waiting for transfers between devices  58.1 us (40%)
  starting transfers between devices  34.2 us (24%)
  Pallas kernels  22.1 us (15%)
  between operations  14.7 us (10%)
  local copies, waits for them, and re-layouts  7.67 us (5%)
  other arithmetic  6.87 us (5%)
    ppermute x1, waiting for transfers between devices, shards(): lax.ppermute(tokens, both, [(i, n_mdl + (i - 1) % n_mdl) for i in range(n...  43 us
    pallas_call x1, Pallas kernels, decode(): pl.pallas_call(functools.partial(decode_kernel, parts=parts), grid=(parts...  11.2 us
    ppermute x1, waiting for transfers between devices, shards(): second = lax.ppermute(behind, both, ring(1, 1))  7.06 us
    ppermute x1, starting transfers between devices, shards(): behind = lax.ppermute(text, both, ring(1, 1))  6.09 us
    ppermute x1, starting transfers between devices, shards(): ahead = lax.ppermute(text, both, ring(1, -1))  5.87 us
    pallas_call x1, Pallas kernels, conv(): pl.pallas_call(conv_kernel, in_specs=[vmem] * 5 + [pl.BlockSpec(memory_sp...  5.53 us
    unnamed x28, local copies, waits for them, and re-layouts  5.02 us
    ppermute x7, starting transfers between devices, spread(): lax.ppermute(v, ('grp', 'seq'), of_group(0, place(dx, dy)))  4.7 us
  transfers between devices with their start and end apart: 21, of which 4 were waited for; matrix products, arithmetic and copies ran while one was open for 5% of the time, Pallas kernels for 8%

profile of v8, /device:TPU:122, one launch (start us, length us, event | category | flops | bytes accessed | tf_op | source)
XLA Modules:
  0.0 143.7 jit_solution(775341916051941588)
XLA Ops:
  6.5 0.7 all-gather.2.cloned.1.call-update
  7.3 6.1 %collective-permute-start.11 = (bf16[192,896]{1,0:T(8,128)(2,1)}, bf16[192,896]{1,0:T(8,128)(2,1)S(1)}, u32[]{:S(2)}, u32[]{:S(2)}) collective-permute-start(bf16[192,896]{1,0:T(8,128)(2,1)} %refs_0_.1), channel_id=1, source_target_pairs={{256,257},{257,258},{258,259},{259,256},{260,261},{261,262},{262,2... | collective-permute-start | bytes 1032200 | tf_op jit(solution)/shard_map/ppermute | solution.py:322
  13.4 5.9 %collective-permute-start.12 = (bf16[192,896]{1,0:T(8,128)(2,1)}, bf16[192,896]{1,0:T(8,128)(2,1)S(1)}, u32[]{:S(2)}, u32[]{:S(2)}) collective-permute-start(bf16[192,896]{1,0:T(8,128)(2,1)} %refs_0_.1), channel_id=1, source_target_pairs={{256,259},{257,256},{258,257},{259,258},{260,263},{261,260},{262,2... | collective-permute-start | bytes 1032200 | tf_op jit(solution)/shard_map/ppermute | solution.py:323
  21.2 0.7 broadcast_in_dim.6.gain_ref
  21.9 1.5 %copy-done.3 = bf16[768,1280]{1,0:T(8,128)(2,1)S(1)} copy-done((bf16[768,1280]{1,0:T(8,128)(2,1)S(1)}, bf16[768,1280]{1,0:T(8,128)(2,1)}, u32[]{:S(2)}) %copy-start.3) | copy-done | bytes 1966104
  23.5 1.4 copy-done.4
  24.9 3.8 %gate.1 = (bf16[768,320]{1,0:T(8,128)(2,1)S(1)}, f32[192,1280]{1,0:T(8,128)S(1)}) custom-call(s32[1]{0:T(128)S(6)} %sub.20.count_ref, bf16[768,1280]{1,0:T(8,128)(2,1)S(1)} %copy-done.3, f32[1,1280]{1,0:T(1,128)S(1)} %broadcast_in_dim.6.gain_ref, bf16[2,320,1280]{2,1,0:T(8,128)(2,1)S(1)} %bitcast.36), custom_call_target="tpu_custom_call" | custom-call | flops 1258291200 | bytes 7864320 | tf_op jit(solution)/shard_map/gate/pallas_call | solution.py:167
  32.0 1.2 copy-done.5
  33.2 5.5 %conv.1 = bf16[192,1280]{1,0:T(8,128)(2,1)S(1)} custom-call(bf16[16,320]{1,0:T(8,128)(2,1)S(1)} %collective-permute-done.9.before_ref, bf16[768,320]{1,0:T(8,128)(2,1)S(1)} %get-tuple-element.8.gated_ref, bf16[16,320]{1,0:T(8,128)(2,1)S(1)} %collective-permute-done.10.after_ref, f32[31,320]{1,0:T(8,128)S(1)} %copy-done.6, bf16[320,1280]{1,0:T(8,128)(2,1)S(1)} %copy-done.5, ...), custom_call_target="tpu_custom_call" | custom-call | flops 5000000000 | bytes 1966080 | tf_op jit(solution)/shard_map/conv/pallas_call | solution.py:229
  38.8 1.5 %collective-permute-start.13 = (bf16[192,1280]{1,0:T(8,128)(2,1)S(1)}, bf16[192,1280]{1,0:T(8,128)(2,1)}, u32[]{:S(2)}, u32[]{:S(2)}) collective-permute-start(bf16[192,1280]{1,0:T(8,128)(2,1)S(1)} %conv.1), channel_id=1, source_target_pairs={{0,1},{1,0},{2,3},{3,2},{4,5},{5,4},{6,7},{7,6},{8,9},{9,8},{10,11... | collective-permute-start | bytes 1474568 | tf_op jit(solution)/shard_map/ppermute | solution.py:335
  40.8 0.7 collective-permute-start.4
  41.5 0.7 collective-permute-start.5
  42.2 0.7 collective-permute-start.6
  43.8 2.5 %collective-permute-start.15 = (bf16[192,896]{1,0:T(8,128)(2,1)S(1)}, bf16[192,896]{1,0:T(8,128)(2,1)S(1)}, u32[]{:S(2)}, u32[]{:S(2)}) collective-permute-start(bf16[192,896]{1,0:T(8,128)(2,1)S(1)} %collective-permute-done.11.refs_0_.refs_3_), channel_id=1, source_target_pairs={{256,257},{257,258},{258,259},{259,256},{260,261},{261,262},{262,2... | collective-permute-start | bytes 1032200 | tf_op jit(solution)/shard_map/ppermute | solution.py:324
  46.4 0.7 collective-permute-start.8
  47.1 1.2 fusion.3
  48.3 0.7 collective-permute-start.14
  49.0 1.4 fusion.refs_9_
  50.4 7.1 %collective-permute-done.15.refs_10_.refs_2_ = bf16[192,896]{1,0:T(8,128)(2,1)S(1)} collective-permute-done((bf16[192,896]{1,0:T(8,128)(2,1)S(1)}, bf16[192,896]{1,0:T(8,128)(2,1)S(1)}, u32[]{:S(2)}, u32[]{:S(2)}) %collective-permute-start.15) | collective-permute-done | bytes 344096 | tf_op jit(solution)/shard_map/ppermute | solution.py:324
  57.5 1.5 %tokens_part.1 = bf16[192,896]{1,0:T(8,128)(2,1)S(1)} custom-call(bf16[160,896]{1,0:T(8,128)(2,1)S(1)} %concatenate.99.refs_0_, bf16[160,896]{1,0:T(8,128)(2,1)S(1)} %collective-permute-done.4.refs_1_, bf16[160,896]{1,0:T(8,128)(2,1)S(1)} %collective-permute-done.5.refs_2_, bf16[160,896]{1,0:T(8,128)(2,1)S(1)} %collective-permute-done.6.refs_3_, ...), custom_call_target="tpu_custom_call" | custom-call | flops 880803840 | bytes 8000000 | tf_op jit(solution)/shard_map/tokens_part/pallas_call | solution.py:290
  59.0 1.3 collective-permute-start.17
  60.3 1.3 collective-permute-start.16
  63.4 43.0 %collective-permute-done.17.refs_5_ = bf16[192,896]{1,0:T(8,128)(2,1)S(1)} collective-permute-done((bf16[192,896]{1,0:T(8,128)(2,1)S(1)}, bf16[192,896]{1,0:T(8,128)(2,1)S(1)}, u32[]{:S(2)}, u32[]{:S(2)}) %collective-permute-start.17) | collective-permute-done | bytes 344096 | tf_op jit(solution)/shard_map/ppermute | solution.py:355
  106.4 3.6 %collective-permute-start.18 = (bf16[192,896]{1,0:T(8,128)(2,1)S(1)}, bf16[192,896]{1,0:T(8,128)(2,1)S(1)}, u32[]{:S(2)}, u32[]{:S(2)}) collective-permute-start(bf16[192,896]{1,0:T(8,128)(2,1)S(1)} %collective-permute-done.17.refs_5_), channel_id=1, source_target_pairs={{256,259},{257,256},{258,257},{259,258},{260,263},{261,260},{262,2... | collective-permute-start | bytes 1032200 | tf_op jit(solution)/shard_map/ppermute | solution.py:356
  110.0 4.0 %collective-permute-start.19 = (bf16[192,896]{1,0:T(8,128)(2,1)S(1)}, bf16[192,896]{1,0:T(8,128)(2,1)S(1)}, u32[]{:S(2)}, u32[]{:S(2)}) collective-permute-start(bf16[192,896]{1,0:T(8,128)(2,1)S(1)} %collective-permute-done.16.refs_4_), channel_id=1, source_target_pairs={{256,257},{257,258},{258,259},{259,256},{260,261},{261,262},{262,2... | collective-permute-start | bytes 1032200 | tf_op jit(solution)/shard_map/ppermute | solution.py:357
  114.0 0.8 fusion.1
  114.8 0.9 pad_maximum_fusion.1
  115.7 3.5 %collective-permute-done.18.refs_6_ = bf16[192,896]{1,0:T(8,128)(2,1)S(1)} collective-permute-done((bf16[192,896]{1,0:T(8,128)(2,1)S(1)}, bf16[192,896]{1,0:T(8,128)(2,1)S(1)}, u32[]{:S(2)}, u32[]{:S(2)}) %collective-permute-start.18) | collective-permute-done | bytes 344096 | tf_op jit(solution)/shard_map/ppermute | solution.py:356
  119.3 3.8 %collective-permute-done.19.refs_7_ = bf16[192,896]{1,0:T(8,128)(2,1)S(1)} collective-permute-done((bf16[192,896]{1,0:T(8,128)(2,1)S(1)}, bf16[192,896]{1,0:T(8,128)(2,1)S(1)}, u32[]{:S(2)}, u32[]{:S(2)}) %collective-permute-start.19) | collective-permute-done | bytes 344096 | tf_op jit(solution)/shard_map/ppermute | solution.py:357
  123.1 0.7 copy-done.11
  123.9 11.2 %decode.1 = bf16[192,896]{1,0:T(8,128)(2,1)} custom-call(s32[4]{0:T(128)} %and_select_fusion.order_ref, bf16[192,896]{1,0:T(8,128)(2,1)} %refs_0_.1, bf16[192,896]{1,0:T(8,128)(2,1)} %copy-done.2, bf16[192,896]{1,0:T(8,128)(2,1)} %copy-done, bf16[192,896]{1,0:T(8,128)(2,1)} %copy-done.1, bf16[192,896]{1,0:T(8,128)(2,1)} %copy-done.9, ...), custom_call_target="tpu_custom_call" | custom-call | flops 1585446912 | bytes 9633792 | tf_op jit(solution)/shard_map/decode/pallas_call | solution.py:109
  135.1 1.8 %select_bitcast_fusion = bf16[1,192,896]{2,1,0:T(8,128)(2,1)} fusion(bf16[192,896]{1,0:T(8,128)(2,1)S(1)} %tokens_part.1, bf16[192,896]{1,0:T(8,128)(2,1)} %decode.1, pred[]{:T(512)S(6)} %eq.85), kind=kLoop, calls=%fused_computation.4 | loop fusion | flops 172032 | bytes 1032193 | tf_op jit(solution)/shard_map/broadcast_in_dim | solution.py:360
  (64 shorter events, 7.6 us)
Async XLA Ops:
  6.5 116.6 %all-gather.2.cloned.1.call-start = ((), (), s32[]{:S(2)}) async-start(), calls=%async_computation | async-start | bytes 8386560 | tf_op jit(solution)/shard_map/all_gather | solution.py:316
  7.3 24.7 %collective-permute-start.11 = (bf16[192,896]{1,0:T(8,128)(2,1)}, bf16[192,896]{1,0:T(8,128)(2,1)S(1)}, u32[]{:S(2)}, u32[]{:S(2)}) collective-permute-start(bf16[192,896]{1,0:T(8,128)(2,1)} %refs_0_.1), channel_id=1, source_target_pairs={{256,257},{257,258},{258,259},{259,256},{260,261},{261,262},{262,2... | collective-permute-start | bytes 1032200 | tf_op jit(solution)/shard_map/ppermute | solution.py:322
  13.4 18.6 %collective-permute-start.12 = (bf16[192,896]{1,0:T(8,128)(2,1)}, bf16[192,896]{1,0:T(8,128)(2,1)S(1)}, u32[]{:S(2)}, u32[]{:S(2)}) collective-permute-start(bf16[192,896]{1,0:T(8,128)(2,1)} %refs_0_.1), channel_id=1, source_target_pairs={{256,259},{257,256},{258,257},{259,258},{260,263},{261,260},{262,2... | collective-permute-start | bytes 1032200 | tf_op jit(solution)/shard_map/ppermute | solution.py:323
  19.2 10.6 %collective-permute-start.1 = (bf16[20,896]{1,0:T(8,128)(2,1)}, bf16[20,896]{1,0:T(8,128)(2,1)S(1)}, u32[]{:S(2)}, u32[]{:S(2)}) collective-permute-start(bf16[20,896]{1,0:T(8,128)(2,1)} %param.17), channel_id=1, source_target_pairs={{0,56},{4,60},{8,0},{12,4},{16,8},{20,12},{24,16},{28,20},{32,24},... | collective-permute-start | bytes 107528 | tf_op jit(solution)/shard_map/ppermute | solution.py:264
  19.9 10.6 %collective-permute-start = (bf16[20,896]{1,0:T(8,128)(2,1)}, bf16[20,896]{1,0:T(8,128)(2,1)S(1)}, u32[]{:S(2)}, u32[]{:S(2)}) collective-permute-start(bf16[20,896]{1,0:T(8,128)(2,1)} %param.17), channel_id=1, source_target_pairs={{0,8},{4,12},{8,16},{12,20},{16,24},{20,28},{24,32},{28,36},{32,40... | collective-permute-start | bytes 107528 | tf_op jit(solution)/shard_map/ppermute | solution.py:264
  21.9 1.5 %copy-start.3 = (bf16[768,1280]{1,0:T(8,128)(2,1)S(1)}, bf16[768,1280]{1,0:T(8,128)(2,1)}, u32[]{:S(2)}) copy-start(bf16[768,1280]{1,0:T(8,128)(2,1)} %audio_ref.1) | copy-start | bytes 5898244
  24.9 5.6 %copy-start.7 = (bf16[20,896]{1,0:T(8,128)(2,1)S(1)}, bf16[20,896]{1,0:T(8,128)(2,1)}, u32[]{:S(2)}) copy-start(bf16[20,896]{1,0:T(8,128)(2,1)} %param.17) | copy-start | bytes 107524
  24.9 7.1 %copy-start.6 = (f32[31,320]{1,0:T(8,128)S(1)}, f32[31,320]{1,0:T(8,128)}, u32[]{:S(2)}) copy-start(f32[31,320]{1,0:T(8,128)} %taps_ref.1) | copy-start | bytes 119044
  28.8 2.5 %collective-permute-start.10 = (bf16[16,320]{1,0:T(8,128)(2,1)S(1)}, bf16[16,320]{1,0:T(8,128)(2,1)S(1)}, u32[]{:S(2)}, u32[]{:S(2)}) collective-permute-start(bf16[16,320]{1,0:T(8,128)(2,1)S(1)} %get-tuple-element.11), channel_id=1, source_target_pairs={{4,0},{8,4},{12,8},{16,12},{20,16},{24,20},{28,24},{32,28},{36,32}... | collective-permute-start | bytes 30728 | tf_op jit(solution)/shard_map/ppermute | solution.py:333
  29.8 2.1 %collective-permute-start.9 = (bf16[16,320]{1,0:T(8,128)(2,1)S(1)}, bf16[16,320]{1,0:T(8,128)(2,1)S(1)}, u32[]{:S(2)}, u32[]{:S(2)}) collective-permute-start(bf16[16,320]{1,0:T(8,128)(2,1)S(1)} %get-tuple-element.12), channel_id=1, source_target_pairs={{0,4},{4,8},{8,12},{12,16},{16,20},{20,24},{24,28},{28,32},{32,36}... | collective-permute-start | bytes 30728 | tf_op jit(solution)/shard_map/ppermute | solution.py:332
  30.5 9.7 %collective-permute-start.2 = (bf16[60,896]{1,0:T(8,128)(2,1)S(1)}, bf16[60,896]{1,0:T(8,128)(2,1)S(1)}, u32[]{:S(2)}, u32[]{:S(2)}) collective-permute-start(bf16[60,896]{1,0:T(8,128)(2,1)S(1)} %pad_maximum_fusion.3), channel_id=1, source_target_pairs={{0,40},{4,44},{8,48},{12,52},{16,56},{20,60},{24,0},{28,4},{32,8},... | collective-permute-start | bytes 322568 | tf_op jit(solution)/shard_map/ppermute | solution.py:264
  31.3 9.0 %collective-permute-start.3 = (bf16[40,896]{1,0:T(8,128)(2,1)S(1)}, bf16[40,896]{1,0:T(8,128)(2,1)S(1)}, u32[]{:S(2)}, u32[]{:S(2)}) collective-permute-start(bf16[40,896]{1,0:T(8,128)(2,1)S(1)} %pad_maximum_fusion.4), channel_id=1, source_target_pairs={{0,24},{4,28},{8,32},{12,36},{16,40},{20,44},{24,48},{28,52},{32,5... | collective-permute-start | bytes 215048 | tf_op jit(solution)/shard_map/ppermute | solution.py:264
  31.9 11.9 %copy-start.1 = (bf16[192,896]{1,0:T(8,128)(2,1)}, bf16[192,896]{1,0:T(8,128)(2,1)S(1)}, u32[]{:S(2)}) copy-start(bf16[192,896]{1,0:T(8,128)(2,1)S(1)} %collective-permute-done.11.refs_0_.refs_3_) | copy-start | bytes 1032196
  33.2 5.5 %copy-start.2 = (bf16[192,896]{1,0:T(8,128)(2,1)}, bf16[192,896]{1,0:T(8,128)(2,1)S(1)}, u32[]{:S(2)}) copy-start(bf16[192,896]{1,0:T(8,128)(2,1)S(1)} %collective-permute-done.12.refs_1_) | copy-start | bytes 1032196
  38.8 8.3 %collective-permute-start.13 = (bf16[192,1280]{1,0:T(8,128)(2,1)S(1)}, bf16[192,1280]{1,0:T(8,128)(2,1)}, u32[]{:S(2)}, u32[]{:S(2)}) collective-permute-start(bf16[192,1280]{1,0:T(8,128)(2,1)S(1)} %conv.1), channel_id=1, source_target_pairs={{0,1},{1,0},{2,3},{3,2},{4,5},{5,4},{6,7},{7,6},{8,9},{9,8},{10,11... | collective-permute-start | bytes 1474568 | tf_op jit(solution)/shard_map/ppermute | solution.py:335
  40.8 3.0 %collective-permute-start.4 = (bf16[160,896]{1,0:T(8,128)(2,1)S(1)}, bf16[160,896]{1,0:T(8,128)(2,1)S(1)}, u32[]{:S(2)}, u32[]{:S(2)}) collective-permute-start(bf16[160,896]{1,0:T(8,128)(2,1)S(1)} %concatenate.99.refs_0_), channel_id=1, source_target_pairs={{0,64},{4,68},{8,72},{12,76},{16,80},{20,84},{24,88},{28,92},{32,9... | collective-permute-start | bytes 860168 | tf_op jit(solution)/shard_map/ppermute | solution.py:264
  41.5 4.8 %collective-permute-start.5 = (bf16[160,896]{1,0:T(8,128)(2,1)S(1)}, bf16[160,896]{1,0:T(8,128)(2,1)S(1)}, u32[]{:S(2)}, u32[]{:S(2)}) collective-permute-start(bf16[160,896]{1,0:T(8,128)(2,1)S(1)} %concatenate.99.refs_0_), channel_id=1, source_target_pairs={{0,192},{4,196},{8,200},{12,204},{16,208},{20,212},{24,216},{28,22... | collective-permute-start | bytes 860168 | tf_op jit(solution)/shard_map/ppermute | solution.py:264
  42.2 4.1 %collective-permute-start.6 = (bf16[160,896]{1,0:T(8,128)(2,1)S(1)}, bf16[160,896]{1,0:T(8,128)(2,1)S(1)}, u32[]{:S(2)}, u32[]{:S(2)}) collective-permute-start(bf16[160,896]{1,0:T(8,128)(2,1)S(1)} %concatenate.99.refs_0_), channel_id=1, source_target_pairs={{0,128},{4,132},{8,136},{12,140},{16,144},{20,148},{24,152},{28,15... | collective-permute-start | bytes 860168 | tf_op jit(solution)/shard_map/ppermute | solution.py:264
  43.1 7.3 %collective-permute-start.7 = (bf16[160,896]{1,0:T(8,128)(2,1)S(1)}, bf16[160,896]{1,0:T(8,128)(2,1)S(1)}, u32[]{:S(2)}, u32[]{:S(2)}) collective-permute-start(bf16[160,896]{1,0:T(8,128)(2,1)S(1)} %concatenate.99.refs_0_), channel_id=1, source_target_pairs={{0,4},{4,0},{8,12},{12,8},{16,20},{20,16},{24,28},{28,24},{32,36},... | collective-permute-start | bytes 860168 | tf_op jit(solution)/shard_map/ppermute | solution.py:318
  43.8 13.6 %collective-permute-start.15 = (bf16[192,896]{1,0:T(8,128)(2,1)S(1)}, bf16[192,896]{1,0:T(8,128)(2,1)S(1)}, u32[]{:S(2)}, u32[]{:S(2)}) collective-permute-start(bf16[192,896]{1,0:T(8,128)(2,1)S(1)} %collective-permute-done.11.refs_0_.refs_3_), channel_id=1, source_target_pairs={{256,257},{257,258},{258,259},{259,256},{260,261},{261,262},{262,2... | collective-permute-start | bytes 1032200 | tf_op jit(solution)/shard_map/ppermute | solution.py:324
  46.4 11.1 %collective-permute-start.8 = (bf16[480,896]{1,0:T(8,128)(2,1)S(1)}, bf16[480,896]{1,0:T(8,128)(2,1)S(1)}, u32[]{:S(2)}, u32[]{:S(2)}) collective-permute-start(bf16[480,896]{1,0:T(8,128)(2,1)S(1)} %pad_maximum_fusion), channel_id=1, source_target_pairs={{0,4},{4,0},{8,12},{12,8},{16,20},{20,16},{24,28},{28,24},{32,36},... | collective-permute-start | bytes 2580488 | tf_op jit(solution)/shard_map/ppermute | solution.py:318
  48.3 9.2 %collective-permute-start.14 = (bf16[192,1280]{1,0:T(8,128)(2,1)S(1)}, bf16[192,1280]{1,0:T(8,128)(2,1)S(1)}, u32[]{:S(2)}, u32[]{:S(2)}) collective-permute-start(bf16[192,1280]{1,0:T(8,128)(2,1)S(1)} %get-tuple-element.9), channel_id=1, source_target_pairs={{1,2},{2,1},{3,0},{0,3},{5,6},{6,5},{7,4},{4,7},{9,10},{10,9},{11,... | collective-permute-start | bytes 1474568 | tf_op jit(solution)/shard_map/ppermute | solution.py:338
  57.5 1.5 %copy-start = (bf16[192,896]{1,0:T(8,128)(2,1)}, bf16[192,896]{1,0:T(8,128)(2,1)S(1)}, u32[]{:S(2)}) copy-start(bf16[192,896]{1,0:T(8,128)(2,1)S(1)} %collective-permute-done.15.refs_10_.refs_2_) | copy-start | bytes 1032196
  57.5 4.1 %copy-start.12 = (f32[3584]{0:T(1024)S(1)}, f32[3584]{0:T(1024)}, u32[]{:S(2)}) copy-start(f32[3584]{0:T(1024)} %param.19) | copy-start | bytes 43012
  57.5 4.7 %copy-start.13 = (f32[1152]{0:T(1024)S(1)}, f32[1152]{0:T(1024)}, u32[]{:S(2)}) copy-start(f32[1152]{0:T(1024)} %param.21) | copy-start | bytes 13828
  59.0 47.4 %collective-permute-start.17 = (bf16[192,896]{1,0:T(8,128)(2,1)S(1)}, bf16[192,896]{1,0:T(8,128)(2,1)S(1)}, u32[]{:S(2)}, u32[]{:S(2)}) collective-permute-start(bf16[192,896]{1,0:T(8,128)(2,1)S(1)} %tokens_part.1), channel_id=1, source_target_pairs={{0,259},{1,256},{2,257},{3,258},{4,263},{5,260},{6,261},{7,262},{8... | collective-permute-start | bytes 1032200 | tf_op jit(solution)/shard_map/ppermute | solution.py:355
  60.3 49.7 %collective-permute-start.16 = (bf16[192,896]{1,0:T(8,128)(2,1)S(1)}, bf16[192,896]{1,0:T(8,128)(2,1)S(1)}, u32[]{:S(2)}, u32[]{:S(2)}) collective-permute-start(bf16[192,896]{1,0:T(8,128)(2,1)S(1)} %tokens_part.1), channel_id=1, source_target_pairs={{0,256},{1,257},{2,258},{3,259},{4,260},{5,261},{6,262},{7,263},{8... | collective-permute-start | bytes 1032200 | tf_op jit(solution)/shard_map/ppermute | solution.py:354
  106.4 16.7 %copy-start.8 = (bf16[192,896]{1,0:T(8,128)(2,1)}, bf16[192,896]{1,0:T(8,128)(2,1)S(1)}, u32[]{:S(2)}) copy-start(bf16[192,896]{1,0:T(8,128)(2,1)S(1)} %collective-permute-done.17.refs_5_) | copy-start | bytes 1032196
  106.4 12.9 %collective-permute-start.18 = (bf16[192,896]{1,0:T(8,128)(2,1)S(1)}, bf16[192,896]{1,0:T(8,128)(2,1)S(1)}, u32[]{:S(2)}, u32[]{:S(2)}) collective-permute-start(bf16[192,896]{1,0:T(8,128)(2,1)S(1)} %collective-permute-done.17.refs_5_), channel_id=1, source_target_pairs={{256,259},{257,256},{258,257},{259,258},{260,263},{261,260},{262,2... | collective-permute-start | bytes 1032200 | tf_op jit(solution)/shard_map/ppermute | solution.py:356
  110.0 13.1 %copy-start.9 = (bf16[192,896]{1,0:T(8,128)(2,1)}, bf16[192,896]{1,0:T(8,128)(2,1)S(1)}, u32[]{:S(2)}) copy-start(bf16[192,896]{1,0:T(8,128)(2,1)S(1)} %collective-permute-done.16.refs_4_) | copy-start | bytes 1032196
  110.0 13.1 %collective-permute-start.19 = (bf16[192,896]{1,0:T(8,128)(2,1)S(1)}, bf16[192,896]{1,0:T(8,128)(2,1)S(1)}, u32[]{:S(2)}, u32[]{:S(2)}) collective-permute-start(bf16[192,896]{1,0:T(8,128)(2,1)S(1)} %collective-permute-done.16.refs_4_), channel_id=1, source_target_pairs={{256,257},{257,258},{258,259},{259,256},{260,261},{261,262},{262,2... | collective-permute-start | bytes 1032200 | tf_op jit(solution)/shard_map/ppermute | solution.py:357
  119.3 3.8 %copy-start.10 = (bf16[192,896]{1,0:T(8,128)(2,1)}, bf16[192,896]{1,0:T(8,128)(2,1)S(1)}, u32[]{:S(2)}) copy-start(bf16[192,896]{1,0:T(8,128)(2,1)S(1)} %collective-permute-done.18.refs_6_) | copy-start | bytes 1032196
  (3 other events, 3.5 us)
Sparse Core Ops, SparseCore 0:
  10.6 91.8 all-gather.1
